TPU v7x, 128 devices: a whole 4x4x4 slice. The times are simulated.
128 devices in a mesh: lat: 8 (over x, core), lon: 16 (over y, z).
Axes of the slice: x: 4, y: 4, z: 4, core: 2. Of those that a mesh axis runs over, the one named last changes fastest.
Arguments:
- grid_in: bfloat16 [65536, 227], P(('lat', 'lon')), may hold values from -6 to 6
- grid_export: int32 [16384], P(('lat', 'lon')), may hold values from 0 to 511
- mesh_init: bfloat16 [20480, 512], P(('lat', 'lon')), may hold values from -6 to 6
- encode_senders: int32 [1024, 128], P(('lat', 'lon')), may hold values from 0 to 511, as said below
- encode_slots: int32 [1024], P(('lat', 'lon')), may hold values from 0 to 8, as said below
- encode_receivers: int32 [1024, 128], P(('lat', 'lon')), may hold values from 0 to 159
- encode_live: int32 [128], P(('lat', 'lon')), may hold values from 4 to 8, as said below
- mesh_export: int32 [16384], P(('lat', 'lon')), may hold values from 0 to 159
- process_senders: int32 [1024, 128], P(('lat', 'lon')), may hold values from 0 to 159, as said below
- process_slots: int32 [1024], P(('lat', 'lon')), may hold values from 0 to 8, as said below
- process_receivers: int32 [1024, 128], P(('lat', 'lon')), may hold values from 0 to 159
- process_live: int32 [128], P(('lat', 'lon')), may hold values from 4 to 8, as said below
- grid_weight: bfloat16 [227, 512], replicated, may hold values from -0.375 to 0.375
- sender_weight: bfloat16 [512, 512], replicated, may hold values from -0.25 to 0.25
- receiver_weight: bfloat16 [512, 512], replicated, may hold values from -0.25 to 0.25
- message_weight: bfloat16 [512, 512], replicated, may hold values from -0.25 to 0.25
- update_weight: bfloat16 [512, 512], replicated, may hold values from -0.25 to 0.25
- encode_gain: float32 [512], replicated, may hold values from 0.1 to 1.9
- edge_sender: bfloat16 [512, 512], replicated, may hold values from -0.25 to 0.25
- edge_receiver: bfloat16 [512, 512], replicated, may hold values from -0.25 to 0.25
- edge_message: bfloat16 [512, 512], replicated, may hold values from -0.25 to 0.25
- node_update: bfloat16 [512, 512], replicated, may hold values from -0.25 to 0.25
- node_gain: float32 [512], replicated, may hold values from 0.1 to 1.9
- cotangent: bfloat16 [20480, 512], P(('lat', 'lon')), may hold values from -6 to 6
Outputs:
- mesh_out: bfloat16 [20480, 512], P(('lat', 'lon'))
- grid_grad: float32 [227, 512], replicated
- sender_grad: float32 [512, 512], replicated
- edge_grad: float32 [512, 512], replicated
Inputs may be any that keep to these rules, and one draw needn't show every extreme that they name: `encode_slots`: slot of the tile a block's senders lie in: 3 i + j for the tile i - 1 bands and j - 1 sectors away; no slot reaches past the first or the last band. `encode_senders`: in a block of slot 4 a grid row of the tile itself; in other blocks a position below 128 in the source tile's grid_export list. Only a tile's first encode_live blocks hold edges; some tile fills all 8. `process_slots`: slot of the tile a block's senders lie in: 3 i + j for the tile i - 1 bands and j - 1 sectors away; no slot reaches past the first or the last band. `process_senders`: in a block of slot 4 a mesh row of the tile itself; in other blocks a position below 128 in the source tile's mesh_export list. Only a tile's first process_live blocks hold edges; some tile fills all 8.
All inputs are finite; a program needn't handle non-finite values.
Results may differ from a plain program's by a relative error of at most 0.023.
Values may be sent and summed in bfloat16 or wider, within the bound.
No kernel may reach another device: no remote copies, remote signals or barrier semaphores. Data moves between devices by JAX's collectives and lax.ppermute only.
A program may use at most 128 MiB of HBM per device.

v0:
```python
import jax
import jax.numpy as jnp
from jax import lax
from jax.experimental import pallas as pl
from jax.experimental.pallas import tpu as pltpu
from jax.sharding import PartitionSpec as P

norm_epsilon = 1e-05
blocks_per_turn = 4
lanes = 128
f32 = jnp.float32
bf16 = jnp.bfloat16


def dot(left, right):
    return jnp.dot(left, right, preferred_element_type=f32)


def back_dot(left, weight):
    return lax.dot_general(left, weight, (((1,), (1,)), ((), ())), preferred_element_type=f32)


def cross_dot(left, right):
    return lax.dot_general(left, right, (((0,), (0,)), ((), ())), preferred_element_type=f32)


def sigmoid(values):
    return 0.5 * jnp.tanh(0.5 * values) + 0.5


def row_mean(values):
    return jnp.mean(values, axis=-1, keepdims=True)


def normalise(values):
    center = values - row_mean(values)
    scale = lax.rsqrt(row_mean(center * center) + norm_epsilon)
    return center * scale, scale


def norm_back(normed, scale, upstream):
    inner = row_mean(upstream * normed)
    return scale * (upstream - row_mean(upstream) - normed * inner)


def lane_hot(row, width):
    spread = jnp.transpose(jnp.broadcast_to(row.astype(f32), (lanes, lanes)))
    column = lax.broadcasted_iota(jnp.int32, (lanes, lanes), 1).astype(f32)
    parts = [
        jnp.where(spread == column + float(start), 1.0, 0.0).astype(bf16)
        for start in range(0, width, lanes)
    ]
    return jnp.concatenate(parts, 1)


def row_hot(row, count):
    index = lax.broadcasted_iota(jnp.int32, (count, lanes), 0)
    return jnp.where(index == row, 1.0, 0.0).astype(bf16)


def live_row(rows, block, live):
    return jnp.where(block < live, rows[pl.ds(block, 1), :], -1)


def window(slots, block, own_rows, copy_rows):
    slot = slots[block]
    return pl.multiple_of(jnp.where(slot == 4, 0, own_rows + slot * copy_rows), lanes)


def encode_kernel(
    live_ref,
    slots,
    grid_own,
    grid_near,
    base,
    senders,
    receivers,
    export,
    grid_weight,
    sender_weight,
    receiver_weight,
    message_weight,
    update_weight,
    gain,
    state,
    picked,
    inputs,
    hidden,
    pre_slope,
    mix_slope,
    normed_out,
    scale_out,
    update_normed,
    update_scale,
    table,
    projected,
    total,
):
    own, copies = grid_own.shape[0], grid_near.shape[0]
    nodes = base.shape[0]
    live = live_ref[0]
    table[0:own, :] = grid_own[...]
    table[own : own + copies, :] = grid_near[...]
    table[own + copies :, :] = jnp.zeros_like(table[own + copies :, :])
    projected[0:nodes, :] = dot(base[...], receiver_weight[...]).astype(bf16)
    projected[nodes:, :] = jnp.zeros_like(projected[nodes:, :])
    total[...] = jnp.zeros_like(total)
    turn_rows = blocks_per_turn * lanes

    def turn(step, carry):
        gathered, received, placed = [], [], []
        for part in range(blocks_per_turn):
            block = step * blocks_per_turn + part
            start = window(slots, block, own, lanes)
            pick = lane_hot(senders[pl.ds(block, 1), :], own)
            gathered.append(dot(pick, table[pl.ds(start, own), :]).astype(bf16))
            ends = live_row(receivers, block, live)
            received.append(lane_hot(ends, projected.shape[0]))
            placed.append(row_hot(ends, nodes))
        here = pl.ds(pl.multiple_of(step * turn_rows, turn_rows), turn_rows)
        rows = jnp.concatenate(gathered, 0)
        inputs[here, :] = rows
        pre = dot(rows, grid_weight[...])
        gate = sigmoid(pre)
        pre_slope[here, :] = (gate * (1.0 + pre * (1.0 - gate))).astype(bf16)
        embedded = (pre * gate).astype(bf16)
        hidden[here, :] = embedded
        sent = dot(embedded, sender_weight[...]).astype(bf16).astype(f32)
        mix = sent + dot(jnp.concatenate(received, 0), projected[...])
        gate = sigmoid(mix)
        mix_slope[here, :] = (gate * (1.0 + mix * (1.0 - gate))).astype(bf16)
        product = dot((mix * gate).astype(bf16), message_weight[...])
        normed, scale = normalise(product)
        normed = normed.astype(bf16)
        normed_out[here, :] = normed
        scale_out[here, :] = jnp.broadcast_to(scale, (turn_rows, lanes))
        total[...] += dot(jnp.concatenate(placed, 1), normed)
        return carry

    lax.fori_loop(0, senders.shape[0] // blocks_per_turn, turn, 0)
    update = dot(total[...].astype(bf16), update_weight[...])
    normed, scale = normalise(update)
    update_normed[...] = normed
    update_scale[...] = jnp.broadcast_to(scale, update_scale.shape)
    new_state = (base[...].astype(f32) + normed * gain[...]).astype(bf16)
    state[...] = new_state
    padded_state = jnp.concatenate(
        [new_state, jnp.zeros((256 - nodes, new_state.shape[1]), bf16)], 0
    )
    picked[...] = dot(lane_hot(export[...], 256), padded_state).astype(bf16)


def process_kernel(
    live_ref,
    slots,
    state,
    near,
    senders,
    receivers,
    edge_sender,
    edge_receiver,
    edge_message,
    node_update,
    gain,
    cotangent,
    mesh_out,
    own_grad,
    leaving,
    sender_rows,
    mix_grad_out,
    receiver_grad,
    table,
    terms,
    total,
    slope,
    normed_all,
    scale_all,
    upstream,
    table_grad,
    receiver_total,
):
    nodes, copies = state.shape[0], near.shape[0]
    reach = 256
    live = live_ref[0]
    table[0:nodes, :] = state[...]
    table[nodes:reach, :] = jnp.zeros_like(table[nodes:reach, :])
    table[reach : reach + copies, :] = near[...]
    table[reach + copies :, :] = jnp.zeros_like(table[reach + copies :, :])
    terms[0:nodes, :] = dot(state[...], edge_receiver[...]).astype(bf16)
    terms[nodes:, :] = jnp.zeros_like(terms[nodes:, :])
    total[...] = jnp.zeros_like(total)
    turn_rows = blocks_per_turn * lanes
    turns = senders.shape[0] // blocks_per_turn

    def forward(step, carry):
        gathered, received, placed = [], [], []
        for part in range(blocks_per_turn):
            block = step * blocks_per_turn + part
            start = window(slots, block, reach, lanes)
            pick = lane_hot(senders[pl.ds(block, 1), :], reach)
            gathered.append(dot(pick, table[pl.ds(start, reach), :]).astype(bf16))
            ends = live_row(receivers, block, live)
            received.append(lane_hot(ends, reach))
            placed.append(row_hot(ends, nodes))
        here = pl.ds(pl.multiple_of(step * turn_rows, turn_rows), turn_rows)
        rows = jnp.concatenate(gathered, 0)
        sender_rows[here, :] = rows
        sent = dot(rows, edge_sender[...]).astype(bf16).astype(f32)
        mix = sent + dot(jnp.concatenate(received, 0), terms[...])
        gate = sigmoid(mix)
        slope[here, :] = gate * (1.0 + mix * (1.0 - gate))
        product = dot((mix * gate).astype(bf16), edge_message[...])
        normed, scale = normalise(product)
        normed_all[here, :] = normed
        scale_all[here, :] = jnp.broadcast_to(scale, (turn_rows, lanes))
        total[...] += dot(jnp.concatenate(placed, 1), normed.astype(bf16))
        return carry

    lax.fori_loop(0, turns, forward, 0)
    update = dot(total[...].astype(bf16), node_update[...])
    normed, scale = normalise(update)
    mesh_out[...] = (state[...].astype(f32) + normed * gain[...]).astype(bf16)
    update_grad = norm_back(normed, scale, cotangent[...].astype(f32) * gain[...])
    upstream[0:nodes, :] = back_dot(update_grad.astype(bf16), node_update[...]).astype(bf16)
    upstream[nodes:, :] = jnp.zeros_like(upstream[nodes:, :])
    table_grad[...] = jnp.zeros_like(table_grad)
    receiver_total[...] = jnp.zeros_like(receiver_total)

    def backward(step, carry):
        received, placed = [], []
        for part in range(blocks_per_turn):
            ends = live_row(receivers, step * blocks_per_turn + part, live)
            received.append(lane_hot(ends, reach))
            placed.append(row_hot(ends, nodes))
        here = pl.ds(pl.multiple_of(step * turn_rows, turn_rows), turn_rows)
        arriving = dot(jnp.concatenate(received, 0), upstream[...])
        product_grad = norm_back(normed_all[here, :], scale_all[here, 0:1], arriving)
        mix_grad = back_dot(product_grad.astype(bf16), edge_message[...]) * slope[here, :]
        mix_grad = mix_grad.astype(bf16)
        mix_grad_out[here, :] = mix_grad
        receiver_total[...] += dot(jnp.concatenate(placed, 1), mix_grad)
        for part in range(blocks_per_turn):
            block = step * blocks_per_turn + part
            start = window(slots, block, reach, lanes)
            place = row_hot(senders[pl.ds(block, 1), :], nodes)
            table_grad[pl.ds(start, nodes), :] += dot(
                place, mix_grad[part * lanes : (part + 1) * lanes, :]
            )
        return carry

    lax.fori_loop(0, turns, backward, 0)
    own_grad[...] = table_grad[0:nodes, :]
    leaving[...] = table_grad[reach : reach + copies, :].astype(bf16)
    receiver_grad[...] = receiver_total[...].astype(bf16)


def encode_back_kernel(
    live_ref,
    receivers,
    export,
    state_part,
    own_grad,
    kept,
    from_left,
    from_right,
    edge_sender,
    update_normed,
    update_scale,
    gain,
    update_weight,
    normed_all,
    scale_all,
    mix_slope,
    pre_slope,
    message_weight,
    sender_weight,
    mix_grad_out,
    pre_grad_out,
    upstream,
):
    nodes = state_part.shape[0]
    live = live_ref[0]
    arrived = kept[...].astype(f32) + from_left[...].astype(f32) + from_right[...].astype(f32)
    table_grad = own_grad[...] + dot(row_hot(export[...], nodes), arrived.astype(bf16))
    state_grad = state_part[...] + back_dot(table_grad.astype(bf16), edge_sender[...])
    update_grad = norm_back(update_normed[...], update_scale[:, 0:1], state_grad * gain[...])
    upstream[0:nodes, :] = back_dot(update_grad.astype(bf16), update_weight[...]).astype(bf16)
    upstream[nodes:, :] = jnp.zeros_like(upstream[nodes:, :])
    turn_rows = blocks_per_turn * lanes

    def turn(step, carry):
        received = [
            lane_hot(live_row(receivers, step * blocks_per_turn + part, live), upstream.shape[0])
            for part in range(blocks_per_turn)
        ]
        here = pl.ds(pl.multiple_of(step * turn_rows, turn_rows), turn_rows)
        arriving = dot(jnp.concatenate(received, 0), upstream[...])
        product_grad = norm_back(
            normed_all[here, :].astype(f32), scale_all[here, 0:1], arriving
        ).astype(bf16)
        mix_grad = back_dot(product_grad, message_weight[...]) * mix_slope[here, :].astype(f32)
        mix_grad = mix_grad.astype(bf16)
        mix_grad_out[here, :] = mix_grad
        pre_grad = back_dot(mix_grad, sender_weight[...]) * pre_slope[here, :].astype(f32)
        pre_grad_out[here, :] = pre_grad.astype(bf16)
        return carry

    lax.fori_loop(0, receivers.shape[0] // blocks_per_turn, turn, 0)


def call(kernel, operands, outs, scratch, scalars=1, flops=0):
    smem = pl.BlockSpec(memory_space=pltpu.SMEM)
    vmem = pl.BlockSpec(memory_space=pltpu.VMEM)
    return pl.pallas_call(
        kernel,
        out_shape=[jax.ShapeDtypeStruct(shape, dtype) for shape, dtype in outs],
        in_specs=[smem] * scalars + [vmem] * (len(operands) - scalars),
        out_specs=[vmem] * len(outs),
        scratch_shapes=[pltpu.VMEM(shape, dtype) for shape, dtype in scratch],
        compiler_params=pltpu.CompilerParams(vmem_limit_bytes=40 * 1024 * 1024),
        cost_estimate=pl.CostEstimate(flops=flops, bytes_accessed=8 << 20, transcendentals=0),
    )(*operands)


def shifted(x, axis, step):
    size = lax.axis_size(axis)
    if axis == "lon":
        pairs = [(i, (i + step) % size) for i in range(size)]
    else:
        pairs = [(i, i + step) for i in range(size) if 0 <= i + step < size]
    return lax.ppermute(x, axis, pairs)


def around(rows):
    for axis in ("lat", "lon"):
        before, after = shifted(rows, axis, 1), shifted(rows, axis, -1)
        dim = 0 if axis == "lat" else 1
        rows = jnp.stack([before, rows, after], dim)
    return rows.reshape(9 * rows.shape[2], rows.shape[3])


def partner(x, axis, flip):
    return lax.ppermute(x, axis, [(i, i ^ flip) for i in range(lax.axis_size(axis))])


def add(left, right):
    return (left.astype(f32) + right.astype(f32)).astype(bf16)


halving = (("lat", 1, 0), ("lat", 2, 1), ("lat", 6, 2))
doubling = (("lon", 1), ("lon", 3), ("lon", 4), ("lon", 12))


def summed(values):
    index = lax.axis_index("lat")
    bits = (index & 1, ((index >> 1) ^ (index >> 2)) & 1, (index >> 2) & 1)
    for axis, flip, bit in halving:
        half = values.shape[0] // 2
        mine = lax.dynamic_slice_in_dim(values, bits[bit] * half, half, 0)
        other = lax.dynamic_slice_in_dim(values, (1 - bits[bit]) * half, half, 0)
        values = add(mine, partner(other, axis, flip))
    for axis, flip in doubling:
        values = add(values, partner(values, axis, flip))
    for axis, flip, bit in halving[::-1]:
        got = partner(values, axis, flip)
        low = bits[bit] == 0
        values = jnp.concatenate([jnp.where(low, values, got), jnp.where(low, got, values)], 0)
    return values


def local(
    grid_in,
    grid_export,
    mesh_init,
    encode_senders,
    encode_slots,
    encode_receivers,
    encode_live,
    mesh_export,
    process_senders,
    process_slots,
    process_receivers,
    process_live,
    grid_weight,
    sender_weight,
    receiver_weight,
    message_weight,
    update_weight,
    encode_gain,
    edge_sender,
    edge_receiver,
    edge_message,
    node_update,
    node_gain,
    cotangent,
):
    grid_count, variables = grid_in.shape
    nodes, width = mesh_init.shape
    copies = mesh_export.shape[0]
    edges = encode_senders.shape[0] * encode_senders.shape[1]
    depth = 256
    grid_rows = jnp.pad(grid_in, ((0, 0), (0, depth - variables)))
    select = (grid_export[:, None] == jnp.arange(grid_count)[None, :]).astype(bf16)
    grid_near = around(dot(select, grid_rows).astype(bf16))
    grid_weight = jnp.pad(grid_weight, ((0, depth - variables), (0, 0)))
    export = mesh_export[None]
    encode_gain, node_gain = encode_gain[None], node_gain[None]
    (
        state,
        picked,
        inputs,
        hidden,
        pre_slope,
        mix_slope,
        normed,
        scale,
        update_normed,
        update_scale,
    ) = call(
        encode_kernel,
        (
            encode_live,
            encode_slots,
            grid_rows,
            grid_near,
            mesh_init,
            encode_senders,
            encode_receivers,
            export,
            grid_weight,
            sender_weight,
            receiver_weight,
            message_weight,
            update_weight,
            encode_gain,
        ),
        [
            ((nodes, width), bf16),
            ((copies, width), bf16),
            ((edges, depth), bf16),
            ((edges, width), bf16),
            ((edges, width), bf16),
            ((edges, width), bf16),
            ((edges, width), bf16),
            ((edges, lanes), f32),
            ((nodes, width), f32),
            ((nodes, lanes), f32),
        ],
        [
            ((grid_count + 9 * lanes + grid_count - lanes, depth), bf16),
            ((256, width), bf16),
            ((nodes, width), f32),
        ],
        scalars=2,
    )
    near = around(picked)
    mesh_out, own_grad, leaving, sender_rows, mix_grad, receiver_grad = call(
        process_kernel,
        (
            process_live,
            process_slots,
            state,
            near,
            process_senders,
            process_receivers,
            edge_sender,
            edge_receiver,
            edge_message,
            node_update,
            node_gain,
            cotangent,
        ),
        [
            ((nodes, width), bf16),
            ((nodes, width), f32),
            ((9 * copies, width), bf16),
            ((edges, width), bf16),
            ((edges, width), bf16),
            ((nodes, width), bf16),
        ],
        [
            ((256 + 9 * copies + 128, width), bf16),
            ((256, width), bf16),
            ((nodes, width), f32),
            ((edges, width), f32),
            ((edges, width), f32),
            ((edges, lanes), f32),
            ((256, width), bf16),
            ((256 + 9 * copies + 128, width), f32),
            ((nodes, width), f32),
        ],
        scalars=2,
    )
    leaving = leaving.reshape(3, 3 * copies, width)
    from_above = shifted(leaving[0], "lat", -1)
    from_below = shifted(leaving[2], "lat", 1)
    columns = (
        leaving[1].astype(f32) + from_above.astype(f32) + from_below.astype(f32)
    ).astype(bf16).reshape(3, copies, width)
    from_right = shifted(columns[0], "lon", -1)
    from_left = shifted(columns[2], "lon", 1)
    state_part = cotangent.astype(f32) + back_dot(receiver_grad, edge_receiver)
    edge_grad = cross_dot(sender_rows, mix_grad).astype(bf16)
    mix_grad, pre_grad = call(
        encode_back_kernel,
        (
            encode_live,
            encode_receivers,
            export,
            state_part,
            own_grad,
            columns[1],
            from_left,
            from_right,
            edge_sender,
            update_normed,
            update_scale,
            encode_gain,
            update_weight,
            normed,
            scale,
            mix_slope,
            pre_slope,
            message_weight,
            sender_weight,
        ),
        [((edges, width), bf16), ((edges, width), bf16)],
        [((256, width), bf16)],
    )
    sender_grad = cross_dot(hidden, mix_grad).astype(bf16)
    grid_grad = cross_dot(inputs, pre_grad).astype(bf16)
    totals = summed(jnp.concatenate([sender_grad, edge_grad, grid_grad], 0)).astype(f32)
    return (
        mesh_out,
        totals[2 * width : 2 * width + variables],
        totals[:width],
        totals[width : 2 * width],
    )


def solution(mesh):
    tiles, shared = P(("lat", "lon")), P()
    wide = P(("lat", "lon"), None)
    return jax.shard_map(
        local,
        mesh=mesh,
        in_specs=(
            (wide, tiles, wide, wide, tiles, wide, tiles, tiles, wide, tiles, wide, tiles)
            + (shared,) * 11
            + (wide,)
        ),
        out_specs=(wide, shared, shared, shared),
        check_vma=False,
    )
```

profile of v0, /device:TPU:1, one launch (start us, length us, event | category | flops | bytes accessed | tf_op | source)
XLA Modules:
  0.0 160.0 jit_solution(11317287255761105031)
XLA Ops:
  2.7 3.3 %collective-permute-start.1 = (bf16[128,256]{1,0:T(8,128)(2,1)S(1)}, bf16[128,256]{1,0:T(8,128)(2,1)S(1)}, u32[]{:S(2)}, u32[]{:S(2)}) collective-permute-start(bf16[128,256]{1,0:T(8,128)(2,1)S(1)} %convolution_convert_fusion.3), channel_id=1, source_target_pairs={{16,0},{32,16},{48,32},{64,48},{80,64},{96,80},{112,96},{17,1},{33... | collective-permute-start | bytes 196616 | tf_op jit(solution)/shard_map/ppermute | solution.py:331
  6.0 3.1 %collective-permute-start = (bf16[128,256]{1,0:T(8,128)(2,1)S(1)}, bf16[128,256]{1,0:T(8,128)(2,1)S(1)}, u32[]{:S(2)}, u32[]{:S(2)}) collective-permute-start(bf16[128,256]{1,0:T(8,128)(2,1)S(1)} %convolution_convert_fusion.3), channel_id=1, source_target_pairs={{0,16},{16,32},{32,48},{48,64},{64,80},{80,96},{96,112},{1,17},{17... | collective-permute-start | bytes 196616 | tf_op jit(solution)/shard_map/ppermute | solution.py:331
  10.4 6.3 %collective-permute-start.3 = (bf16[3,128,256]{2,1,0:T(8,128)(2,1)S(1)}, bf16[3,128,256]{2,1,0:T(8,128)(2,1)S(1)}, u32[]{:S(2)}, u32[]{:S(2)}) collective-permute-start(bf16[3,128,256]{2,1,0:T(8,128)(2,1)S(1)} %get-tuple-element.56), channel_id=1, source_target_pairs={{0,15},{1,0},{2,1},{3,2},{4,3},{5,4},{6,5},{7,6},{8,7},{9,8},{10,9... | collective-permute-start | bytes 589832 | tf_op jit(solution)/shard_map/ppermute | solution.py:331
  17.6 3.3 %collective-permute-done.3 = bf16[3,128,256]{2,1,0:T(8,128)(2,1)S(1)} collective-permute-done((bf16[3,128,256]{2,1,0:T(8,128)(2,1)S(1)}, bf16[3,128,256]{2,1,0:T(8,128)(2,1)S(1)}, u32[]{:S(2)}, u32[]{:S(2)}) %collective-permute-start.3) | collective-permute-done | bytes 196640 | tf_op jit(solution)/shard_map/ppermute | solution.py:331
  20.9 5.5 %collective-permute-done.2 = bf16[3,128,256]{2,1,0:T(8,128)(2,1)S(1)} collective-permute-done((bf16[3,128,256]{2,1,0:T(8,128)(2,1)S(1)}, bf16[3,128,256]{2,1,0:T(8,128)(2,1)S(1)}, u32[]{:S(2)}, u32[]{:S(2)}) %collective-permute-start.2) | collective-permute-done | bytes 196640 | tf_op jit(solution)/shard_map/ppermute | solution.py:331
  26.6 5.8 %shard_map.255 = (bf16[160,512]{1,0:T(8,128)(2,1)S(1)}, bf16[128,512]{1,0:T(8,128)(2,1)S(1)}, bf16[1024,256]{1,0:T(8,128)(2,1)S(1)}, bf16[1024,512]{1,0:T(8,128)...) custom-call(s32[1]{0:T(128)S(6)} %copy.31.live_ref, ...), custom_call_target="tpu_custom_call" | custom-call | bytes 8388608 | tf_op jit(solution)/shard_map/pallas_call | solution.py:314
  37.3 3.6 %collective-permute-start.4 = (bf16[128,512]{1,0:T(8,128)(2,1)S(1)}, bf16[128,512]{1,0:T(8,128)(2,1)S(1)}, u32[]{:S(2)}, u32[]{:S(2)}) collective-permute-start(bf16[128,512]{1,0:T(8,128)(2,1)S(1)} %get-tuple-element.23), channel_id=1, source_target_pairs={{0,16},{16,32},{32,48},{48,64},{64,80},{80,96},{96,112},{1,17},{17... | collective-permute-start | bytes 393224 | tf_op jit(solution)/shard_map/ppermute | solution.py:331
  45.0 7.3 %collective-permute-done.7 = bf16[3,128,512]{2,1,0:T(8,128)(2,1)S(1)} collective-permute-done((bf16[3,128,512]{2,1,0:T(8,128)(2,1)S(1)}, bf16[3,128,512]{2,1,0:T(8,128)(2,1)S(1)}, u32[]{:S(2)}, u32[]{:S(2)}) %collective-permute-start.7) | collective-permute-done | bytes 393248 | tf_op jit(solution)/shard_map/ppermute | solution.py:331
  52.4 3.1 %collective-permute-done.6 = bf16[3,128,512]{2,1,0:T(8,128)(2,1)S(1)} collective-permute-done((bf16[3,128,512]{2,1,0:T(8,128)(2,1)S(1)}, bf16[3,128,512]{2,1,0:T(8,128)(2,1)S(1)}, u32[]{:S(2)}, u32[]{:S(2)}) %collective-permute-start.6) | collective-permute-done | bytes 393248 | tf_op jit(solution)/shard_map/ppermute | solution.py:331
  57.3 8.6 %shard_map.256 = (bf16[160,512]{1,0:T(8,128)(2,1)}, f32[160,512]{1,0:T(8,128)S(1)}, bf16[1152,512]{1,0:T(8,128)(2,1)S(1)}, bf16[1024,512]{1,0:T(8,128)(2,1)S(1)}...) custom-call(s32[1]{0:T(128)S(6)} %copy.32.live_ref, s32[8]{0:T(128)S(1)} %copy-done.32, ...), custom_call_target="tpu_custom_call" | custom-call | bytes 8388608 | tf_op jit(solution)/shard_map/pallas_call | solution.py:314
  70.7 5.4 %collective-permute-start.9 = (bf16[384,512]{1,0:T(8,128)(2,1)}, bf16[384,512]{1,0:T(8,128)(2,1)}, u32[]{:S(2)}, u32[]{:S(2)}) collective-permute-start(bf16[384,512]{1,0:T(8,128)(2,1)} %get-tuple-element.45), channel_id=1, source_target_pairs={{0,16},{16,32},{32,48},{48,64},{64,80},{80,96},{96,112},{1,17},{17... | collective-permute-start | bytes 1179656 | tf_op jit(solution)/shard_map/ppermute | solution.py:331
  76.1 2.3 %convolution_convert_fusion = bf16[512,512]{1,0:T(8,128)(2,1)S(1)} fusion(bf16[1024,512]{1,0:T(8,128)(2,1)} %copy-done.35, bf16[1024,512]{1,0:T(8,128)(2,1)} %copy-done.36), kind=kOutput, calls=%fused_computation.2 | convolution fusion | flops 537133056 | bytes 2621440 | tf_op jit(solution)/shard_map/dot_general | solution.py:24
  86.6 3.6 %collective-permute-done.10.from_left = bf16[128,512]{1,0:T(8,128)(2,1)S(1)} collective-permute-done((bf16[128,512]{1,0:T(8,128)(2,1)S(1)}, bf16[128,512]{1,0:T(8,128)(2,1)S(1)}, u32[]{:S(2)}, u32[]{:S(2)}) %collective-permute-start.10) | collective-permute-done | bytes 131104 | tf_op jit(solution)/shard_map/ppermute | solution.py:331
  90.3 3.3 %shard_map.257 = (bf16[1024,512]{1,0:T(8,128)(2,1)S(1)}, bf16[1024,512]{1,0:T(8,128)(2,1)S(1)}) custom-call(s32[1]{0:T(128)S(6)} %copy.31.live_ref, s32[8,128]{1,0:T(8,128)S(1)} %copy-done.22, s32[1,128]{1,0:T(1,128)S(1)} %bitcast.34, f32[160,512]{1,0:T(8,128)S(1)} %convolution_add_fusion.state_part, f32[160,512]{1,0:T(8,128)S(1)} %copy-done.19, ...), custom_call_target="tpu_custom_call" | custom-call | bytes 8388608 | tf_op jit(solution)/shard_map/pallas_call | solution.py:314
  98.0 3.5 %collective-permute-start.13 = (bf16[320,512]{1,0:T(8,128)(2,1)S(1)}, bf16[320,512]{1,0:T(8,128)(2,1)S(1)}, u32[]{:S(2)}, u32[]{:S(2)}) collective-permute-start(bf16[320,512]{1,0:T(8,128)(2,1)S(1)} %constant_dynamic-slice_fusion.1), channel_id=1, source_target_pairs={{0,32},{16,48},{32,0},{48,16},{64,96},{80,112},{96,64},{112,80},{1... | collective-permute-start | bytes 983048 | tf_op jit(solution)/shard_map/ppermute | solution.py:343
  101.5 7.8 %collective-permute-done.13 = bf16[320,512]{1,0:T(8,128)(2,1)S(1)} collective-permute-done((bf16[320,512]{1,0:T(8,128)(2,1)S(1)}, bf16[320,512]{1,0:T(8,128)(2,1)S(1)}, u32[]{:S(2)}, u32[]{:S(2)}) %collective-permute-start.13) | collective-permute-done | bytes 327712 | tf_op jit(solution)/shard_map/ppermute | solution.py:343
  111.0 4.6 %collective-permute-done.14 = bf16[160,512]{1,0:T(8,128)(2,1)S(1)} collective-permute-done((bf16[160,512]{1,0:T(8,128)(2,1)S(1)}, bf16[160,512]{1,0:T(8,128)(2,1)S(1)}, u32[]{:S(2)}, u32[]{:S(2)}) %collective-permute-start.14) | collective-permute-done | bytes 163872 | tf_op jit(solution)/shard_map/ppermute | solution.py:343
  115.7 4.2 %collective-permute-done.15 = bf16[160,512]{1,0:T(8,128)(2,1)S(1)} collective-permute-done((bf16[160,512]{1,0:T(8,128)(2,1)S(1)}, bf16[160,512]{1,0:T(8,128)(2,1)S(1)}, u32[]{:S(2)}, u32[]{:S(2)}) %collective-permute-start.15) | collective-permute-done | bytes 163872 | tf_op jit(solution)/shard_map/ppermute | solution.py:343
  120.0 5.4 %collective-permute-done.16 = bf16[160,512]{1,0:T(8,128)(2,1)S(1)} collective-permute-done((bf16[160,512]{1,0:T(8,128)(2,1)S(1)}, bf16[160,512]{1,0:T(8,128)(2,1)S(1)}, u32[]{:S(2)}, u32[]{:S(2)}) %collective-permute-start.16) | collective-permute-done | bytes 163872 | tf_op jit(solution)/shard_map/ppermute | solution.py:343
  125.5 4.2 %collective-permute-done.17 = bf16[160,512]{1,0:T(8,128)(2,1)S(1)} collective-permute-done((bf16[160,512]{1,0:T(8,128)(2,1)S(1)}, bf16[160,512]{1,0:T(8,128)(2,1)S(1)}, u32[]{:S(2)}, u32[]{:S(2)}) %collective-permute-start.17) | collective-permute-done | bytes 163872 | tf_op jit(solution)/shard_map/ppermute | solution.py:343
  129.8 5.4 %collective-permute-done.18 = bf16[160,512]{1,0:T(8,128)(2,1)S(1)} collective-permute-done((bf16[160,512]{1,0:T(8,128)(2,1)S(1)}, bf16[160,512]{1,0:T(8,128)(2,1)S(1)}, u32[]{:S(2)}, u32[]{:S(2)}) %collective-permute-start.18) | collective-permute-done | bytes 163872 | tf_op jit(solution)/shard_map/ppermute | solution.py:343
  136.4 4.5 %collective-permute-done.19 = bf16[160,512]{1,0:T(8,128)(2,1)S(1)} collective-permute-done((bf16[160,512]{1,0:T(8,128)(2,1)S(1)}, bf16[160,512]{1,0:T(8,128)(2,1)S(1)}, u32[]{:S(2)}, u32[]{:S(2)}) %collective-permute-start.19) | collective-permute-done | bytes 163872 | tf_op jit(solution)/shard_map/ppermute | solution.py:343
  141.1 6.2 %collective-permute-done.20 = bf16[320,512]{1,0:T(8,128)(2,1)S(1)} collective-permute-done((bf16[320,512]{1,0:T(8,128)(2,1)S(1)}, bf16[320,512]{1,0:T(8,128)(2,1)S(1)}, u32[]{:S(2)}, u32[]{:S(2)}) %collective-permute-start.20) | collective-permute-done | bytes 327712 | tf_op jit(solution)/shard_map/ppermute | solution.py:343
  147.5 8.2 %collective-permute-start.21 = (bf16[640,512]{1,0:T(8,128)(2,1)S(1)}, bf16[640,512]{1,0:T(8,128)(2,1)S(1)}, u32[]{:S(2)}, u32[]{:S(2)}) collective-permute-start(bf16[640,512]{1,0:T(8,128)(2,1)S(1)} %pad_maximum_fusion.2), channel_id=1, source_target_pairs={{0,16},{16,0},{32,48},{48,32},{64,80},{80,64},{96,112},{112,96},{1... | collective-permute-start | bytes 1966088 | tf_op jit(solution)/shard_map/ppermute | solution.py:343
  (138 shorter events, 39.1 us)
Async XLA Ops:
  2.7 6.5 %collective-permute-start.1 = (bf16[128,256]{1,0:T(8,128)(2,1)S(1)}, bf16[128,256]{1,0:T(8,128)(2,1)S(1)}, u32[]{:S(2)}, u32[]{:S(2)}) collective-permute-start(bf16[128,256]{1,0:T(8,128)(2,1)S(1)} %convolution_convert_fusion.3), channel_id=1, source_target_pairs={{16,0},{32,16},{48,32},{64,48},{80,64},{96,80},{112,96},{17,1},{33... | collective-permute-start | bytes 196616 | tf_op jit(solution)/shard_map/ppermute | solution.py:331
  6.0 4.4 %collective-permute-start = (bf16[128,256]{1,0:T(8,128)(2,1)S(1)}, bf16[128,256]{1,0:T(8,128)(2,1)S(1)}, u32[]{:S(2)}, u32[]{:S(2)}) collective-permute-start(bf16[128,256]{1,0:T(8,128)(2,1)S(1)} %convolution_convert_fusion.3), channel_id=1, source_target_pairs={{0,16},{16,32},{32,48},{48,64},{64,80},{80,96},{96,112},{1,17},{17... | collective-permute-start | bytes 196616 | tf_op jit(solution)/shard_map/ppermute | solution.py:331
  10.4 10.4 %collective-permute-start.3 = (bf16[3,128,256]{2,1,0:T(8,128)(2,1)S(1)}, bf16[3,128,256]{2,1,0:T(8,128)(2,1)S(1)}, u32[]{:S(2)}, u32[]{:S(2)}) collective-permute-start(bf16[3,128,256]{2,1,0:T(8,128)(2,1)S(1)} %get-tuple-element.56), channel_id=1, source_target_pairs={{0,15},{1,0},{2,1},{3,2},{4,3},{5,4},{6,5},{7,6},{8,7},{9,8},{10,9... | collective-permute-start | bytes 589832 | tf_op jit(solution)/shard_map/ppermute | solution.py:331
  16.7 9.7 %collective-permute-start.2 = (bf16[3,128,256]{2,1,0:T(8,128)(2,1)S(1)}, bf16[3,128,256]{2,1,0:T(8,128)(2,1)S(1)}, u32[]{:S(2)}, u32[]{:S(2)}) collective-permute-start(bf16[3,128,256]{2,1,0:T(8,128)(2,1)S(1)} %get-tuple-element.56), channel_id=1, source_target_pairs={{0,1},{1,2},{2,3},{3,4},{4,5},{5,6},{6,7},{7,8},{8,9},{9,10},{10,1... | collective-permute-start | bytes 589832 | tf_op jit(solution)/shard_map/ppermute | solution.py:331
  35.0 20.7 %copy-start.8 = (bf16[1024,512]{1,0:T(8,128)(2,1)}, bf16[1024,512]{1,0:T(8,128)(2,1)S(1)}, u32[]{:S(2)}) copy-start(bf16[1024,512]{1,0:T(8,128)(2,1)S(1)} %get-tuple-element.33.mix_slope) | copy-start | bytes 3145732
  35.0 20.7 %copy-start.10 = (bf16[1024,512]{1,0:T(8,128)(2,1)}, bf16[1024,512]{1,0:T(8,128)(2,1)S(1)}, u32[]{:S(2)}) copy-start(bf16[1024,512]{1,0:T(8,128)(2,1)S(1)} %get-tuple-element.31.normed_all) | copy-start | bytes 3145732
  35.0 6.6 %collective-permute-start.5 = (bf16[128,512]{1,0:T(8,128)(2,1)S(1)}, bf16[128,512]{1,0:T(8,128)(2,1)S(1)}, u32[]{:S(2)}, u32[]{:S(2)}) collective-permute-start(bf16[128,512]{1,0:T(8,128)(2,1)S(1)} %get-tuple-element.23), channel_id=1, source_target_pairs={{16,0},{32,16},{48,32},{64,48},{80,64},{96,80},{112,96},{17,1},{33... | collective-permute-start | bytes 393224 | tf_op jit(solution)/shard_map/ppermute | solution.py:331
  37.3 5.5 %collective-permute-start.4 = (bf16[128,512]{1,0:T(8,128)(2,1)S(1)}, bf16[128,512]{1,0:T(8,128)(2,1)S(1)}, u32[]{:S(2)}, u32[]{:S(2)}) collective-permute-start(bf16[128,512]{1,0:T(8,128)(2,1)S(1)} %get-tuple-element.23), channel_id=1, source_target_pairs={{0,16},{16,32},{32,48},{48,64},{64,80},{80,96},{96,112},{1,17},{17... | collective-permute-start | bytes 393224 | tf_op jit(solution)/shard_map/ppermute | solution.py:331
  42.9 9.5 %collective-permute-start.7 = (bf16[3,128,512]{2,1,0:T(8,128)(2,1)S(1)}, bf16[3,128,512]{2,1,0:T(8,128)(2,1)S(1)}, u32[]{:S(2)}, u32[]{:S(2)}) collective-permute-start(bf16[3,128,512]{2,1,0:T(8,128)(2,1)S(1)} %get-tuple-element.52), channel_id=1, source_target_pairs={{0,15},{1,0},{2,1},{3,2},{4,3},{5,4},{6,5},{7,6},{8,7},{9,8},{10,9... | collective-permute-start | bytes 1179656 | tf_op jit(solution)/shard_map/ppermute | solution.py:331
  43.0 12.5 %collective-permute-start.6 = (bf16[3,128,512]{2,1,0:T(8,128)(2,1)S(1)}, bf16[3,128,512]{2,1,0:T(8,128)(2,1)S(1)}, u32[]{:S(2)}, u32[]{:S(2)}) collective-permute-start(bf16[3,128,512]{2,1,0:T(8,128)(2,1)S(1)} %get-tuple-element.52), channel_id=1, source_target_pairs={{0,1},{1,2},{2,3},{3,4},{4,5},{5,6},{6,7},{7,8},{8,9},{9,10},{10,1... | collective-permute-start | bytes 1179656 | tf_op jit(solution)/shard_map/ppermute | solution.py:331
  68.8 11.1 %collective-permute-start.8 = (bf16[384,512]{1,0:T(8,128)(2,1)}, bf16[384,512]{1,0:T(8,128)(2,1)}, u32[]{:S(2)}, u32[]{:S(2)}) collective-permute-start(bf16[384,512]{1,0:T(8,128)(2,1)} %get-tuple-element.44), channel_id=1, source_target_pairs={{16,0},{32,16},{48,32},{64,48},{80,64},{96,80},{112,96},{17,1},{33... | collective-permute-start | bytes 1179656 | tf_op jit(solution)/shard_map/ppermute | solution.py:331
  70.7 10.4 %collective-permute-start.9 = (bf16[384,512]{1,0:T(8,128)(2,1)}, bf16[384,512]{1,0:T(8,128)(2,1)}, u32[]{:S(2)}, u32[]{:S(2)}) collective-permute-start(bf16[384,512]{1,0:T(8,128)(2,1)} %get-tuple-element.45), channel_id=1, source_target_pairs={{0,16},{16,32},{32,48},{48,64},{64,80},{80,96},{96,112},{1,17},{17... | collective-permute-start | bytes 1179656 | tf_op jit(solution)/shard_map/ppermute | solution.py:331
  82.7 3.9 %collective-permute-start.11 = (bf16[128,512]{1,0:T(8,128)(2,1)S(1)}, bf16[128,512]{1,0:T(8,128)(2,1)S(1)}, u32[]{:S(2)}, u32[]{:S(2)}) collective-permute-start(bf16[128,512]{1,0:T(8,128)(2,1)S(1)} %get-tuple-element.48), channel_id=1, source_target_pairs={{0,15},{1,0},{2,1},{3,2},{4,3},{5,4},{6,5},{7,6},{8,7},{9,8},{10,9... | collective-permute-start | bytes 393224 | tf_op jit(solution)/shard_map/ppermute | solution.py:331
  82.8 7.4 %collective-permute-start.10 = (bf16[128,512]{1,0:T(8,128)(2,1)S(1)}, bf16[128,512]{1,0:T(8,128)(2,1)S(1)}, u32[]{:S(2)}, u32[]{:S(2)}) collective-permute-start(bf16[128,512]{1,0:T(8,128)(2,1)S(1)} %get-tuple-element.49), channel_id=1, source_target_pairs={{0,1},{1,2},{2,3},{3,4},{4,5},{5,6},{6,7},{7,8},{8,9},{9,10},{10,1... | collective-permute-start | bytes 393224 | tf_op jit(solution)/shard_map/ppermute | solution.py:331
  95.6 2.2 %collective-permute-start.12 = (bf16[640,512]{1,0:T(8,128)(2,1)S(1)}, bf16[640,512]{1,0:T(8,128)(2,1)S(1)}, u32[]{:S(2)}, u32[]{:S(2)}) collective-permute-start(bf16[640,512]{1,0:T(8,128)(2,1)S(1)} %constant_dynamic-slice_fusion.2), channel_id=1, source_target_pairs={{0,16},{16,0},{32,48},{48,32},{64,80},{80,64},{96,112},{112,96},{1... | collective-permute-start | bytes 1966088 | tf_op jit(solution)/shard_map/ppermute | solution.py:343
  98.0 11.2 %collective-permute-start.13 = (bf16[320,512]{1,0:T(8,128)(2,1)S(1)}, bf16[320,512]{1,0:T(8,128)(2,1)S(1)}, u32[]{:S(2)}, u32[]{:S(2)}) collective-permute-start(bf16[320,512]{1,0:T(8,128)(2,1)S(1)} %constant_dynamic-slice_fusion.1), channel_id=1, source_target_pairs={{0,32},{16,48},{32,0},{48,16},{64,96},{80,112},{96,64},{112,80},{1... | collective-permute-start | bytes 983048 | tf_op jit(solution)/shard_map/ppermute | solution.py:343
  109.4 6.1 %collective-permute-start.14 = (bf16[160,512]{1,0:T(8,128)(2,1)S(1)}, bf16[160,512]{1,0:T(8,128)(2,1)S(1)}, u32[]{:S(2)}, u32[]{:S(2)}) collective-permute-start(bf16[160,512]{1,0:T(8,128)(2,1)S(1)} %constant_dynamic-slice_fusion), channel_id=1, source_target_pairs={{0,96},{16,112},{32,64},{48,80},{64,32},{80,48},{96,0},{112,16},{1... | collective-permute-start | bytes 491528 | tf_op jit(solution)/shard_map/ppermute | solution.py:343
  115.6 4.2 %collective-permute-start.15 = (bf16[160,512]{1,0:T(8,128)(2,1)S(1)}, bf16[160,512]{1,0:T(8,128)(2,1)S(1)}, u32[]{:S(2)}, u32[]{:S(2)}) collective-permute-start(bf16[160,512]{1,0:T(8,128)(2,1)S(1)} %add_convert_fusion.7), channel_id=1, source_target_pairs={{0,1},{1,0},{2,3},{3,2},{4,5},{5,4},{6,7},{7,6},{8,9},{9,8},{10,11... | collective-permute-start | bytes 491528 | tf_op jit(solution)/shard_map/ppermute | solution.py:343
  119.9 5.5 %collective-permute-start.16 = (bf16[160,512]{1,0:T(8,128)(2,1)S(1)}, bf16[160,512]{1,0:T(8,128)(2,1)S(1)}, u32[]{:S(2)}, u32[]{:S(2)}) collective-permute-start(bf16[160,512]{1,0:T(8,128)(2,1)S(1)} %add_convert_fusion.6), channel_id=1, source_target_pairs={{0,3},{1,2},{2,1},{3,0},{4,7},{5,6},{6,5},{7,4},{8,11},{9,10},{10,... | collective-permute-start | bytes 491528 | tf_op jit(solution)/shard_map/ppermute | solution.py:343
  125.4 4.2 %collective-permute-start.17 = (bf16[160,512]{1,0:T(8,128)(2,1)S(1)}, bf16[160,512]{1,0:T(8,128)(2,1)S(1)}, u32[]{:S(2)}, u32[]{:S(2)}) collective-permute-start(bf16[160,512]{1,0:T(8,128)(2,1)S(1)} %add_convert_fusion.5), channel_id=1, source_target_pairs={{0,4},{1,5},{2,6},{3,7},{4,0},{5,1},{6,2},{7,3},{8,12},{9,13},{10,... | collective-permute-start | bytes 491528 | tf_op jit(solution)/shard_map/ppermute | solution.py:343
  129.7 5.5 %collective-permute-start.18 = (bf16[160,512]{1,0:T(8,128)(2,1)S(1)}, bf16[160,512]{1,0:T(8,128)(2,1)S(1)}, u32[]{:S(2)}, u32[]{:S(2)}) collective-permute-start(bf16[160,512]{1,0:T(8,128)(2,1)S(1)} %add_convert_fusion.4), channel_id=1, source_target_pairs={{0,12},{1,13},{2,14},{3,15},{4,8},{5,9},{6,10},{7,11},{8,4},{9,5},... | collective-permute-start | bytes 491528 | tf_op jit(solution)/shard_map/ppermute | solution.py:343
  135.2 5.8 %collective-permute-start.19 = (bf16[160,512]{1,0:T(8,128)(2,1)S(1)}, bf16[160,512]{1,0:T(8,128)(2,1)S(1)}, u32[]{:S(2)}, u32[]{:S(2)}) collective-permute-start(bf16[160,512]{1,0:T(8,128)(2,1)S(1)} %add_convert_fusion.3), channel_id=1, source_target_pairs={{0,96},{16,112},{32,64},{48,80},{64,32},{80,48},{96,0},{112,16},{1... | collective-permute-start | bytes 491528 | tf_op jit(solution)/shard_map/ppermute | solution.py:343
  141.0 6.3 %collective-permute-start.20 = (bf16[320,512]{1,0:T(8,128)(2,1)S(1)}, bf16[320,512]{1,0:T(8,128)(2,1)S(1)}, u32[]{:S(2)}, u32[]{:S(2)}) collective-permute-start(bf16[320,512]{1,0:T(8,128)(2,1)S(1)} %pad_maximum_fusion.6), channel_id=1, source_target_pairs={{0,32},{16,48},{32,0},{48,16},{64,96},{80,112},{96,64},{112,80},{1... | collective-permute-start | bytes 983048 | tf_op jit(solution)/shard_map/ppermute | solution.py:343
  147.5 9.9 %collective-permute-start.21 = (bf16[640,512]{1,0:T(8,128)(2,1)S(1)}, bf16[640,512]{1,0:T(8,128)(2,1)S(1)}, u32[]{:S(2)}, u32[]{:S(2)}) collective-permute-start(bf16[640,512]{1,0:T(8,128)(2,1)S(1)} %pad_maximum_fusion.2), channel_id=1, source_target_pairs={{0,16},{16,0},{32,48},{48,32},{64,80},{80,64},{96,112},{112,96},{1... | collective-permute-start | bytes 1966088 | tf_op jit(solution)/shard_map/ppermute | solution.py:343
  (38 other events, 223.7 us)
where the time goes:
time: 160 us
  waiting for transfers between devices  76.7 us (48%)
  starting transfers between devices  43.8 us (27%)
  Pallas kernels  17.6 us (11%)
  local copies, waits for them, and re-layouts  9.23 us (6%)
  other arithmetic  5.25 us (3%)
  matrix products  4.71 us (3%)
  between operations  2.69 us (2%)
    ppermute x10, waiting for transfers between devices, partner(): lax.ppermute(x, axis, [(i, i ^ flip) for i in range(lax.axis_size(axis))])  45.9 us
    ppermute x12, waiting for transfers between devices, shifted(): return lax.ppermute(x, axis, pairs)  30.8 us
    ppermute x12, starting transfers between devices, shifted(): return lax.ppermute(x, axis, pairs)  28.9 us
    pallas_call x3, Pallas kernels, call(): pl.pallas_call(kernel, out_shape=[jax.ShapeDtypeStruct(shape, dtype) for...  17.6 us
    ppermute x10, starting transfers between devices, partner(): lax.ppermute(x, axis, [(i, i ^ flip) for i in range(lax.axis_size(axis))])  14.9 us
    unnamed x81, local copies, waits for them, and re-layouts  7.95 us
    dot_general x3, matrix products, cross_dot(): lax.dot_general(left, right, (((0,), (0,)), ((), ())), preferred_element_...  3.51 us
  transfers between devices with their start and end apart: 22, of which 21 were waited for; matrix products, arithmetic and copies ran while one was open for 2% of the time, Pallas kernels for 0%

commit v1 on v0

--- a/solution.py
+++ b/solution.py
@@ -62,16 +62,31 @@
     return jnp.where(block < live, rows[pl.ds(block, 1), :], -1)
 
 
-def window(slots, block, own_rows, copy_rows):
-    slot = slots[block]
-    return pl.multiple_of(jnp.where(slot == 4, 0, own_rows + slot * copy_rows), lanes)
+def window(starts, block):
+    return pl.multiple_of(starts[block], lanes)
+
+
+def fill(table, own, near):
+    table[0 : own.shape[0], :] = own[...]
+    first = own.shape[0] + -own.shape[0] % lanes
+    if first > own.shape[0]:
+        table[own.shape[0] : first, :] = jnp.zeros_like(table[own.shape[0] : first, :])
+    for part in near:
+        table[first : first + part.shape[0], :] = part[...]
+        first += part.shape[0]
+    table[first:, :] = jnp.zeros_like(table[first:, :])
 
 
 def encode_kernel(
     live_ref,
-    slots,
+    starts,
     grid_own,
-    grid_near,
+    near_left,
+    near_right,
+    near_inner,
+    near_inner_corners,
+    near_outer,
+    near_outer_corners,
     base,
     senders,
     receivers,
@@ -96,12 +111,14 @@
     projected,
     total,
 ):
-    own, copies = grid_own.shape[0], grid_near.shape[0]
+    own = grid_own.shape[0]
     nodes = base.shape[0]
     live = live_ref[0]
-    table[0:own, :] = grid_own[...]
-    table[own : own + copies, :] = grid_near[...]
-    table[own + copies :, :] = jnp.zeros_like(table[own + copies :, :])
+    fill(
+        table,
+        grid_own,
+        (near_left, near_right, near_inner, near_inner_corners, near_outer, near_outer_corners),
+    )
     projected[0:nodes, :] = dot(base[...], receiver_weight[...]).astype(bf16)
     projected[nodes:, :] = jnp.zeros_like(projected[nodes:, :])
     total[...] = jnp.zeros_like(total)
@@ -111,7 +128,7 @@
         gathered, received, placed = [], [], []
         for part in range(blocks_per_turn):
             block = step * blocks_per_turn + part
-            start = window(slots, block, own, lanes)
+            start = window(starts, block)
             pick = lane_hot(senders[pl.ds(block, 1), :], own)
             gathered.append(dot(pick, table[pl.ds(start, own), :]).astype(bf16))
             ends = live_row(receivers, block, live)
@@ -152,9 +169,14 @@
 
 def process_kernel(
     live_ref,
-    slots,
+    starts,
     state,
-    near,
+    near_left,
+    near_right,
+    near_inner,
+    near_inner_corners,
+    near_outer,
+    near_outer_corners,
     senders,
     receivers,
     edge_sender,
@@ -165,7 +187,9 @@
     cotangent,
     mesh_out,
     own_grad,
-    leaving,
+    to_lon,
+    to_inner,
+    to_outer,
     sender_rows,
     mix_grad_out,
     receiver_grad,
@@ -179,13 +203,14 @@
     table_grad,
     receiver_total,
 ):
-    nodes, copies = state.shape[0], near.shape[0]
+    nodes = state.shape[0]
     reach = 256
     live = live_ref[0]
-    table[0:nodes, :] = state[...]
-    table[nodes:reach, :] = jnp.zeros_like(table[nodes:reach, :])
-    table[reach : reach + copies, :] = near[...]
-    table[reach + copies :, :] = jnp.zeros_like(table[reach + copies :, :])
+    fill(
+        table,
+        state,
+        (near_left, near_right, near_inner, near_inner_corners, near_outer, near_outer_corners),
+    )
     terms[0:nodes, :] = dot(state[...], edge_receiver[...]).astype(bf16)
     terms[nodes:, :] = jnp.zeros_like(terms[nodes:, :])
     total[...] = jnp.zeros_like(total)
@@ -196,7 +221,7 @@
         gathered, received, placed = [], [], []
         for part in range(blocks_per_turn):
             block = step * blocks_per_turn + part
-            start = window(slots, block, reach, lanes)
+            start = window(starts, block)
             pick = lane_hot(senders[pl.ds(block, 1), :], reach)
             gathered.append(dot(pick, table[pl.ds(start, reach), :]).astype(bf16))
             ends = live_row(receivers, block, live)
@@ -241,7 +266,7 @@
         receiver_total[...] += dot(jnp.concatenate(placed, 1), mix_grad)
         for part in range(blocks_per_turn):
             block = step * blocks_per_turn + part
-            start = window(slots, block, reach, lanes)
+            start = window(starts, block)
             place = row_hot(senders[pl.ds(block, 1), :], nodes)
             table_grad[pl.ds(start, nodes), :] += dot(
                 place, mix_grad[part * lanes : (part + 1) * lanes, :]
@@ -250,7 +275,10 @@
 
     lax.fori_loop(0, turns, backward, 0)
     own_grad[...] = table_grad[0:nodes, :]
-    leaving[...] = table_grad[reach : reach + copies, :].astype(bf16)
+    first = reach
+    for part in (to_lon, to_inner, to_outer):
+        part[...] = table_grad[first : first + part.shape[0], :].astype(bf16)
+        first += part.shape[0]
     receiver_grad[...] = receiver_total[...].astype(bf16)
 
 
@@ -260,7 +288,8 @@
     export,
     state_part,
     own_grad,
-    kept,
+    from_inner,
+    from_outer,
     from_left,
     from_right,
     edge_sender,
@@ -280,7 +309,9 @@
 ):
     nodes = state_part.shape[0]
     live = live_ref[0]
-    arrived = kept[...].astype(f32) + from_left[...].astype(f32) + from_right[...].astype(f32)
+    arrived = from_left[...].astype(f32) + from_right[...].astype(f32)
+    copies = arrived.shape[0]
+    arrived += from_inner[0:copies, :].astype(f32) + from_outer[0:copies, :].astype(f32)
     table_grad = own_grad[...] + dot(row_hot(export[...], nodes), arrived.astype(bf16))
     state_grad = state_part[...] + back_dot(table_grad.astype(bf16), edge_sender[...])
     update_grad = norm_back(update_normed[...], update_scale[:, 0:1], state_grad * gain[...])
@@ -308,7 +339,7 @@
     lax.fori_loop(0, receivers.shape[0] // blocks_per_turn, turn, 0)
 
 
-def call(kernel, operands, outs, scratch, scalars=1, flops=0):
+def call(kernel, operands, outs, scratch, scalars, mib):
     smem = pl.BlockSpec(memory_space=pltpu.SMEM)
     vmem = pl.BlockSpec(memory_space=pltpu.VMEM)
     return pl.pallas_call(
@@ -317,55 +348,81 @@
         in_specs=[smem] * scalars + [vmem] * (len(operands) - scalars),
         out_specs=[vmem] * len(outs),
         scratch_shapes=[pltpu.VMEM(shape, dtype) for shape, dtype in scratch],
-        compiler_params=pltpu.CompilerParams(vmem_limit_bytes=40 * 1024 * 1024),
-        cost_estimate=pl.CostEstimate(flops=flops, bytes_accessed=8 << 20, transcendentals=0),
+        compiler_params=pltpu.CompilerParams(vmem_limit_bytes=mib << 20),
+        cost_estimate=pl.CostEstimate(flops=4 << 30, bytes_accessed=8 << 20, transcendentals=0),
     )(*operands)
 
 
-def shifted(x, axis, step):
-    size = lax.axis_size(axis)
-    if axis == "lon":
-        pairs = [(i, (i + step) % size) for i in range(size)]
-    else:
-        pairs = [(i, i + step) for i in range(size) if 0 <= i + step < size]
-    return lax.ppermute(x, axis, pairs)
-
-
-def around(rows):
-    for axis in ("lat", "lon"):
-        before, after = shifted(rows, axis, 1), shifted(rows, axis, -1)
-        dim = 0 if axis == "lat" else 1
-        rows = jnp.stack([before, rows, after], dim)
-    return rows.reshape(9 * rows.shape[2], rows.shape[3])
+def shifted(x, step):
+    size = lax.axis_size("lon")
+    return lax.ppermute(x, "lon", [(i, (i + step) % size) for i in range(size)])
 
 
 def partner(x, axis, flip):
     return lax.ppermute(x, axis, [(i, i ^ flip) for i in range(lax.axis_size(axis))])
 
 
-def add(left, right):
-    return (left.astype(f32) + right.astype(f32)).astype(bf16)
-
-
-halving = (("lat", 1, 0), ("lat", 2, 1), ("lat", 6, 2))
-doubling = (("lon", 1), ("lon", 3), ("lon", 4), ("lon", 12))
+def inner(x):
+    return partner(x, "lat", 1)
+
+
+def outer(x):
+    ends = range(1, lax.axis_size("lat") - 1, 2)
+    return lax.ppermute(x, "lat", [(i, i + 1) for i in ends] + [(i + 1, i) for i in ends])
+
+
+def around(rows):
+    left, right = shifted(rows, 1), shifted(rows, -1)
+    corners = jnp.concatenate([left, right], 0)
+    return left, right, inner(rows), inner(corners), outer(rows), outer(corners)
+
+
+even_places = (6, 5, 7, 0, -1, 1, 3, 2, 4)
+odd_places = (3, 2, 4, 0, -1, 1, 6, 5, 7)
+
+
+def start_rows(slots, own):
+    places = jnp.where(
+        lax.axis_index("lat") % 2 == 0, jnp.array(even_places), jnp.array(odd_places)
+    )
+    pick = slots[:, None] == jnp.arange(9)[None, :]
+    place = jnp.sum(jnp.where(pick, places[None, :], 0), 1).astype(jnp.int32)
+    return jnp.where(place < 0, 0, own + lanes * place)
+
+
+flips = (1, 3, 2)
+
+
+def total(values):
+    own, one, three, two = [part.astype(f32) for part in values]
+    return ((own + one) + (two + three)).astype(bf16)
 
 
 def summed(values):
     index = lax.axis_index("lat")
-    bits = (index & 1, ((index >> 1) ^ (index >> 2)) & 1, (index >> 2) & 1)
-    for axis, flip, bit in halving:
-        half = values.shape[0] // 2
-        mine = lax.dynamic_slice_in_dim(values, bits[bit] * half, half, 0)
-        other = lax.dynamic_slice_in_dim(values, (1 - bits[bit]) * half, half, 0)
-        values = add(mine, partner(other, axis, flip))
-    for axis, flip in doubling:
-        values = add(values, partner(values, axis, flip))
-    for axis, flip, bit in halving[::-1]:
-        got = partner(values, axis, flip)
-        low = bits[bit] == 0
-        values = jnp.concatenate([jnp.where(low, values, got), jnp.where(low, got, values)], 0)
-    return values
+    core, chip = index & 1, index >> 1
+    half = values.shape[0] // 2
+    mine = lax.dynamic_slice_in_dim(values, core * half, half, 0)
+    other = lax.dynamic_slice_in_dim(values, (1 - core) * half, half, 0)
+    values = (mine.astype(f32) + inner(other).astype(f32)).astype(bf16)
+    quarter = half // 4
+    parts = [
+        lax.dynamic_slice_in_dim(values, (chip ^ flip) * quarter, quarter, 0) for flip in (0,) + flips
+    ]
+    values = total(
+        [parts[0]] + [partner(part, "lat", 2 * flip) for part, flip in zip(parts[1:], flips)]
+    )
+    for scale in (1, 4):
+        values = total([values] + [partner(values, "lon", scale * flip) for flip in flips])
+    one, three, two = [partner(values, "lat", 2 * flip) for flip in flips]
+    low, high = (chip & 1) == 0, chip < 2
+    first = jnp.where(low, values, one), jnp.where(low, one, values)
+    second = jnp.where(low, two, three), jnp.where(low, three, two)
+    values = jnp.concatenate(
+        [jnp.where(high, a, b) for a, b in zip(first + second, second + first)], 0
+    )
+    got = inner(values)
+    return jnp.where(core == 0, values, got), jnp.where(core == 0, got, values)
 
 
 def local(
@@ -401,7 +458,8 @@
     depth = 256
     grid_rows = jnp.pad(grid_in, ((0, 0), (0, depth - variables)))
     select = (grid_export[:, None] == jnp.arange(grid_count)[None, :]).astype(bf16)
-    grid_near = around(dot(select, grid_rows).astype(bf16))
+    grid_picked = jnp.pad(dot(select, grid_in).astype(bf16), ((0, 0), (0, depth - variables)))
+    grid_near = around(grid_picked)
     grid_weight = jnp.pad(grid_weight, ((0, depth - variables), (0, 0)))
     export = mesh_export[None]
     encode_gain, node_gain = encode_gain[None], node_gain[None]
@@ -420,9 +478,9 @@
         encode_kernel,
         (
             encode_live,
-            encode_slots,
+            start_rows(encode_slots, grid_count),
             grid_rows,
-            grid_near,
+            *grid_near,
             mesh_init,
             encode_senders,
             encode_receivers,
@@ -447,20 +505,21 @@
             ((nodes, lanes), f32),
         ],
         [
-            ((grid_count + 9 * lanes + grid_count - lanes, depth), bf16),
+            ((grid_count + 8 * lanes + grid_count - lanes, depth), bf16),
             ((256, width), bf16),
             ((nodes, width), f32),
         ],
-        scalars=2,
+        2,
+        16,
     )
     near = around(picked)
-    mesh_out, own_grad, leaving, sender_rows, mix_grad, receiver_grad = call(
+    mesh_out, own_grad, to_lon, to_inner, to_outer, sender_rows, mix_grad, receiver_grad = call(
         process_kernel,
         (
             process_live,
-            process_slots,
+            start_rows(process_slots, 256),
             state,
-            near,
+            *near,
             process_senders,
             process_receivers,
             edge_sender,
@@ -473,32 +532,37 @@
         [
             ((nodes, width), bf16),
             ((nodes, width), f32),
-            ((9 * copies, width), bf16),
+            ((2 * copies, width), bf16),
+            ((3 * copies, width), bf16),
+            ((3 * copies, width), bf16),
             ((edges, width), bf16),
             ((edges, width), bf16),
             ((nodes, width), bf16),
         ],
         [
-            ((256 + 9 * copies + 128, width), bf16),
+            ((256 + 8 * copies + 128, width), bf16),
             ((256, width), bf16),
             ((nodes, width), f32),
             ((edges, width), f32),
             ((edges, width), f32),
             ((edges, lanes), f32),
             ((256, width), bf16),
-            ((256 + 9 * copies + 128, width), f32),
+            ((256 + 8 * copies + 128, width), f32),
             ((nodes, width), f32),
         ],
-        scalars=2,
-    )
-    leaving = leaving.reshape(3, 3 * copies, width)
-    from_above = shifted(leaving[0], "lat", -1)
-    from_below = shifted(leaving[2], "lat", 1)
-    columns = (
-        leaving[1].astype(f32) + from_above.astype(f32) + from_below.astype(f32)
-    ).astype(bf16).reshape(3, copies, width)
-    from_right = shifted(columns[0], "lon", -1)
-    from_left = shifted(columns[2], "lon", 1)
+        2,
+        24,
+    )
+    from_inner, from_outer = inner(to_inner), outer(to_outer)
+    to_left, to_right = [
+        (
+            to_lon[side * copies : (side + 1) * copies].astype(f32)
+            + from_inner[(side + 1) * copies : (side + 2) * copies].astype(f32)
+            + from_outer[(side + 1) * copies : (side + 2) * copies].astype(f32)
+        ).astype(bf16)
+        for side in (0, 1)
+    ]
+    from_right, from_left = shifted(to_left, -1), shifted(to_right, 1)
     state_part = cotangent.astype(f32) + back_dot(receiver_grad, edge_receiver)
     edge_grad = cross_dot(sender_rows, mix_grad).astype(bf16)
     mix_grad, pre_grad = call(
@@ -509,7 +573,8 @@
             export,
             state_part,
             own_grad,
-            columns[1],
+            from_inner,
+            from_outer,
             from_left,
             from_right,
             edge_sender,
@@ -526,10 +591,13 @@
         ),
         [((edges, width), bf16), ((edges, width), bf16)],
         [((256, width), bf16)],
+        1,
+        12,
     )
     sender_grad = cross_dot(hidden, mix_grad).astype(bf16)
     grid_grad = cross_dot(inputs, pre_grad).astype(bf16)
-    totals = summed(jnp.concatenate([sender_grad, edge_grad, grid_grad], 0)).astype(f32)
+    halves = summed(jnp.concatenate([sender_grad, edge_grad, grid_grad], 0))
+    totals = jnp.concatenate(halves, 0).astype(f32)
     return (
         mesh_out,
         totals[2 * width : 2 * width + variables],

time: 160 us -> 146 us (0.912)
  waiting for transfers between devices: 76.7 us -> 46.9 us
  starting transfers between devices: 43.8 us -> 57.5 us
    ppermute x12 -> x11, waiting for transfers between devices: 30.8 us -> 11 us  [the longest x5 6.83 us: outer(): lax.ppermute(x, 'lat', [(i, i + 1) for i in ends] + [(i + 1, i) for i in...]
    ppermute x10 -> x19, waiting for transfers between devices: 45.9 us -> 35.9 us  [partner(): lax.ppermute(x, axis, [(i, i ^ flip) for i in range(lax.axis_size(axis))])]
    ppermute x10 -> x19, starting transfers between devices: 14.9 us -> 22.4 us  [partner(): lax.ppermute(x, axis, [(i, i ^ flip) for i in range(lax.axis_size(axis))])]
    ppermute x12 -> x11, starting transfers between devices: 28.9 us -> 35.1 us  [the longest x5 18.1 us: outer(): lax.ppermute(x, 'lat', [(i, i + 1) for i in ends] + [(i + 1, i) for i in...]
    convert_element_type x9 -> x6, other arithmetic: 3.61 us -> 2.13 us  [the longest x1 1.6 us: local(): totals = jnp.concatenate(halves, 0).astype(f32)]
    unnamed x81 -> x79, local copies, waits for them, and re-layouts: 7.95 us -> 8.91 us
  transfers between devices with their start and end apart: 22 -> 30, of which waited for: 21 -> 17; matrix products, arithmetic and copies ran while one was open for 2% -> 4% of each run, Pallas kernels for 0% -> 0%
where the time goes in v1:
time: 146 us
  starting transfers between devices  57.5 us (39%)
  waiting for transfers between devices  46.9 us (32%)
  Pallas kernels  18.1 us (12%)
  local copies, waits for them, and re-layouts  10.1 us (7%)
  matrix products  5.32 us (4%)
  other arithmetic  4.95 us (3%)
  between operations  2.79 us (2%)
    ppermute x19, waiting for transfers between devices, partner(): lax.ppermute(x, axis, [(i, i ^ flip) for i in range(lax.axis_size(axis))])  35.9 us
    ppermute x19, starting transfers between devices, partner(): lax.ppermute(x, axis, [(i, i ^ flip) for i in range(lax.axis_size(axis))])  22.4 us
    pallas_call x3, Pallas kernels, call(): pl.pallas_call(kernel, out_shape=[jax.ShapeDtypeStruct(shape, dtype) for...  18.1 us
    ppermute x5, starting transfers between devices, outer(): lax.ppermute(x, 'lat', [(i, i + 1) for i in ends] + [(i + 1, i) for i in...  18.1 us
    ppermute x6, starting transfers between devices, shifted(): return lax.ppermute(x, 'lon', [(i, (i + step) % size) for i in range(size)])  17 us
    unnamed x79, local copies, waits for them, and re-layouts  8.91 us
    ppermute x5, waiting for transfers between devices, outer(): lax.ppermute(x, 'lat', [(i, i + 1) for i in ends] + [(i + 1, i) for i in...  6.83 us
    ppermute x6, waiting for transfers between devices, shifted(): return lax.ppermute(x, 'lon', [(i, (i + step) % size) for i in range(size)])  4.17 us
  transfers between devices with their start and end apart: 30, of which 17 were waited for; matrix products, arithmetic and copies ran while one was open for 4% of the time, Pallas kernels for 0%

profile of v1, /device:TPU:1, one launch (start us, length us, event | category | flops | bytes accessed | tf_op | source)
XLA Modules:
  0.0 145.8 jit_solution(2485671302550994611)
XLA Ops:
  2.3 2.5 %collective-permute-start = (bf16[128,256]{1,0:T(8,128)(2,1)S(1)}, bf16[128,256]{1,0:T(8,128)(2,1)S(1)}, u32[]{:S(2)}, u32[]{:S(2)}) collective-permute-start(bf16[128,256]{1,0:T(8,128)(2,1)S(1)} %pad.13), channel_id=1, source_target_pairs={{0,1},{1,2},{2,3},{3,4},{4,5},{5,6},{6,7},{7,8},{8,9},{9,10},{10,1... | collective-permute-start | bytes 196616 | tf_op jit(solution)/shard_map/ppermute | solution.py:358
  4.8 4.7 %collective-permute-start.1 = (bf16[128,256]{1,0:T(8,128)(2,1)S(1)}, bf16[128,256]{1,0:T(8,128)(2,1)S(1)}, u32[]{:S(2)}, u32[]{:S(2)}) collective-permute-start(bf16[128,256]{1,0:T(8,128)(2,1)S(1)} %pad.13), channel_id=1, source_target_pairs={{0,15},{1,0},{2,1},{3,2},{4,3},{5,4},{6,5},{7,6},{8,7},{9,8},{10,9... | collective-permute-start | bytes 196616 | tf_op jit(solution)/shard_map/ppermute | solution.py:358
  10.4 3.0 %collective-permute-start.4 = (bf16[128,256]{1,0:T(8,128)(2,1)S(1)}, bf16[128,256]{1,0:T(8,128)(2,1)S(1)}, u32[]{:S(2)}, u32[]{:S(2)}) collective-permute-start(bf16[128,256]{1,0:T(8,128)(2,1)S(1)} %pad.13), channel_id=1, source_target_pairs={{16,32},{48,64},{80,96},{32,16},{64,48},{96,80},{17,33},{49,65},{8... | collective-permute-start | bytes 196616 | tf_op jit(solution)/shard_map/ppermute | solution.py:371
  15.1 3.5 %collective-permute-start.5 = (bf16[256,256]{1,0:T(8,128)(2,1)S(1)}, bf16[256,256]{1,0:T(8,128)(2,1)S(1)}, u32[]{:S(2)}, u32[]{:S(2)}) collective-permute-start(bf16[256,256]{1,0:T(8,128)(2,1)S(1)} %constant_dynamic-update-slice_fusion), channel_id=1, source_target_pairs={{16,32},{48,64},{80,96},{32,16},{64,48},{96,80},{17,33},{49,65},{8... | collective-permute-start | bytes 393224 | tf_op jit(solution)/shard_map/ppermute | solution.py:371
  21.6 5.8 %shard_map.291 = (bf16[160,512]{1,0:T(8,128)(2,1)S(1)}, bf16[128,512]{1,0:T(8,128)(2,1)S(1)}, bf16[1024,256]{1,0:T(8,128)(2,1)S(1)}, bf16[1024,512]{1,0:T(8,128)...) custom-call(s32[1]{0:T(128)S(6)} %copy.40.live_ref, ...), custom_call_target="tpu_custom_call" | custom-call | flops 4294967296 | bytes 8388608 | tf_op jit(solution)/shard_map/pallas_call | solution.py:345
  32.8 4.8 %collective-permute-start.7 = (bf16[128,512]{1,0:T(8,128)(2,1)S(1)}, bf16[128,512]{1,0:T(8,128)(2,1)S(1)}, u32[]{:S(2)}, u32[]{:S(2)}) collective-permute-start(bf16[128,512]{1,0:T(8,128)(2,1)S(1)} %get-tuple-element.25), channel_id=1, source_target_pairs={{0,15},{1,0},{2,1},{3,2},{4,3},{5,4},{6,5},{7,6},{8,7},{9,8},{10,9... | collective-permute-start | bytes 393224 | tf_op jit(solution)/shard_map/ppermute | solution.py:358
  39.9 5.2 %collective-permute-start.11 = (bf16[256,512]{1,0:T(8,128)(2,1)S(1)}, bf16[256,512]{1,0:T(8,128)(2,1)S(1)}, u32[]{:S(2)}, u32[]{:S(2)}) collective-permute-start(bf16[256,512]{1,0:T(8,128)(2,1)S(1)} %constant_dynamic-update-slice_fusion.2), channel_id=1, source_target_pairs={{16,32},{48,64},{80,96},{32,16},{64,48},{96,80},{17,33},{49,65},{8... | collective-permute-start | bytes 786440 | tf_op jit(solution)/shard_map/ppermute | solution.py:371
  45.8 3.2 %collective-permute-start.10 = (bf16[128,512]{1,0:T(8,128)(2,1)S(1)}, bf16[128,512]{1,0:T(8,128)(2,1)S(1)}, u32[]{:S(2)}, u32[]{:S(2)}) collective-permute-start(bf16[128,512]{1,0:T(8,128)(2,1)S(1)} %get-tuple-element.25), channel_id=1, source_target_pairs={{16,32},{48,64},{80,96},{32,16},{64,48},{96,80},{17,33},{49,65},{8... | collective-permute-start | bytes 393224 | tf_op jit(solution)/shard_map/ppermute | solution.py:371
  49.2 3.0 %collective-permute-done.10.near_outer = bf16[128,512]{1,0:T(8,128)(2,1)S(1)} collective-permute-done((bf16[128,512]{1,0:T(8,128)(2,1)S(1)}, bf16[128,512]{1,0:T(8,128)(2,1)S(1)}, u32[]{:S(2)}, u32[]{:S(2)}) %collective-permute-start.10) | collective-permute-done | bytes 131104 | tf_op jit(solution)/shard_map/ppermute | solution.py:371
  52.2 9.0 %shard_map.292 = (bf16[160,512]{1,0:T(8,128)(2,1)}, f32[160,512]{1,0:T(8,128)S(1)}, bf16[256,512]{1,0:T(8,128)(2,1)S(1)}, bf16[384,512]{1,0:T(8,128)(2,1)}, bf16...) custom-call(s32[1]{0:T(128)S(6)} %copy.41.live_ref, ...), custom_call_target="tpu_custom_call" | custom-call | flops 4294967296 | bytes 8388608 | tf_op jit(solution)/shard_map/pallas_call | solution.py:345
  63.3 3.2 %collective-permute-start.13 = (bf16[384,512]{1,0:T(8,128)(2,1)}, bf16[384,512]{1,0:T(8,128)(2,1)S(1)}, u32[]{:S(2)}, u32[]{:S(2)}) collective-permute-start(bf16[384,512]{1,0:T(8,128)(2,1)} %get-tuple-element.31), channel_id=1, source_target_pairs={{16,32},{48,64},{80,96},{32,16},{64,48},{96,80},{17,33},{49,65},{8... | collective-permute-start | bytes 1179656 | tf_op jit(solution)/shard_map/ppermute | solution.py:371
  69.1 3.9 %collective-permute-done.13.from_outer = bf16[384,512]{1,0:T(8,128)(2,1)S(1)} collective-permute-done((bf16[384,512]{1,0:T(8,128)(2,1)}, bf16[384,512]{1,0:T(8,128)(2,1)S(1)}, u32[]{:S(2)}, u32[]{:S(2)}) %collective-permute-start.13) | collective-permute-done | bytes 393248 | tf_op jit(solution)/shard_map/ppermute | solution.py:371
  73.1 5.0 %collective-permute-start.15 = (bf16[128,512]{1,0:T(8,128)(2,1)S(1)}, bf16[128,512]{1,0:T(8,128)(2,1)S(1)}, u32[]{:S(2)}, u32[]{:S(2)}) collective-permute-start(bf16[128,512]{1,0:T(8,128)(2,1)S(1)} %get-tuple-element.50), channel_id=1, source_target_pairs={{0,15},{1,0},{2,1},{3,2},{4,3},{5,4},{6,5},{7,6},{8,7},{9,8},{10,9... | collective-permute-start | bytes 393224 | tf_op jit(solution)/shard_map/ppermute | solution.py:358
  80.3 3.3 %shard_map.293 = (bf16[1024,512]{1,0:T(8,128)(2,1)S(1)}, bf16[1024,512]{1,0:T(8,128)(2,1)S(1)}) custom-call(s32[1]{0:T(128)S(6)} %copy.40.live_ref, s32[8,128]{1,0:T(8,128)S(1)} %copy-done.14, s32[1,128]{1,0:T(1,128)S(1)} %bitcast.16, f32[160,512]{1,0:T(8,128)S(1)} %convolution_add_fusion.state_part, f32[160,512]{1,0:T(8,128)S(1)} %copy-done.35, ...), custom_call_target="tpu_custom_call" | custom-call | flops 4294967296 | bytes 8388608 | tf_op jit(solution)/shard_map/pallas_call | solution.py:345
  94.5 4.2 %collective-permute-done.18 = bf16[160,512]{1,0:T(8,128)(2,1)S(1)} collective-permute-done((bf16[160,512]{1,0:T(8,128)(2,1)S(1)}, bf16[160,512]{1,0:T(8,128)(2,1)S(1)}, u32[]{:S(2)}, u32[]{:S(2)}) %collective-permute-start.18) | collective-permute-done | bytes 163872 | tf_op jit(solution)/shard_map/ppermute | solution.py:362
  101.6 3.6 %collective-permute-start.22 = (bf16[160,512]{1,0:T(8,128)(2,1)S(1)}, bf16[160,512]{1,0:T(8,128)(2,1)S(1)}, u32[]{:S(2)}, u32[]{:S(2)}) collective-permute-start(bf16[160,512]{1,0:T(8,128)(2,1)S(1)} %add_convert_fusion.3), channel_id=1, source_target_pairs={{0,3},{1,2},{2,1},{3,0},{4,7},{5,6},{6,5},{7,4},{8,11},{9,10},{10,... | collective-permute-start | bytes 491528 | tf_op jit(solution)/shard_map/ppermute | solution.py:362
  105.9 3.1 %collective-permute-done.21 = bf16[160,512]{1,0:T(8,128)(2,1)S(1)} collective-permute-done((bf16[160,512]{1,0:T(8,128)(2,1)S(1)}, bf16[160,512]{1,0:T(8,128)(2,1)S(1)}, u32[]{:S(2)}, u32[]{:S(2)}) %collective-permute-start.21) | collective-permute-done | bytes 163872 | tf_op jit(solution)/shard_map/ppermute | solution.py:362
  109.0 3.6 %collective-permute-done.22 = bf16[160,512]{1,0:T(8,128)(2,1)S(1)} collective-permute-done((bf16[160,512]{1,0:T(8,128)(2,1)S(1)}, bf16[160,512]{1,0:T(8,128)(2,1)S(1)}, u32[]{:S(2)}, u32[]{:S(2)}) %collective-permute-start.22) | collective-permute-done | bytes 163872 | tf_op jit(solution)/shard_map/ppermute | solution.py:362
  112.8 5.8 %collective-permute-start.24 = (bf16[160,512]{1,0:T(8,128)(2,1)S(1)}, bf16[160,512]{1,0:T(8,128)(2,1)S(1)}, u32[]{:S(2)}, u32[]{:S(2)}) collective-permute-start(bf16[160,512]{1,0:T(8,128)(2,1)S(1)} %add_convert_fusion.2), channel_id=1, source_target_pairs={{0,8},{1,9},{2,10},{3,11},{4,12},{5,13},{6,14},{7,15},{8,0},{9,1},... | collective-permute-start | bytes 491528 | tf_op jit(solution)/shard_map/ppermute | solution.py:362
  118.6 5.9 %collective-permute-done.24 = bf16[160,512]{1,0:T(8,128)(2,1)S(1)} collective-permute-done((bf16[160,512]{1,0:T(8,128)(2,1)S(1)}, bf16[160,512]{1,0:T(8,128)(2,1)S(1)}, u32[]{:S(2)}, u32[]{:S(2)}) %collective-permute-start.24) | collective-permute-done | bytes 163872 | tf_op jit(solution)/shard_map/ppermute | solution.py:362
  124.5 3.0 %collective-permute-done.25 = bf16[160,512]{1,0:T(8,128)(2,1)S(1)} collective-permute-done((bf16[160,512]{1,0:T(8,128)(2,1)S(1)}, bf16[160,512]{1,0:T(8,128)(2,1)S(1)}, u32[]{:S(2)}, u32[]{:S(2)}) %collective-permute-start.25) | collective-permute-done | bytes 163872 | tf_op jit(solution)/shard_map/ppermute | solution.py:362
  127.7 2.9 %collective-permute-start.27 = (bf16[160,512]{1,0:T(8,128)(2,1)S(1)}, bf16[160,512]{1,0:T(8,128)(2,1)S(1)}, u32[]{:S(2)}, u32[]{:S(2)}) collective-permute-start(bf16[160,512]{1,0:T(8,128)(2,1)S(1)} %add_convert_fusion.1), channel_id=1, source_target_pairs={{0,64},{16,80},{32,96},{48,112},{64,0},{80,16},{96,32},{112,48},{1... | collective-permute-start | bytes 491528 | tf_op jit(solution)/shard_map/ppermute | solution.py:362
  131.8 4.4 %collective-permute-done.27 = bf16[160,512]{1,0:T(8,128)(2,1)S(1)} collective-permute-done((bf16[160,512]{1,0:T(8,128)(2,1)S(1)}, bf16[160,512]{1,0:T(8,128)(2,1)S(1)}, u32[]{:S(2)}, u32[]{:S(2)}) %collective-permute-start.27) | collective-permute-done | bytes 163872 | tf_op jit(solution)/shard_map/ppermute | solution.py:362
  136.2 2.7 %collective-permute-done.28 = bf16[160,512]{1,0:T(8,128)(2,1)S(1)} collective-permute-done((bf16[160,512]{1,0:T(8,128)(2,1)S(1)}, bf16[160,512]{1,0:T(8,128)(2,1)S(1)}, u32[]{:S(2)}, u32[]{:S(2)}) %collective-permute-start.28) | collective-permute-done | bytes 163872 | tf_op jit(solution)/shard_map/ppermute | solution.py:362
  (146 shorter events, 43.9 us)
Async XLA Ops:
  2.3 12.7 %collective-permute-start = (bf16[128,256]{1,0:T(8,128)(2,1)S(1)}, bf16[128,256]{1,0:T(8,128)(2,1)S(1)}, u32[]{:S(2)}, u32[]{:S(2)}) collective-permute-start(bf16[128,256]{1,0:T(8,128)(2,1)S(1)} %pad.13), channel_id=1, source_target_pairs={{0,1},{1,2},{2,3},{3,4},{4,5},{5,6},{6,7},{7,8},{8,9},{9,10},{10,1... | collective-permute-start | bytes 196616 | tf_op jit(solution)/shard_map/ppermute | solution.py:358
  4.8 10.2 %collective-permute-start.1 = (bf16[128,256]{1,0:T(8,128)(2,1)S(1)}, bf16[128,256]{1,0:T(8,128)(2,1)S(1)}, u32[]{:S(2)}, u32[]{:S(2)}) collective-permute-start(bf16[128,256]{1,0:T(8,128)(2,1)S(1)} %pad.13), channel_id=1, source_target_pairs={{0,15},{1,0},{2,1},{3,2},{4,3},{5,4},{6,5},{7,6},{8,7},{9,8},{10,9... | collective-permute-start | bytes 196616 | tf_op jit(solution)/shard_map/ppermute | solution.py:358
  9.5 11.9 %collective-permute-start.2 = (bf16[128,256]{1,0:T(8,128)(2,1)S(1)}, bf16[128,256]{1,0:T(8,128)(2,1)S(1)}, u32[]{:S(2)}, u32[]{:S(2)}) collective-permute-start(bf16[128,256]{1,0:T(8,128)(2,1)S(1)} %pad.13), channel_id=1, source_target_pairs={{0,16},{16,0},{32,48},{48,32},{64,80},{80,64},{96,112},{112,96},{1... | collective-permute-start | bytes 196616 | tf_op jit(solution)/shard_map/ppermute | solution.py:362
  10.4 11.0 %collective-permute-start.4 = (bf16[128,256]{1,0:T(8,128)(2,1)S(1)}, bf16[128,256]{1,0:T(8,128)(2,1)S(1)}, u32[]{:S(2)}, u32[]{:S(2)}) collective-permute-start(bf16[128,256]{1,0:T(8,128)(2,1)S(1)} %pad.13), channel_id=1, source_target_pairs={{16,32},{48,64},{80,96},{32,16},{64,48},{96,80},{17,33},{49,65},{8... | collective-permute-start | bytes 196616 | tf_op jit(solution)/shard_map/ppermute | solution.py:371
  15.0 6.4 %collective-permute-start.3 = (bf16[256,256]{1,0:T(8,128)(2,1)S(1)}, bf16[256,256]{1,0:T(8,128)(2,1)S(1)}, u32[]{:S(2)}, u32[]{:S(2)}) collective-permute-start(bf16[256,256]{1,0:T(8,128)(2,1)S(1)} %constant_dynamic-update-slice_fusion), channel_id=1, source_target_pairs={{0,16},{16,0},{32,48},{48,32},{64,80},{80,64},{96,112},{112,96},{1... | collective-permute-start | bytes 393224 | tf_op jit(solution)/shard_map/ppermute | solution.py:362
  15.1 6.3 %collective-permute-start.5 = (bf16[256,256]{1,0:T(8,128)(2,1)S(1)}, bf16[256,256]{1,0:T(8,128)(2,1)S(1)}, u32[]{:S(2)}, u32[]{:S(2)}) collective-permute-start(bf16[256,256]{1,0:T(8,128)(2,1)S(1)} %constant_dynamic-update-slice_fusion), channel_id=1, source_target_pairs={{16,32},{48,64},{80,96},{32,16},{64,48},{96,80},{17,33},{49,65},{8... | collective-permute-start | bytes 393224 | tf_op jit(solution)/shard_map/ppermute | solution.py:371
  32.8 7.1 %collective-permute-start.6 = (bf16[128,512]{1,0:T(8,128)(2,1)S(1)}, bf16[128,512]{1,0:T(8,128)(2,1)S(1)}, u32[]{:S(2)}, u32[]{:S(2)}) collective-permute-start(bf16[128,512]{1,0:T(8,128)(2,1)S(1)} %get-tuple-element.25), channel_id=1, source_target_pairs={{0,1},{1,2},{2,3},{3,4},{4,5},{5,6},{6,7},{7,8},{8,9},{9,10},{10,1... | collective-permute-start | bytes 393224 | tf_op jit(solution)/shard_map/ppermute | solution.py:358
  32.8 7.2 %collective-permute-start.7 = (bf16[128,512]{1,0:T(8,128)(2,1)S(1)}, bf16[128,512]{1,0:T(8,128)(2,1)S(1)}, u32[]{:S(2)}, u32[]{:S(2)}) collective-permute-start(bf16[128,512]{1,0:T(8,128)(2,1)S(1)} %get-tuple-element.25), channel_id=1, source_target_pairs={{0,15},{1,0},{2,1},{3,2},{4,3},{5,4},{6,5},{7,6},{8,7},{9,8},{10,9... | collective-permute-start | bytes 393224 | tf_op jit(solution)/shard_map/ppermute | solution.py:358
  39.9 12.2 %collective-permute-start.11 = (bf16[256,512]{1,0:T(8,128)(2,1)S(1)}, bf16[256,512]{1,0:T(8,128)(2,1)S(1)}, u32[]{:S(2)}, u32[]{:S(2)}) collective-permute-start(bf16[256,512]{1,0:T(8,128)(2,1)S(1)} %constant_dynamic-update-slice_fusion.2), channel_id=1, source_target_pairs={{16,32},{48,64},{80,96},{32,16},{64,48},{96,80},{17,33},{49,65},{8... | collective-permute-start | bytes 786440 | tf_op jit(solution)/shard_map/ppermute | solution.py:371
  45.1 7.0 %collective-permute-start.9 = (bf16[256,512]{1,0:T(8,128)(2,1)S(1)}, bf16[256,512]{1,0:T(8,128)(2,1)S(1)}, u32[]{:S(2)}, u32[]{:S(2)}) collective-permute-start(bf16[256,512]{1,0:T(8,128)(2,1)S(1)} %constant_dynamic-update-slice_fusion.2), channel_id=1, source_target_pairs={{0,16},{16,0},{32,48},{48,32},{64,80},{80,64},{96,112},{112,96},{1... | collective-permute-start | bytes 786440 | tf_op jit(solution)/shard_map/ppermute | solution.py:362
  45.8 6.3 %collective-permute-start.10 = (bf16[128,512]{1,0:T(8,128)(2,1)S(1)}, bf16[128,512]{1,0:T(8,128)(2,1)S(1)}, u32[]{:S(2)}, u32[]{:S(2)}) collective-permute-start(bf16[128,512]{1,0:T(8,128)(2,1)S(1)} %get-tuple-element.25), channel_id=1, source_target_pairs={{16,32},{48,64},{80,96},{32,16},{64,48},{96,80},{17,33},{49,65},{8... | collective-permute-start | bytes 393224 | tf_op jit(solution)/shard_map/ppermute | solution.py:371
  62.0 7.1 %collective-permute-start.12 = (bf16[384,512]{1,0:T(8,128)(2,1)}, bf16[384,512]{1,0:T(8,128)(2,1)S(1)}, u32[]{:S(2)}, u32[]{:S(2)}) collective-permute-start(bf16[384,512]{1,0:T(8,128)(2,1)} %get-tuple-element.30), channel_id=1, source_target_pairs={{0,16},{16,0},{32,48},{48,32},{64,80},{80,64},{96,112},{112,96},{1... | collective-permute-start | bytes 1179656 | tf_op jit(solution)/shard_map/ppermute | solution.py:362
  63.3 9.6 %collective-permute-start.13 = (bf16[384,512]{1,0:T(8,128)(2,1)}, bf16[384,512]{1,0:T(8,128)(2,1)S(1)}, u32[]{:S(2)}, u32[]{:S(2)}) collective-permute-start(bf16[384,512]{1,0:T(8,128)(2,1)} %get-tuple-element.31), channel_id=1, source_target_pairs={{16,32},{48,64},{80,96},{32,16},{64,48},{96,80},{17,33},{49,65},{8... | collective-permute-start | bytes 1179656 | tf_op jit(solution)/shard_map/ppermute | solution.py:371
  73.0 7.2 %collective-permute-start.14 = (bf16[128,512]{1,0:T(8,128)(2,1)S(1)}, bf16[128,512]{1,0:T(8,128)(2,1)S(1)}, u32[]{:S(2)}, u32[]{:S(2)}) collective-permute-start(bf16[128,512]{1,0:T(8,128)(2,1)S(1)} %get-tuple-element.51), channel_id=1, source_target_pairs={{0,1},{1,2},{2,3},{3,4},{4,5},{5,6},{6,7},{7,8},{8,9},{9,10},{10,1... | collective-permute-start | bytes 393224 | tf_op jit(solution)/shard_map/ppermute | solution.py:358
  73.1 7.1 %collective-permute-start.15 = (bf16[128,512]{1,0:T(8,128)(2,1)S(1)}, bf16[128,512]{1,0:T(8,128)(2,1)S(1)}, u32[]{:S(2)}, u32[]{:S(2)}) collective-permute-start(bf16[128,512]{1,0:T(8,128)(2,1)S(1)} %get-tuple-element.50), channel_id=1, source_target_pairs={{0,15},{1,0},{2,1},{3,2},{4,3},{5,4},{6,5},{7,6},{8,7},{9,8},{10,9... | collective-permute-start | bytes 393224 | tf_op jit(solution)/shard_map/ppermute | solution.py:358
  87.7 6.8 %collective-permute-start.17 = (bf16[160,512]{1,0:T(8,128)(2,1)S(1)}, bf16[160,512]{1,0:T(8,128)(2,1)S(1)}, u32[]{:S(2)}, u32[]{:S(2)}) collective-permute-start(bf16[160,512]{1,0:T(8,128)(2,1)S(1)} %get-tuple-element.56), channel_id=1, source_target_pairs={{0,32},{16,48},{32,0},{48,16},{64,96},{80,112},{96,64},{112,80},{1... | collective-permute-start | bytes 491528 | tf_op jit(solution)/shard_map/ppermute | solution.py:362
  90.2 8.4 %collective-permute-start.18 = (bf16[160,512]{1,0:T(8,128)(2,1)S(1)}, bf16[160,512]{1,0:T(8,128)(2,1)S(1)}, u32[]{:S(2)}, u32[]{:S(2)}) collective-permute-start(bf16[160,512]{1,0:T(8,128)(2,1)S(1)} %get-tuple-element.58), channel_id=1, source_target_pairs={{0,64},{16,80},{32,96},{48,112},{64,0},{80,16},{96,32},{112,48},{1... | collective-permute-start | bytes 491528 | tf_op jit(solution)/shard_map/ppermute | solution.py:362
  90.9 10.2 %collective-permute-start.19 = (bf16[160,512]{1,0:T(8,128)(2,1)S(1)}, bf16[160,512]{1,0:T(8,128)(2,1)S(1)}, u32[]{:S(2)}, u32[]{:S(2)}) collective-permute-start(bf16[160,512]{1,0:T(8,128)(2,1)S(1)} %get-tuple-element.57), channel_id=1, source_target_pairs={{0,96},{16,112},{32,64},{48,80},{64,32},{80,48},{96,0},{112,16},{1... | collective-permute-start | bytes 491528 | tf_op jit(solution)/shard_map/ppermute | solution.py:362
  101.3 7.7 %collective-permute-start.21 = (bf16[160,512]{1,0:T(8,128)(2,1)S(1)}, bf16[160,512]{1,0:T(8,128)(2,1)S(1)}, u32[]{:S(2)}, u32[]{:S(2)}) collective-permute-start(bf16[160,512]{1,0:T(8,128)(2,1)S(1)} %add_convert_fusion.3), channel_id=1, source_target_pairs={{0,2},{1,3},{2,0},{3,1},{4,6},{5,7},{6,4},{7,5},{8,10},{9,11},{10,... | collective-permute-start | bytes 491528 | tf_op jit(solution)/shard_map/ppermute | solution.py:362
  101.6 11.0 %collective-permute-start.22 = (bf16[160,512]{1,0:T(8,128)(2,1)S(1)}, bf16[160,512]{1,0:T(8,128)(2,1)S(1)}, u32[]{:S(2)}, u32[]{:S(2)}) collective-permute-start(bf16[160,512]{1,0:T(8,128)(2,1)S(1)} %add_convert_fusion.3), channel_id=1, source_target_pairs={{0,3},{1,2},{2,1},{3,0},{4,7},{5,6},{6,5},{7,4},{8,11},{9,10},{10,... | collective-permute-start | bytes 491528 | tf_op jit(solution)/shard_map/ppermute | solution.py:362
  112.8 11.7 %collective-permute-start.24 = (bf16[160,512]{1,0:T(8,128)(2,1)S(1)}, bf16[160,512]{1,0:T(8,128)(2,1)S(1)}, u32[]{:S(2)}, u32[]{:S(2)}) collective-permute-start(bf16[160,512]{1,0:T(8,128)(2,1)S(1)} %add_convert_fusion.2), channel_id=1, source_target_pairs={{0,8},{1,9},{2,10},{3,11},{4,12},{5,13},{6,14},{7,15},{8,0},{9,1},... | collective-permute-start | bytes 491528 | tf_op jit(solution)/shard_map/ppermute | solution.py:362
  118.6 8.9 %collective-permute-start.25 = (bf16[160,512]{1,0:T(8,128)(2,1)S(1)}, bf16[160,512]{1,0:T(8,128)(2,1)S(1)}, u32[]{:S(2)}, u32[]{:S(2)}) collective-permute-start(bf16[160,512]{1,0:T(8,128)(2,1)S(1)} %add_convert_fusion.2), channel_id=1, source_target_pairs={{0,12},{1,13},{2,14},{3,15},{4,8},{5,9},{6,10},{7,11},{8,4},{9,5},... | collective-permute-start | bytes 491528 | tf_op jit(solution)/shard_map/ppermute | solution.py:362
  127.7 8.5 %collective-permute-start.27 = (bf16[160,512]{1,0:T(8,128)(2,1)S(1)}, bf16[160,512]{1,0:T(8,128)(2,1)S(1)}, u32[]{:S(2)}, u32[]{:S(2)}) collective-permute-start(bf16[160,512]{1,0:T(8,128)(2,1)S(1)} %add_convert_fusion.1), channel_id=1, source_target_pairs={{0,64},{16,80},{32,96},{48,112},{64,0},{80,16},{96,32},{112,48},{1... | collective-permute-start | bytes 491528 | tf_op jit(solution)/shard_map/ppermute | solution.py:362
  130.6 8.3 %collective-permute-start.28 = (bf16[160,512]{1,0:T(8,128)(2,1)S(1)}, bf16[160,512]{1,0:T(8,128)(2,1)S(1)}, u32[]{:S(2)}, u32[]{:S(2)}) collective-permute-start(bf16[160,512]{1,0:T(8,128)(2,1)S(1)} %add_convert_fusion.1), channel_id=1, source_target_pairs={{0,96},{16,112},{32,64},{48,80},{64,32},{80,48},{96,0},{112,16},{1... | collective-permute-start | bytes 491528 | tf_op jit(solution)/shard_map/ppermute | solution.py:362
  (44 other events, 616.8 us)

commit v2 on v1

--- a/solution.py
+++ b/solution.py
@@ -62,8 +62,14 @@
     return jnp.where(block < live, rows[pl.ds(block, 1), :], -1)
 
 
-def window(starts, block):
-    return pl.multiple_of(starts[block], lanes)
+def window(slots, block, own_rows, core):
+    slot = slots[block]
+    band = jnp.where(slot >= 6, 2, jnp.where(slot >= 3, 1, 0))
+    sector = slot - 3 * band
+    side = jnp.where(sector == 1, 0, jnp.where(sector == 0, 1, 2))
+    inside = (band == 2) == (core == 0)
+    place = jnp.where(band == 1, jnp.where(sector == 0, 0, 1), jnp.where(inside, 2, 5) + side)
+    return pl.multiple_of(jnp.where(slot == 4, 0, own_rows + lanes * place), lanes)
 
 
 def fill(table, own, near):
@@ -77,9 +83,18 @@
     table[first:, :] = jnp.zeros_like(table[first:, :])
 
 
+def send(source, target, sem):
+    pltpu.make_async_copy(source, target, sem).start()
+
+
+def finish(source, target, sem):
+    pltpu.make_async_copy(source, target, sem).wait()
+
+
 def encode_kernel(
     live_ref,
-    starts,
+    place_ref,
+    slots,
     grid_own,
     near_left,
     near_right,
@@ -99,21 +114,31 @@
     gain,
     state,
     picked,
+    inputs_out,
+    hidden_out,
+    pre_slope_out,
+    mix_slope_out,
+    normed_out,
+    scale_out,
+    update_normed_out,
+    update_scale_out,
+    table,
+    projected,
+    total,
     inputs,
     hidden,
     pre_slope,
     mix_slope,
-    normed_out,
-    scale_out,
+    normed_all,
+    scale_all,
     update_normed,
     update_scale,
-    table,
-    projected,
-    total,
+    sems,
+    last_sems,
 ):
     own = grid_own.shape[0]
     nodes = base.shape[0]
-    live = live_ref[0]
+    live, core = live_ref[0], place_ref[0]
     fill(
         table,
         grid_own,
@@ -123,12 +148,21 @@
     projected[nodes:, :] = jnp.zeros_like(projected[nodes:, :])
     total[...] = jnp.zeros_like(total)
     turn_rows = blocks_per_turn * lanes
+    turns = senders.shape[0] // blocks_per_turn
+    saved = (
+        (inputs, inputs_out),
+        (hidden, hidden_out),
+        (pre_slope, pre_slope_out),
+        (mix_slope, mix_slope_out),
+        (normed_all, normed_out),
+        (scale_all, scale_out),
+    )
 
     def turn(step, carry):
         gathered, received, placed = [], [], []
         for part in range(blocks_per_turn):
             block = step * blocks_per_turn + part
-            start = window(starts, block)
+            start = window(slots, block, own, core)
             pick = lane_hot(senders[pl.ds(block, 1), :], own)
             gathered.append(dot(pick, table[pl.ds(start, own), :]).astype(bf16))
             ends = live_row(receivers, block, live)
@@ -149,27 +183,38 @@
         product = dot((mix * gate).astype(bf16), message_weight[...])
         normed, scale = normalise(product)
         normed = normed.astype(bf16)
-        normed_out[here, :] = normed
-        scale_out[here, :] = jnp.broadcast_to(scale, (turn_rows, lanes))
+        normed_all[here, :] = normed
+        scale_all[here, :] = jnp.broadcast_to(scale, (turn_rows, lanes))
         total[...] += dot(jnp.concatenate(placed, 1), normed)
+        for index, (source, target) in enumerate(saved):
+            send(source.at[here, :], target.at[here, :], sems.at[index, step])
         return carry
 
-    lax.fori_loop(0, senders.shape[0] // blocks_per_turn, turn, 0)
+    lax.fori_loop(0, turns, turn, 0)
     update = dot(total[...].astype(bf16), update_weight[...])
     normed, scale = normalise(update)
     update_normed[...] = normed
     update_scale[...] = jnp.broadcast_to(scale, update_scale.shape)
+    send(update_normed, update_normed_out, last_sems.at[0])
+    send(update_scale, update_scale_out, last_sems.at[1])
     new_state = (base[...].astype(f32) + normed * gain[...]).astype(bf16)
     state[...] = new_state
     padded_state = jnp.concatenate(
         [new_state, jnp.zeros((256 - nodes, new_state.shape[1]), bf16)], 0
     )
     picked[...] = dot(lane_hot(export[...], 256), padded_state).astype(bf16)
+    for step in range(turns):
+        here = pl.ds(step * turn_rows, turn_rows)
+        for index, (source, target) in enumerate(saved):
+            finish(source.at[here, :], target.at[here, :], sems.at[index, step])
+    finish(update_normed, update_normed_out, last_sems.at[0])
+    finish(update_scale, update_scale_out, last_sems.at[1])
 
 
 def process_kernel(
     live_ref,
-    starts,
+    place_ref,
+    slots,
     state,
     near_left,
     near_right,
@@ -185,12 +230,12 @@
     node_update,
     gain,
     cotangent,
-    mesh_out,
+    mesh_hbm,
     own_grad,
     to_lon,
     to_inner,
     to_outer,
-    sender_rows,
+    sender_rows_out,
     mix_grad_out,
     receiver_grad,
     table,
@@ -202,10 +247,15 @@
     upstream,
     table_grad,
     receiver_total,
+    mesh_out,
+    sender_rows,
+    mix_grads,
+    sems,
+    last_sems,
 ):
     nodes = state.shape[0]
     reach = 256
-    live = live_ref[0]
+    live, core = live_ref[0], place_ref[0]
     fill(
         table,
         state,
@@ -221,7 +271,7 @@
         gathered, received, placed = [], [], []
         for part in range(blocks_per_turn):
             block = step * blocks_per_turn + part
-            start = window(starts, block)
+            start = window(slots, block, reach, core)
             pick = lane_hot(senders[pl.ds(block, 1), :], reach)
             gathered.append(dot(pick, table[pl.ds(start, reach), :]).astype(bf16))
             ends = live_row(receivers, block, live)
@@ -239,12 +289,14 @@
         normed_all[here, :] = normed
         scale_all[here, :] = jnp.broadcast_to(scale, (turn_rows, lanes))
         total[...] += dot(jnp.concatenate(placed, 1), normed.astype(bf16))
+        send(sender_rows.at[here, :], sender_rows_out.at[here, :], sems.at[0, step])
         return carry
 
     lax.fori_loop(0, turns, forward, 0)
     update = dot(total[...].astype(bf16), node_update[...])
     normed, scale = normalise(update)
     mesh_out[...] = (state[...].astype(f32) + normed * gain[...]).astype(bf16)
+    send(mesh_out, mesh_hbm, last_sems.at[0])
     update_grad = norm_back(normed, scale, cotangent[...].astype(f32) * gain[...])
     upstream[0:nodes, :] = back_dot(update_grad.astype(bf16), node_update[...]).astype(bf16)
     upstream[nodes:, :] = jnp.zeros_like(upstream[nodes:, :])
@@ -262,11 +314,12 @@
         product_grad = norm_back(normed_all[here, :], scale_all[here, 0:1], arriving)
         mix_grad = back_dot(product_grad.astype(bf16), edge_message[...]) * slope[here, :]
         mix_grad = mix_grad.astype(bf16)
-        mix_grad_out[here, :] = mix_grad
+        mix_grads[here, :] = mix_grad
+        send(mix_grads.at[here, :], mix_grad_out.at[here, :], sems.at[1, step])
         receiver_total[...] += dot(jnp.concatenate(placed, 1), mix_grad)
         for part in range(blocks_per_turn):
             block = step * blocks_per_turn + part
-            start = window(starts, block)
+            start = window(slots, block, reach, core)
             place = row_hot(senders[pl.ds(block, 1), :], nodes)
             table_grad[pl.ds(start, nodes), :] += dot(
                 place, mix_grad[part * lanes : (part + 1) * lanes, :]
@@ -274,16 +327,23 @@
         return carry
 
     lax.fori_loop(0, turns, backward, 0)
-    own_grad[...] = table_grad[0:nodes, :]
+    send(table_grad.at[0:nodes, :], own_grad, last_sems.at[1])
     first = reach
     for part in (to_lon, to_inner, to_outer):
         part[...] = table_grad[first : first + part.shape[0], :].astype(bf16)
         first += part.shape[0]
     receiver_grad[...] = receiver_total[...].astype(bf16)
+    for step in range(turns):
+        here = pl.ds(step * turn_rows, turn_rows)
+        finish(sender_rows.at[here, :], sender_rows_out.at[here, :], sems.at[0, step])
+        finish(mix_grads.at[here, :], mix_grad_out.at[here, :], sems.at[1, step])
+    finish(mesh_out, mesh_hbm, last_sems.at[0])
+    finish(table_grad.at[0:nodes, :], own_grad, last_sems.at[1])
 
 
 def encode_back_kernel(
     live_ref,
+    place_ref,
     receivers,
     export,
     state_part,
@@ -301,13 +361,17 @@
     scale_all,
     mix_slope,
     pre_slope,
+    inputs,
+    hidden,
     message_weight,
     sender_weight,
-    mix_grad_out,
-    pre_grad_out,
+    edge_grad,
+    given,
+    kept,
     upstream,
+    grads,
 ):
-    nodes = state_part.shape[0]
+    nodes, width = state_part.shape
     live = live_ref[0]
     arrived = from_left[...].astype(f32) + from_right[...].astype(f32)
     copies = arrived.shape[0]
@@ -318,6 +382,10 @@
     upstream[0:nodes, :] = back_dot(update_grad.astype(bf16), update_weight[...]).astype(bf16)
     upstream[nodes:, :] = jnp.zeros_like(upstream[nodes:, :])
     turn_rows = blocks_per_turn * lanes
+    variables = inputs.shape[1]
+    grads[0:width, :] = jnp.zeros_like(grads[0:width, :])
+    grads[width : 2 * width, :] = edge_grad[...].astype(f32)
+    grads[2 * width :, :] = jnp.zeros_like(grads[2 * width :, :])
 
     def turn(step, carry):
         received = [
@@ -331,23 +399,62 @@
         ).astype(bf16)
         mix_grad = back_dot(product_grad, message_weight[...]) * mix_slope[here, :].astype(f32)
         mix_grad = mix_grad.astype(bf16)
-        mix_grad_out[here, :] = mix_grad
+        grads[0:width, :] += cross_dot(hidden[here, :], mix_grad)
         pre_grad = back_dot(mix_grad, sender_weight[...]) * pre_slope[here, :].astype(f32)
-        pre_grad_out[here, :] = pre_grad.astype(bf16)
+        grads[2 * width : 2 * width + variables, :] += cross_dot(
+            inputs[here, :], pre_grad.astype(bf16)
+        )
         return carry
 
     lax.fori_loop(0, receivers.shape[0] // blocks_per_turn, turn, 0)
+    core, near, far = place_ref[0], place_ref[1], place_ref[2]
+    piece = grads.shape[0] // 16
+    for block in range(16):
+        half, first, second = block // 4 % 2, block // 2 % 2, block % 2
+        bits = (first ^ near, second ^ far) if half == 0 else (first ^ far, second ^ near)
+        side = core ^ (1 - block // 8)
+        origin = (((side * 2 + half) * 2 + bits[0]) * 2 + bits[1]) * piece
+        rows = grads[pl.ds(pl.multiple_of(origin, 16), piece), :].astype(bf16)
+        target = given if block < 8 else kept
+        target[block % 8 * piece : (block % 8 + 1) * piece, :] = rows
+
+
+def order_kernel(
+    place_ref, mine, other, sender_grad, edge_grad, grid_grad, grads, last, sems
+):
+    core, near, far = place_ref[0], place_ref[1], place_ref[2]
+    piece = grads.shape[0] // 16
+    for block in range(16):
+        half, first, second = block // 4 % 2, block // 2 % 2, block % 2
+        bits = (first ^ near, second ^ far) if half == 0 else (first ^ far, second ^ near)
+        side = core ^ (block // 8)
+        origin = (((side * 2 + half) * 2 + bits[0]) * 2 + bits[1]) * piece
+        source = mine if block < 8 else other
+        rows = source[block % 8 * piece : (block % 8 + 1) * piece, :].astype(f32)
+        grads[pl.ds(pl.multiple_of(origin, 16), piece), :] = rows
+    width = sender_grad.shape[0]
+    last[...] = grads[2 * width : 2 * width + last.shape[0], :]
+    copies = (
+        (grads.at[0:width, :], sender_grad, sems.at[0]),
+        (grads.at[width : 2 * width, :], edge_grad, sems.at[1]),
+        (last, grid_grad, sems.at[2]),
+    )
+    for copy in copies:
+        send(*copy)
+    for copy in copies:
+        finish(*copy)
 
 
 def call(kernel, operands, outs, scratch, scalars, mib):
     smem = pl.BlockSpec(memory_space=pltpu.SMEM)
     vmem = pl.BlockSpec(memory_space=pltpu.VMEM)
+    hbm = pl.BlockSpec(memory_space=pl.ANY)
     return pl.pallas_call(
         kernel,
-        out_shape=[jax.ShapeDtypeStruct(shape, dtype) for shape, dtype in outs],
+        out_shape=[jax.ShapeDtypeStruct(shape, dtype) for shape, dtype, _ in outs],
         in_specs=[smem] * scalars + [vmem] * (len(operands) - scalars),
-        out_specs=[vmem] * len(outs),
-        scratch_shapes=[pltpu.VMEM(shape, dtype) for shape, dtype in scratch],
+        out_specs=[hbm if kind else vmem for _, _, kind in outs],
+        scratch_shapes=[pltpu.VMEM(*shape) if isinstance(shape, tuple) else shape for shape in scratch],
         compiler_params=pltpu.CompilerParams(vmem_limit_bytes=mib << 20),
         cost_estimate=pl.CostEstimate(flops=4 << 30, bytes_accessed=8 << 20, transcendentals=0),
     )(*operands)
@@ -373,56 +480,36 @@
 
 def around(rows):
     left, right = shifted(rows, 1), shifted(rows, -1)
+    above, below = inner(rows), outer(rows)
+    left, right, above, below = lax.optimization_barrier((left, right, above, below))
     corners = jnp.concatenate([left, right], 0)
-    return left, right, inner(rows), inner(corners), outer(rows), outer(corners)
-
-
-even_places = (6, 5, 7, 0, -1, 1, 3, 2, 4)
-odd_places = (3, 2, 4, 0, -1, 1, 6, 5, 7)
-
-
-def start_rows(slots, own):
-    places = jnp.where(
-        lax.axis_index("lat") % 2 == 0, jnp.array(even_places), jnp.array(odd_places)
-    )
-    pick = slots[:, None] == jnp.arange(9)[None, :]
-    place = jnp.sum(jnp.where(pick, places[None, :], 0), 1).astype(jnp.int32)
-    return jnp.where(place < 0, 0, own + lanes * place)
-
-
-flips = (1, 3, 2)
-
-
-def total(values):
-    own, one, three, two = [part.astype(f32) for part in values]
-    return ((own + one) + (two + three)).astype(bf16)
-
-
-def summed(values):
-    index = lax.axis_index("lat")
-    core, chip = index & 1, index >> 1
+    return left, right, above, inner(corners), below, outer(corners)
+
+
+def add(left, right):
+    return (left.astype(f32) + right.astype(f32)).astype(bf16)
+
+
+def half_chain(values, flips):
+    one, two = flips
+    for flip in flips:
+        half = values.shape[0] // 2
+        values = add(values[:half], partner(values[half:], "lat", 2 * flip))
+    for scale in (1, 4):
+        for flip in flips:
+            values = add(values, partner(values, "lon", scale * flip))
+    for flip in flips[::-1]:
+        values = jnp.concatenate([values, partner(values, "lat", 2 * flip)], 0)
+    return values
+
+
+def summed(given, kept):
+    values = add(kept, inner(given))
     half = values.shape[0] // 2
-    mine = lax.dynamic_slice_in_dim(values, core * half, half, 0)
-    other = lax.dynamic_slice_in_dim(values, (1 - core) * half, half, 0)
-    values = (mine.astype(f32) + inner(other).astype(f32)).astype(bf16)
-    quarter = half // 4
-    parts = [
-        lax.dynamic_slice_in_dim(values, (chip ^ flip) * quarter, quarter, 0) for flip in (0,) + flips
-    ]
-    values = total(
-        [parts[0]] + [partner(part, "lat", 2 * flip) for part, flip in zip(parts[1:], flips)]
-    )
-    for scale in (1, 4):
-        values = total([values] + [partner(values, "lon", scale * flip) for flip in flips])
-    one, three, two = [partner(values, "lat", 2 * flip) for flip in flips]
-    low, high = (chip & 1) == 0, chip < 2
-    first = jnp.where(low, values, one), jnp.where(low, one, values)
-    second = jnp.where(low, two, three), jnp.where(low, three, two)
     values = jnp.concatenate(
-        [jnp.where(high, a, b) for a, b in zip(first + second, second + first)], 0
-    )
-    got = inner(values)
-    return jnp.where(core == 0, values, got), jnp.where(core == 0, got, values)
+        [half_chain(values[:half], (1, 3)), half_chain(values[half:], (3, 1))], 0
+    )
+    return values, inner(values)
 
 
 def local(
@@ -455,31 +542,30 @@
     nodes, width = mesh_init.shape
     copies = mesh_export.shape[0]
     edges = encode_senders.shape[0] * encode_senders.shape[1]
-    depth = 256
-    grid_rows = jnp.pad(grid_in, ((0, 0), (0, depth - variables)))
+    index = lax.axis_index("lat")
+    place = jnp.stack([index & 1, (index >> 1 ^ index >> 2) & 1, index >> 2 & 1]).astype(jnp.int32)
     select = (grid_export[:, None] == jnp.arange(grid_count)[None, :]).astype(bf16)
-    grid_picked = jnp.pad(dot(select, grid_in).astype(bf16), ((0, 0), (0, depth - variables)))
-    grid_near = around(grid_picked)
-    grid_weight = jnp.pad(grid_weight, ((0, depth - variables), (0, 0)))
+    grid_near = around(dot(select, grid_in).astype(bf16))
     export = mesh_export[None]
     encode_gain, node_gain = encode_gain[None], node_gain[None]
-    (
-        state,
-        picked,
-        inputs,
-        hidden,
-        pre_slope,
-        mix_slope,
-        normed,
-        scale,
-        update_normed,
-        update_scale,
-    ) = call(
+    turns = encode_senders.shape[0] // blocks_per_turn
+    saved = [
+        ((edges, variables), bf16),
+        ((edges, width), bf16),
+        ((edges, width), bf16),
+        ((edges, width), bf16),
+        ((edges, width), bf16),
+        ((edges, lanes), f32),
+        ((nodes, width), f32),
+        ((nodes, lanes), f32),
+    ]
+    state, picked, inputs, hidden, pre_slope, mix_slope, normed, scale, *update = call(
         encode_kernel,
         (
             encode_live,
-            start_rows(encode_slots, grid_count),
-            grid_rows,
+            place,
+            encode_slots,
+            grid_in,
             *grid_near,
             mesh_init,
             encode_senders,
@@ -492,32 +578,33 @@
             update_weight,
             encode_gain,
         ),
+        [((nodes, width), bf16, 0), ((copies, width), bf16, 0)] + [each + (1,) for each in saved],
         [
-            ((nodes, width), bf16),
-            ((copies, width), bf16),
-            ((edges, depth), bf16),
-            ((edges, width), bf16),
-            ((edges, width), bf16),
-            ((edges, width), bf16),
-            ((edges, width), bf16),
-            ((edges, lanes), f32),
-            ((nodes, width), f32),
-            ((nodes, lanes), f32),
-        ],
-        [
-            ((grid_count + 8 * lanes + grid_count - lanes, depth), bf16),
+            ((grid_count + 8 * lanes + grid_count - lanes, variables), bf16),
             ((256, width), bf16),
             ((nodes, width), f32),
-        ],
-        2,
-        16,
+        ]
+        + saved
+        + [pltpu.SemaphoreType.DMA((6, turns)), pltpu.SemaphoreType.DMA((2,))],
+        3,
+        20,
     )
     near = around(picked)
-    mesh_out, own_grad, to_lon, to_inner, to_outer, sender_rows, mix_grad, receiver_grad = call(
+    (
+        mesh_out,
+        own_grad,
+        to_lon,
+        to_inner,
+        to_outer,
+        sender_rows,
+        mix_grad,
+        receiver_grad,
+    ) = call(
         process_kernel,
         (
             process_live,
-            start_rows(process_slots, 256),
+            place,
+            process_slots,
             state,
             *near,
             process_senders,
@@ -530,14 +617,14 @@
             cotangent,
         ),
         [
-            ((nodes, width), bf16),
-            ((nodes, width), f32),
-            ((2 * copies, width), bf16),
-            ((3 * copies, width), bf16),
-            ((3 * copies, width), bf16),
-            ((edges, width), bf16),
-            ((edges, width), bf16),
-            ((nodes, width), bf16),
+            ((nodes, width), bf16, 1),
+            ((nodes, width), f32, 1),
+            ((2 * copies, width), bf16, 0),
+            ((3 * copies, width), bf16, 0),
+            ((3 * copies, width), bf16, 0),
+            ((edges, width), bf16, 1),
+            ((edges, width), bf16, 1),
+            ((nodes, width), bf16, 0),
         ],
         [
             ((256 + 8 * copies + 128, width), bf16),
@@ -549,9 +636,14 @@
             ((256, width), bf16),
             ((256 + 8 * copies + 128, width), f32),
             ((nodes, width), f32),
+            ((nodes, width), bf16),
+            ((edges, width), bf16),
+            ((edges, width), bf16),
+            pltpu.SemaphoreType.DMA((2, turns)),
+            pltpu.SemaphoreType.DMA((2,)),
         ],
-        2,
-        24,
+        3,
+        26,
     )
     from_inner, from_outer = inner(to_inner), outer(to_outer)
     to_left, to_right = [
@@ -565,10 +657,11 @@
     from_right, from_left = shifted(to_left, -1), shifted(to_right, 1)
     state_part = cotangent.astype(f32) + back_dot(receiver_grad, edge_receiver)
     edge_grad = cross_dot(sender_rows, mix_grad).astype(bf16)
-    mix_grad, pre_grad = call(
+    given, kept = call(
         encode_back_kernel,
         (
             encode_live,
+            place,
             encode_receivers,
             export,
             state_part,
@@ -578,32 +671,35 @@
             from_left,
             from_right,
             edge_sender,
-            update_normed,
-            update_scale,
+            update[0],
+            update[1],
             encode_gain,
             update_weight,
             normed,
             scale,
             mix_slope,
             pre_slope,
+            inputs,
+            hidden,
             message_weight,
             sender_weight,
+            edge_grad,
         ),
-        [((edges, width), bf16), ((edges, width), bf16)],
-        [((256, width), bf16)],
+        [((640, width), bf16, 0)] * 2,
+        [((256, width), bf16), ((1280, width), f32)],
+        2,
+        16,
+    )
+    mine, other = summed(given, kept)
+    sender_grad, edge_grad, grid_grad = call(
+        order_kernel,
+        (place, mine, other),
+        [((width, width), f32, 1), ((width, width), f32, 1), ((variables, width), f32, 1)],
+        [((1280, width), f32), ((variables, width), f32), pltpu.SemaphoreType.DMA((3,))],
         1,
-        12,
-    )
-    sender_grad = cross_dot(hidden, mix_grad).astype(bf16)
-    grid_grad = cross_dot(inputs, pre_grad).astype(bf16)
-    halves = summed(jnp.concatenate([sender_grad, edge_grad, grid_grad], 0))
-    totals = jnp.concatenate(halves, 0).astype(f32)
-    return (
-        mesh_out,
-        totals[2 * width : 2 * width + variables],
-        totals[:width],
-        totals[width : 2 * width],
-    )
+        8,
+    )
+    return mesh_out, grid_grad, sender_grad, edge_grad
 
 
 def solution(mesh):

time: 146 us -> 155 us (1.062)
  waiting for transfers between devices: 46.9 us -> 68.1 us
  local copies, waits for them, and re-layouts: 10.1 us -> 5.2 us
  starting transfers between devices: 57.5 us -> 52.7 us
  Pallas kernels: 18.1 us -> 22.6 us
  other arithmetic: 4.95 us -> 0.68 us
  matrix products: 5.32 us -> 2.31 us
    ppermute x6, waiting for transfers between devices: 4.17 us -> 17.7 us  [shifted(): return lax.ppermute(x, 'lon', [(i, (i + step) % size) for i in range(size)])]
    ppermute x6, starting transfers between devices: 17 us -> 9.34 us  [shifted(): return lax.ppermute(x, 'lon', [(i, (i + step) % size) for i in range(size)])]
    pallas_call x3 -> x4, Pallas kernels: 18.1 us -> 22.6 us  [call(): pl.pallas_call(kernel, out_shape=[jax.ShapeDtypeStruct(shape, dtype) for...]
    ppermute x19 -> x23, waiting for transfers between devices: 35.9 us -> 40.3 us  [partner(): lax.ppermute(x, axis, [(i, i ^ flip) for i in range(lax.axis_size(axis))])]
    unnamed x79 -> x50, local copies, waits for them, and re-layouts: 8.91 us -> 5.13 us
    ppermute x5, waiting for transfers between devices: 6.83 us -> 10 us  [outer(): lax.ppermute(x, 'lat', [(i, i + 1) for i in ends] + [(i + 1, i) for i in...]
    dot_general x3 -> x1, matrix products: 3.6 us -> 0.73 us  [cross_dot(): lax.dot_general(left, right, (((0,), (0,)), ((), ())), preferred_element_...]
    ppermute x5, starting transfers between devices: 18.1 us -> 20.6 us  [outer(): lax.ppermute(x, 'lat', [(i, i + 1) for i in ends] + [(i + 1, i) for i in...]
  transfers between devices with their start and end apart: 30 -> 34, of which waited for: 17 -> 26; matrix products, arithmetic and copies ran while one was open for 4% -> 2% of each run, Pallas kernels for 0% -> 0%
where the time goes in v2:
time: 155 us; the launch traced here: 154 us
  waiting for transfers between devices  68.1 us (44%)
  starting transfers between devices  52.7 us (34%)
  Pallas kernels  22.6 us (15%)
  local copies, waits for them, and re-layouts  5.2 us (3%)
  between operations  2.69 us (2%)
  matrix products  2.31 us (1%)
    ppermute x23, waiting for transfers between devices, partner(): lax.ppermute(x, axis, [(i, i ^ flip) for i in range(lax.axis_size(axis))])  40.3 us
    ppermute x23, starting transfers between devices, partner(): lax.ppermute(x, axis, [(i, i ^ flip) for i in range(lax.axis_size(axis))])  22.8 us
    pallas_call x4, Pallas kernels, call(): pl.pallas_call(kernel, out_shape=[jax.ShapeDtypeStruct(shape, dtype) for...  22.6 us
    ppermute x5, starting transfers between devices, outer(): lax.ppermute(x, 'lat', [(i, i + 1) for i in ends] + [(i + 1, i) for i in...  20.6 us
    ppermute x6, waiting for transfers between devices, shifted(): return lax.ppermute(x, 'lon', [(i, (i + step) % size) for i in range(size)])  17.7 us
    ppermute x5, waiting for transfers between devices, outer(): lax.ppermute(x, 'lat', [(i, i + 1) for i in ends] + [(i + 1, i) for i in...  10 us
    ppermute x6, starting transfers between devices, shifted(): return lax.ppermute(x, 'lon', [(i, (i + step) % size) for i in range(size)])  9.34 us
    unnamed x50, local copies, waits for them, and re-layouts  5.13 us
  transfers between devices with their start and end apart: 34, of which 26 were waited for; matrix products, arithmetic and copies ran while one was open for 2% of the time, Pallas kernels for 0%

profile of v2, /device:TPU:1, one launch (start us, length us, event | category | flops | bytes accessed | tf_op | source)
XLA Modules:
  0.0 154.2 jit_solution(17790343282153044649)
XLA Ops:
  2.0 4.5 %collective-permute-start.3 = (bf16[128,227]{1,0:T(8,128)(2,1)S(1)}, bf16[128,227]{1,0:T(8,128)(2,1)S(1)}, u32[]{:S(2)}, u32[]{:S(2)}) collective-permute-start(bf16[128,227]{1,0:T(8,128)(2,1)S(1)} %convolution_convert_fusion.1), channel_id=1, source_target_pairs={{16,32},{48,64},{80,96},{32,16},{64,48},{96,80},{17,33},{49,65},{8... | collective-permute-start | bytes 174344 | tf_op jit(solution)/shard_map/ppermute | solution.py:478
  6.6 6.3 %collective-permute-start.1 = (bf16[128,227]{1,0:T(8,128)(2,1)S(1)}, bf16[128,227]{1,0:T(8,128)(2,1)S(1)}, u32[]{:S(2)}, u32[]{:S(2)}) collective-permute-start(bf16[128,227]{1,0:T(8,128)(2,1)S(1)} %convolution_convert_fusion.1), channel_id=1, source_target_pairs={{0,15},{1,0},{2,1},{3,2},{4,3},{5,4},{6,5},{7,6},{8,7},{9,8},{10,9... | collective-permute-start | bytes 174344 | tf_op jit(solution)/shard_map/ppermute | solution.py:465
  14.2 5.1 %collective-permute-done.near_left = bf16[128,227]{1,0:T(8,128)(2,1)S(1)} collective-permute-done((bf16[128,227]{1,0:T(8,128)(2,1)S(1)}, bf16[128,227]{1,0:T(8,128)(2,1)S(1)}, u32[]{:S(2)}, u32[]{:S(2)}) %collective-permute-start) | collective-permute-done | bytes 58144 | tf_op jit(solution)/shard_map/ppermute | solution.py:465
  19.3 4.9 %collective-permute-start.5 = (bf16[256,227]{1,0:T(8,128)(2,1)S(1)}, bf16[256,227]{1,0:T(8,128)(2,1)S(1)}, u32[]{:S(2)}, u32[]{:S(2)}) collective-permute-start(bf16[256,227]{1,0:T(8,128)(2,1)S(1)} %constant_dynamic-update-slice_fusion), channel_id=1, source_target_pairs={{16,32},{48,64},{80,96},{32,16},{64,48},{96,80},{17,33},{49,65},{8... | collective-permute-start | bytes 348680 | tf_op jit(solution)/shard_map/ppermute | solution.py:478
  30.9 6.7 %shard_map.255 = (bf16[160,512]{1,0:T(8,128)(2,1)S(1)}, bf16[128,512]{1,0:T(8,128)(2,1)S(1)}, bf16[1024,227]{1,0:T(8,128)(2,1)S(1)}, bf16[1024,512]{1,0:T(8,128)...) custom-call(s32[1]{0:T(128)S(6)} %copy.38.live_ref, ...), custom_call_target="tpu_custom_call" | custom-call | flops 4294967296 | bytes 8388608 | tf_op jit(solution)/shard_map/pallas_call | solution.py:452
  37.6 3.6 %collective-permute-start.9 = (bf16[128,512]{1,0:T(8,128)(2,1)S(1)}, bf16[128,512]{1,0:T(8,128)(2,1)S(1)}, u32[]{:S(2)}, u32[]{:S(2)}) collective-permute-start(bf16[128,512]{1,0:T(8,128)(2,1)S(1)} %get-tuple-element.40), channel_id=1, source_target_pairs={{16,32},{48,64},{80,96},{32,16},{64,48},{96,80},{17,33},{49,65},{8... | collective-permute-start | bytes 393224 | tf_op jit(solution)/shard_map/ppermute | solution.py:478
  46.1 3.5 %collective-permute-done.6.near_left = bf16[128,512]{1,0:T(8,128)(2,1)S(1)} collective-permute-done((bf16[128,512]{1,0:T(8,128)(2,1)S(1)}, bf16[128,512]{1,0:T(8,128)(2,1)S(1)}, u32[]{:S(2)}, u32[]{:S(2)}) %collective-permute-start.6) | collective-permute-done | bytes 131104 | tf_op jit(solution)/shard_map/ppermute | solution.py:465
  49.6 3.9 %collective-permute-start.11 = (bf16[256,512]{1,0:T(8,128)(2,1)S(1)}, bf16[256,512]{1,0:T(8,128)(2,1)S(1)}, u32[]{:S(2)}, u32[]{:S(2)}) collective-permute-start(bf16[256,512]{1,0:T(8,128)(2,1)S(1)} %constant_dynamic-update-slice_fusion.2), channel_id=1, source_target_pairs={{16,32},{48,64},{80,96},{32,16},{64,48},{96,80},{17,33},{49,65},{8... | collective-permute-start | bytes 786440 | tf_op jit(solution)/shard_map/ppermute | solution.py:478
  54.2 3.3 %collective-permute-done.11.near_outer_corners = bf16[256,512]{1,0:T(8,128)(2,1)S(1)} collective-permute-done((bf16[256,512]{1,0:T(8,128)(2,1)S(1)}, bf16[256,512]{1,0:T(8,128)(2,1)S(1)}, u32[]{:S(2)}, u32[]{:S(2)}) %collective-permute-start.11) | collective-permute-done | bytes 262176 | tf_op jit(solution)/shard_map/ppermute | solution.py:478
  57.6 8.5 %shard_map.256 = (bf16[160,512]{1,0:T(8,128)(2,1)}, f32[160,512]{1,0:T(8,128)S(1)}, bf16[256,512]{1,0:T(8,128)(2,1)S(1)}, bf16[384,512]{1,0:T(8,128)(2,1)S(1)}, ...) custom-call(s32[1]{0:T(128)S(6)} %copy.39.live_ref, ...), custom_call_target="tpu_custom_call" | custom-call | flops 4294967296 | bytes 8388608 | tf_op jit(solution)/shard_map/pallas_call | solution.py:452
  66.2 3.6 %collective-permute-start.13 = (bf16[384,512]{1,0:T(8,128)(2,1)S(1)}, bf16[384,512]{1,0:T(8,128)(2,1)S(1)}, u32[]{:S(2)}, u32[]{:S(2)}) collective-permute-start(bf16[384,512]{1,0:T(8,128)(2,1)S(1)} %get-tuple-element.49), channel_id=1, source_target_pairs={{16,32},{48,64},{80,96},{32,16},{64,48},{96,80},{17,33},{49,65},{8... | collective-permute-start | bytes 1179656 | tf_op jit(solution)/shard_map/ppermute | solution.py:478
  70.6 5.0 %collective-permute-done.13.from_outer = bf16[384,512]{1,0:T(8,128)(2,1)S(1)} collective-permute-done((bf16[384,512]{1,0:T(8,128)(2,1)S(1)}, bf16[384,512]{1,0:T(8,128)(2,1)S(1)}, u32[]{:S(2)}, u32[]{:S(2)}) %collective-permute-start.13) | collective-permute-done | bytes 393248 | tf_op jit(solution)/shard_map/ppermute | solution.py:478
  79.6 3.6 %collective-permute-done.14.from_left = bf16[128,512]{1,0:T(8,128)(2,1)S(1)} collective-permute-done((bf16[128,512]{1,0:T(8,128)(2,1)S(1)}, bf16[128,512]{1,0:T(8,128)(2,1)S(1)}, u32[]{:S(2)}, u32[]{:S(2)}) %collective-permute-start.14) | collective-permute-done | bytes 131104 | tf_op jit(solution)/shard_map/ppermute | solution.py:465
  83.2 5.1 %shard_map.257 = (bf16[640,512]{1,0:T(8,128)(2,1)S(1)}, bf16[640,512]{1,0:T(8,128)(2,1)S(1)}) custom-call(s32[1]{0:T(128)S(6)} %copy.38.live_ref, s32[3]{0:T(128)S(1)} %pad_add_fusion.place_ref, s32[8,128]{1,0:T(8,128)S(1)} %copy-done.16, s32[1,128]{1,0:T(1,128)S(1)} %bitcast.15, f32[160,512]{1,0:T(8,128)S(1)} %convolution_add_fusion.state_part, ...), custom_call_target="tpu_custom_call" | custom-call | flops 4294967296 | bytes 8388608 | tf_op jit(solution)/shard_map/pallas_call | solution.py:452
  94.3 3.4 %collective-permute-done.25 = bf16[160,512]{1,0:T(8,128)(2,1)S(1)} collective-permute-done((bf16[160,512]{1,0:T(8,128)(2,1)S(1)}, bf16[160,512]{1,0:T(8,128)(2,1)S(1)}, u32[]{:S(2)}, u32[]{:S(2)}) %collective-permute-start.25) | collective-permute-done | bytes 163872 | tf_op jit(solution)/shard_map/ppermute | solution.py:469
  100.3 2.6 %collective-permute-done.18 = bf16[80,512]{1,0:T(8,128)(2,1)S(1)} collective-permute-done((bf16[80,512]{1,0:T(8,128)(2,1)S(1)}, bf16[80,512]{1,0:T(8,128)(2,1)S(1)}, u32[]{:S(2)}, u32[]{:S(2)}) %collective-permute-start.18) | collective-permute-done | bytes 81952 | tf_op jit(solution)/shard_map/ppermute | solution.py:469
  103.0 3.3 %collective-permute-done.19 = bf16[80,512]{1,0:T(8,128)(2,1)S(1)} collective-permute-done((bf16[80,512]{1,0:T(8,128)(2,1)S(1)}, bf16[80,512]{1,0:T(8,128)(2,1)S(1)}, u32[]{:S(2)}, u32[]{:S(2)}) %collective-permute-start.19) | collective-permute-done | bytes 81952 | tf_op jit(solution)/shard_map/ppermute | solution.py:469
  106.6 4.3 %collective-permute-done.20 = bf16[80,512]{1,0:T(8,128)(2,1)S(1)} collective-permute-done((bf16[80,512]{1,0:T(8,128)(2,1)S(1)}, bf16[80,512]{1,0:T(8,128)(2,1)S(1)}, u32[]{:S(2)}, u32[]{:S(2)}) %collective-permute-start.20) | collective-permute-done | bytes 81952 | tf_op jit(solution)/shard_map/ppermute | solution.py:469
  115.9 3.3 %collective-permute-done.22 = bf16[80,512]{1,0:T(8,128)(2,1)S(1)} collective-permute-done((bf16[80,512]{1,0:T(8,128)(2,1)S(1)}, bf16[80,512]{1,0:T(8,128)(2,1)S(1)}, u32[]{:S(2)}, u32[]{:S(2)}) %collective-permute-start.22) | collective-permute-done | bytes 81952 | tf_op jit(solution)/shard_map/ppermute | solution.py:469
  121.6 2.2 %collective-permute-done.23 = bf16[80,512]{1,0:T(8,128)(2,1)S(1)} collective-permute-done((bf16[80,512]{1,0:T(8,128)(2,1)S(1)}, bf16[80,512]{1,0:T(8,128)(2,1)S(1)}, u32[]{:S(2)}, u32[]{:S(2)}) %collective-permute-start.23) | collective-permute-done | bytes 81952 | tf_op jit(solution)/shard_map/ppermute | solution.py:469
  123.9 2.4 %collective-permute-done.29 = bf16[80,512]{1,0:T(8,128)(2,1)S(1)} collective-permute-done((bf16[80,512]{1,0:T(8,128)(2,1)S(1)}, bf16[80,512]{1,0:T(8,128)(2,1)S(1)}, u32[]{:S(2)}, u32[]{:S(2)}) %collective-permute-start.29) | collective-permute-done | bytes 81952 | tf_op jit(solution)/shard_map/ppermute | solution.py:469
  129.8 3.6 %collective-permute-done.31 = bf16[80,512]{1,0:T(8,128)(2,1)S(1)} collective-permute-done((bf16[80,512]{1,0:T(8,128)(2,1)S(1)}, bf16[80,512]{1,0:T(8,128)(2,1)S(1)}, u32[]{:S(2)}, u32[]{:S(2)}) %collective-permute-start.31) | collective-permute-done | bytes 81952 | tf_op jit(solution)/shard_map/ppermute | solution.py:469
  134.4 4.5 %collective-permute-done.32 = bf16[160,512]{1,0:T(8,128)(2,1)S(1)} collective-permute-done((bf16[160,512]{1,0:T(8,128)(2,1)S(1)}, bf16[160,512]{1,0:T(8,128)(2,1)S(1)}, u32[]{:S(2)}, u32[]{:S(2)}) %collective-permute-start.32) | collective-permute-done | bytes 163872 | tf_op jit(solution)/shard_map/ppermute | solution.py:469
  138.9 11.2 %collective-permute-start.33 = (bf16[640,512]{1,0:T(8,128)(2,1)S(1)}, bf16[640,512]{1,0:T(8,128)(2,1)S(1)}, u32[]{:S(2)}, u32[]{:S(2)}) collective-permute-start(bf16[640,512]{1,0:T(8,128)(2,1)S(1)} %constant_dynamic-update-slice_fusion.4.mine), channel_id=1, source_target_pairs={{0,16},{16,0},{32,48},{48,32},{64,80},{80,64},{96,112},{112,96},{1... | collective-permute-start | bytes 1966088 | tf_op jit(solution)/shard_map/ppermute | solution.py:469
  (123 shorter events, 43.1 us)
Async XLA Ops:
  2.0 10.9 %collective-permute-start.3 = (bf16[128,227]{1,0:T(8,128)(2,1)S(1)}, bf16[128,227]{1,0:T(8,128)(2,1)S(1)}, u32[]{:S(2)}, u32[]{:S(2)}) collective-permute-start(bf16[128,227]{1,0:T(8,128)(2,1)S(1)} %convolution_convert_fusion.1), channel_id=1, source_target_pairs={{16,32},{48,64},{80,96},{32,16},{64,48},{96,80},{17,33},{49,65},{8... | collective-permute-start | bytes 174344 | tf_op jit(solution)/shard_map/ppermute | solution.py:478
  6.5 6.4 %collective-permute-start.2 = (bf16[128,227]{1,0:T(8,128)(2,1)S(1)}, bf16[128,227]{1,0:T(8,128)(2,1)S(1)}, u32[]{:S(2)}, u32[]{:S(2)}) collective-permute-start(bf16[128,227]{1,0:T(8,128)(2,1)S(1)} %convolution_convert_fusion.1), channel_id=1, source_target_pairs={{0,16},{16,0},{32,48},{48,32},{64,80},{80,64},{96,112},{112,96},{1... | collective-permute-start | bytes 174344 | tf_op jit(solution)/shard_map/ppermute | solution.py:469
  6.6 7.6 %collective-permute-start.1 = (bf16[128,227]{1,0:T(8,128)(2,1)S(1)}, bf16[128,227]{1,0:T(8,128)(2,1)S(1)}, u32[]{:S(2)}, u32[]{:S(2)}) collective-permute-start(bf16[128,227]{1,0:T(8,128)(2,1)S(1)} %convolution_convert_fusion.1), channel_id=1, source_target_pairs={{0,15},{1,0},{2,1},{3,2},{4,3},{5,4},{6,5},{7,6},{8,7},{9,8},{10,9... | collective-permute-start | bytes 174344 | tf_op jit(solution)/shard_map/ppermute | solution.py:465
  12.9 6.4 %collective-permute-start = (bf16[128,227]{1,0:T(8,128)(2,1)S(1)}, bf16[128,227]{1,0:T(8,128)(2,1)S(1)}, u32[]{:S(2)}, u32[]{:S(2)}) collective-permute-start(bf16[128,227]{1,0:T(8,128)(2,1)S(1)} %convolution_convert_fusion.1), channel_id=1, source_target_pairs={{0,1},{1,2},{2,3},{3,4},{4,5},{5,6},{6,7},{7,8},{8,9},{9,10},{10,1... | collective-permute-start | bytes 174344 | tf_op jit(solution)/shard_map/ppermute | solution.py:465
  19.3 7.5 %collective-permute-start.5 = (bf16[256,227]{1,0:T(8,128)(2,1)S(1)}, bf16[256,227]{1,0:T(8,128)(2,1)S(1)}, u32[]{:S(2)}, u32[]{:S(2)}) collective-permute-start(bf16[256,227]{1,0:T(8,128)(2,1)S(1)} %constant_dynamic-update-slice_fusion), channel_id=1, source_target_pairs={{16,32},{48,64},{80,96},{32,16},{64,48},{96,80},{17,33},{49,65},{8... | collective-permute-start | bytes 348680 | tf_op jit(solution)/shard_map/ppermute | solution.py:478
  37.6 6.3 %collective-permute-start.9 = (bf16[128,512]{1,0:T(8,128)(2,1)S(1)}, bf16[128,512]{1,0:T(8,128)(2,1)S(1)}, u32[]{:S(2)}, u32[]{:S(2)}) collective-permute-start(bf16[128,512]{1,0:T(8,128)(2,1)S(1)} %get-tuple-element.40), channel_id=1, source_target_pairs={{16,32},{48,64},{80,96},{32,16},{64,48},{96,80},{17,33},{49,65},{8... | collective-permute-start | bytes 393224 | tf_op jit(solution)/shard_map/ppermute | solution.py:478
  41.4 4.7 %collective-permute-start.7 = (bf16[128,512]{1,0:T(8,128)(2,1)S(1)}, bf16[128,512]{1,0:T(8,128)(2,1)S(1)}, u32[]{:S(2)}, u32[]{:S(2)}) collective-permute-start(bf16[128,512]{1,0:T(8,128)(2,1)S(1)} %get-tuple-element.40), channel_id=1, source_target_pairs={{0,15},{1,0},{2,1},{3,2},{4,3},{5,4},{6,5},{7,6},{8,7},{9,8},{10,9... | collective-permute-start | bytes 393224 | tf_op jit(solution)/shard_map/ppermute | solution.py:465
  41.4 8.1 %collective-permute-start.6 = (bf16[128,512]{1,0:T(8,128)(2,1)S(1)}, bf16[128,512]{1,0:T(8,128)(2,1)S(1)}, u32[]{:S(2)}, u32[]{:S(2)}) collective-permute-start(bf16[128,512]{1,0:T(8,128)(2,1)S(1)} %get-tuple-element.40), channel_id=1, source_target_pairs={{0,1},{1,2},{2,3},{3,4},{4,5},{5,6},{6,7},{7,8},{8,9},{9,10},{10,1... | collective-permute-start | bytes 393224 | tf_op jit(solution)/shard_map/ppermute | solution.py:465
  49.6 8.0 %collective-permute-start.11 = (bf16[256,512]{1,0:T(8,128)(2,1)S(1)}, bf16[256,512]{1,0:T(8,128)(2,1)S(1)}, u32[]{:S(2)}, u32[]{:S(2)}) collective-permute-start(bf16[256,512]{1,0:T(8,128)(2,1)S(1)} %constant_dynamic-update-slice_fusion.2), channel_id=1, source_target_pairs={{16,32},{48,64},{80,96},{32,16},{64,48},{96,80},{17,33},{49,65},{8... | collective-permute-start | bytes 786440 | tf_op jit(solution)/shard_map/ppermute | solution.py:478
  66.1 4.5 %collective-permute-start.12 = (bf16[384,512]{1,0:T(8,128)(2,1)S(1)}, bf16[384,512]{1,0:T(8,128)(2,1)S(1)}, u32[]{:S(2)}, u32[]{:S(2)}) collective-permute-start(bf16[384,512]{1,0:T(8,128)(2,1)S(1)} %get-tuple-element.48), channel_id=1, source_target_pairs={{0,16},{16,0},{32,48},{48,32},{64,80},{80,64},{96,112},{112,96},{1... | collective-permute-start | bytes 1179656 | tf_op jit(solution)/shard_map/ppermute | solution.py:469
  66.2 9.4 %collective-permute-start.13 = (bf16[384,512]{1,0:T(8,128)(2,1)S(1)}, bf16[384,512]{1,0:T(8,128)(2,1)S(1)}, u32[]{:S(2)}, u32[]{:S(2)}) collective-permute-start(bf16[384,512]{1,0:T(8,128)(2,1)S(1)} %get-tuple-element.49), channel_id=1, source_target_pairs={{16,32},{48,64},{80,96},{32,16},{64,48},{96,80},{17,33},{49,65},{8... | collective-permute-start | bytes 1179656 | tf_op jit(solution)/shard_map/ppermute | solution.py:478
  75.8 7.4 %collective-permute-start.14 = (bf16[128,512]{1,0:T(8,128)(2,1)S(1)}, bf16[128,512]{1,0:T(8,128)(2,1)S(1)}, u32[]{:S(2)}, u32[]{:S(2)}) collective-permute-start(bf16[128,512]{1,0:T(8,128)(2,1)S(1)} %get-tuple-element.71), channel_id=1, source_target_pairs={{0,1},{1,2},{2,3},{3,4},{4,5},{5,6},{6,7},{7,8},{8,9},{9,10},{10,1... | collective-permute-start | bytes 393224 | tf_op jit(solution)/shard_map/ppermute | solution.py:465
  90.7 7.0 %collective-permute-start.25 = (bf16[160,512]{1,0:T(8,128)(2,1)S(1)}, bf16[160,512]{1,0:T(8,128)(2,1)S(1)}, u32[]{:S(2)}, u32[]{:S(2)}) collective-permute-start(bf16[160,512]{1,0:T(8,128)(2,1)S(1)} %get-tuple-element.74), channel_id=1, source_target_pairs={{0,96},{16,112},{32,64},{48,80},{64,32},{80,48},{96,0},{112,16},{1... | collective-permute-start | bytes 491528 | tf_op jit(solution)/shard_map/ppermute | solution.py:469
  92.6 5.5 %collective-permute-start.17 = (bf16[160,512]{1,0:T(8,128)(2,1)S(1)}, bf16[160,512]{1,0:T(8,128)(2,1)S(1)}, u32[]{:S(2)}, u32[]{:S(2)}) collective-permute-start(bf16[160,512]{1,0:T(8,128)(2,1)S(1)} %get-tuple-element.75), channel_id=1, source_target_pairs={{0,32},{16,48},{32,0},{48,16},{64,96},{80,112},{96,64},{112,80},{1... | collective-permute-start | bytes 491528 | tf_op jit(solution)/shard_map/ppermute | solution.py:469
  98.3 4.6 %collective-permute-start.18 = (bf16[80,512]{1,0:T(8,128)(2,1)S(1)}, bf16[80,512]{1,0:T(8,128)(2,1)S(1)}, u32[]{:S(2)}, u32[]{:S(2)}) collective-permute-start(bf16[80,512]{1,0:T(8,128)(2,1)S(1)} %slice.69), channel_id=1, source_target_pairs={{0,96},{16,112},{32,64},{48,80},{64,32},{80,48},{96,0},{112,16},{1... | collective-permute-start | bytes 245768 | tf_op jit(solution)/shard_map/ppermute | solution.py:469
  106.3 4.6 %collective-permute-start.20 = (bf16[80,512]{1,0:T(8,128)(2,1)S(1)}, bf16[80,512]{1,0:T(8,128)(2,1)S(1)}, u32[]{:S(2)}, u32[]{:S(2)}) collective-permute-start(bf16[80,512]{1,0:T(8,128)(2,1)S(1)} %add_convert_fusion.13), channel_id=1, source_target_pairs={{0,3},{1,2},{2,1},{3,0},{4,7},{5,6},{6,5},{7,4},{8,11},{9,10},{10,... | collective-permute-start | bytes 245768 | tf_op jit(solution)/shard_map/ppermute | solution.py:469
  106.4 4.6 %collective-permute-start.26 = (bf16[80,512]{1,0:T(8,128)(2,1)S(1)}, bf16[80,512]{1,0:T(8,128)(2,1)S(1)}, u32[]{:S(2)}, u32[]{:S(2)}) collective-permute-start(bf16[80,512]{1,0:T(8,128)(2,1)S(1)} %slice.73), channel_id=1, source_target_pairs={{0,32},{16,48},{32,0},{48,16},{64,96},{80,112},{96,64},{112,80},{1... | collective-permute-start | bytes 245768 | tf_op jit(solution)/shard_map/ppermute | solution.py:469
  111.0 4.8 %collective-permute-start.27 = (bf16[80,512]{1,0:T(8,128)(2,1)S(1)}, bf16[80,512]{1,0:T(8,128)(2,1)S(1)}, u32[]{:S(2)}, u32[]{:S(2)}) collective-permute-start(bf16[80,512]{1,0:T(8,128)(2,1)S(1)} %add_convert_fusion.9), channel_id=1, source_target_pairs={{0,3},{1,2},{2,1},{3,0},{4,7},{5,6},{6,5},{7,4},{8,11},{9,10},{10,... | collective-permute-start | bytes 245768 | tf_op jit(solution)/shard_map/ppermute | solution.py:469
  114.6 4.6 %collective-permute-start.22 = (bf16[80,512]{1,0:T(8,128)(2,1)S(1)}, bf16[80,512]{1,0:T(8,128)(2,1)S(1)}, u32[]{:S(2)}, u32[]{:S(2)}) collective-permute-start(bf16[80,512]{1,0:T(8,128)(2,1)S(1)} %add_convert_fusion.11), channel_id=1, source_target_pairs={{0,12},{1,13},{2,14},{3,15},{4,8},{5,9},{6,10},{7,11},{8,4},{9,5},... | collective-permute-start | bytes 245768 | tf_op jit(solution)/shard_map/ppermute | solution.py:469
  115.8 5.4 %collective-permute-start.28 = (bf16[80,512]{1,0:T(8,128)(2,1)S(1)}, bf16[80,512]{1,0:T(8,128)(2,1)S(1)}, u32[]{:S(2)}, u32[]{:S(2)}) collective-permute-start(bf16[80,512]{1,0:T(8,128)(2,1)S(1)} %add_convert_fusion.8), channel_id=1, source_target_pairs={{0,1},{1,0},{2,3},{3,2},{4,5},{5,4},{6,7},{7,6},{8,9},{9,8},{10,11... | collective-permute-start | bytes 245768 | tf_op jit(solution)/shard_map/ppermute | solution.py:469
  119.2 4.6 %collective-permute-start.23 = (bf16[80,512]{1,0:T(8,128)(2,1)S(1)}, bf16[80,512]{1,0:T(8,128)(2,1)S(1)}, u32[]{:S(2)}, u32[]{:S(2)}) collective-permute-start(bf16[80,512]{1,0:T(8,128)(2,1)S(1)} %get-tuple-element.69), channel_id=1, source_target_pairs={{0,96},{16,112},{32,64},{48,80},{64,32},{80,48},{96,0},{112,16},{1... | collective-permute-start | bytes 245768 | tf_op jit(solution)/shard_map/ppermute | solution.py:469
  121.2 5.1 %collective-permute-start.29 = (bf16[80,512]{1,0:T(8,128)(2,1)S(1)}, bf16[80,512]{1,0:T(8,128)(2,1)S(1)}, u32[]{:S(2)}, u32[]{:S(2)}) collective-permute-start(bf16[80,512]{1,0:T(8,128)(2,1)S(1)} %add_convert_fusion.7), channel_id=1, source_target_pairs={{0,12},{1,13},{2,14},{3,15},{4,8},{5,9},{6,10},{7,11},{8,4},{9,5},... | collective-permute-start | bytes 245768 | tf_op jit(solution)/shard_map/ppermute | solution.py:469
  133.4 5.5 %collective-permute-start.32 = (bf16[160,512]{1,0:T(8,128)(2,1)S(1)}, bf16[160,512]{1,0:T(8,128)(2,1)S(1)}, u32[]{:S(2)}, u32[]{:S(2)}) collective-permute-start(bf16[160,512]{1,0:T(8,128)(2,1)S(1)} %pad_maximum_fusion.1), channel_id=1, source_target_pairs={{0,96},{16,112},{32,64},{48,80},{64,32},{80,48},{96,0},{112,16},{1... | collective-permute-start | bytes 491528 | tf_op jit(solution)/shard_map/ppermute | solution.py:469
  138.9 12.9 %collective-permute-start.33 = (bf16[640,512]{1,0:T(8,128)(2,1)S(1)}, bf16[640,512]{1,0:T(8,128)(2,1)S(1)}, u32[]{:S(2)}, u32[]{:S(2)}) collective-permute-start(bf16[640,512]{1,0:T(8,128)(2,1)S(1)} %constant_dynamic-update-slice_fusion.4.mine), channel_id=1, source_target_pairs={{0,16},{16,0},{32,48},{48,32},{64,80},{80,64},{96,112},{112,96},{1... | collective-permute-start | bytes 1966088 | tf_op jit(solution)/shard_map/ppermute | solution.py:469
  (32 other events, 476.6 us)

commit v3 on v2

--- a/solution.py
+++ b/solution.py
@@ -58,17 +58,15 @@
     return jnp.where(index == row, 1.0, 0.0).astype(bf16)
 
 
-def live_row(rows, block, live):
-    return jnp.where(block < live, rows[pl.ds(block, 1), :], -1)
-
-
-def window(slots, block, own_rows, core):
+def window(slots, block, own_rows, place_ref):
+    core, odd = place_ref[0], place_ref[3]
     slot = slots[block]
     band = jnp.where(slot >= 6, 2, jnp.where(slot >= 3, 1, 0))
     sector = slot - 3 * band
-    side = jnp.where(sector == 1, 0, jnp.where(sector == 0, 1, 2))
+    close = (sector == 2) == (odd == 0)
+    side = jnp.where(sector == 1, 0, jnp.where(close, 1, 2))
     inside = (band == 2) == (core == 0)
-    place = jnp.where(band == 1, jnp.where(sector == 0, 0, 1), jnp.where(inside, 2, 5) + side)
+    place = jnp.where(band == 1, -1, jnp.where(inside, 2, 5)) + side
     return pl.multiple_of(jnp.where(slot == 4, 0, own_rows + lanes * place), lanes)
 
 
@@ -91,27 +89,56 @@
     pltpu.make_async_copy(source, target, sem).wait()
 
 
+def prepare_kernel(live_ref, senders, receivers, state, weight, *refs):
+    count = (len(refs) - 1) // 2
+    targets, (terms, *hots), sems = refs[:count], refs[count:-1], refs[-1]
+    nodes = state.shape[0]
+    terms[0:nodes, :] = dot(state[...], weight[...]).astype(bf16)
+    terms[nodes:, :] = jnp.zeros_like(terms[nodes:, :])
+    hot_rows(live_ref, senders, receivers, *hots)
+    copies = [
+        (source, target, sems.at[index])
+        for index, (source, target) in enumerate(zip((terms, *hots), targets))
+    ]
+    for copy in copies:
+        send(*copy)
+    for copy in copies:
+        finish(*copy)
+
+
+def hot_rows(
+    live_ref, senders, receivers, send_hot, receive_hot, place_hot, sender_place_hot=None
+):
+    for block in range(senders.shape[0]):
+        here = slice(block * lanes, (block + 1) * lanes)
+        begins = senders[block : block + 1, :]
+        ends = jnp.where(block < live_ref[0], receivers[block : block + 1, :], -1)
+        send_hot[here, :] = lane_hot(begins, send_hot.shape[1])
+        receive_hot[here, :] = lane_hot(ends, receive_hot.shape[1])
+        place_hot[:, here] = row_hot(ends, place_hot.shape[0])
+        if sender_place_hot is not None:
+            sender_place_hot[:, here] = row_hot(begins, sender_place_hot.shape[0])
+
+
 def encode_kernel(
     live_ref,
     place_ref,
     slots,
     grid_own,
-    near_left,
-    near_right,
+    near_close,
+    near_far,
     near_inner,
-    near_inner_corners,
     near_outer,
-    near_outer_corners,
     base,
     senders,
     receivers,
     export,
+    gain,
+    receiver_weight,
     grid_weight,
     sender_weight,
-    receiver_weight,
     message_weight,
     update_weight,
-    gain,
     state,
     picked,
     inputs_out,
@@ -123,7 +150,6 @@
     update_normed_out,
     update_scale_out,
     table,
-    projected,
     total,
     inputs,
     hidden,
@@ -133,22 +159,22 @@
     scale_all,
     update_normed,
     update_scale,
+    projected,
+    send_hot,
+    receive_hot,
+    place_hot,
     sems,
     last_sems,
 ):
     own = grid_own.shape[0]
     nodes = base.shape[0]
-    live, core = live_ref[0], place_ref[0]
-    fill(
-        table,
-        grid_own,
-        (near_left, near_right, near_inner, near_inner_corners, near_outer, near_outer_corners),
-    )
     projected[0:nodes, :] = dot(base[...], receiver_weight[...]).astype(bf16)
     projected[nodes:, :] = jnp.zeros_like(projected[nodes:, :])
+    hot_rows(live_ref, senders, receivers, send_hot, receive_hot, place_hot)
+    fill(table, grid_own, (near_close, near_far, near_inner, near_outer))
     total[...] = jnp.zeros_like(total)
     turn_rows = blocks_per_turn * lanes
-    turns = senders.shape[0] // blocks_per_turn
+    turns = slots.shape[0] // blocks_per_turn
     saved = (
         (inputs, inputs_out),
         (hidden, hidden_out),
@@ -157,18 +183,13 @@
         (normed_all, normed_out),
         (scale_all, scale_out),
     )
-
-    def turn(step, carry):
-        gathered, received, placed = [], [], []
-        for part in range(blocks_per_turn):
-            block = step * blocks_per_turn + part
-            start = window(slots, block, own, core)
-            pick = lane_hot(senders[pl.ds(block, 1), :], own)
+    for step in range(turns):
+        here = pl.ds(step * turn_rows, turn_rows)
+        gathered = []
+        for block in range(step * blocks_per_turn, (step + 1) * blocks_per_turn):
+            start = window(slots, block, own, place_ref)
+            pick = send_hot[block * lanes : (block + 1) * lanes, :]
             gathered.append(dot(pick, table[pl.ds(start, own), :]).astype(bf16))
-            ends = live_row(receivers, block, live)
-            received.append(lane_hot(ends, projected.shape[0]))
-            placed.append(row_hot(ends, nodes))
-        here = pl.ds(pl.multiple_of(step * turn_rows, turn_rows), turn_rows)
         rows = jnp.concatenate(gathered, 0)
         inputs[here, :] = rows
         pre = dot(rows, grid_weight[...])
@@ -177,7 +198,7 @@
         embedded = (pre * gate).astype(bf16)
         hidden[here, :] = embedded
         sent = dot(embedded, sender_weight[...]).astype(bf16).astype(f32)
-        mix = sent + dot(jnp.concatenate(received, 0), projected[...])
+        mix = sent + dot(receive_hot[here, :], projected[...])
         gate = sigmoid(mix)
         mix_slope[here, :] = (gate * (1.0 + mix * (1.0 - gate))).astype(bf16)
         product = dot((mix * gate).astype(bf16), message_weight[...])
@@ -185,12 +206,9 @@
         normed = normed.astype(bf16)
         normed_all[here, :] = normed
         scale_all[here, :] = jnp.broadcast_to(scale, (turn_rows, lanes))
-        total[...] += dot(jnp.concatenate(placed, 1), normed)
+        total[...] += dot(place_hot[:, here], normed)
         for index, (source, target) in enumerate(saved):
             send(source.at[here, :], target.at[here, :], sems.at[index, step])
-        return carry
-
-    lax.fori_loop(0, turns, turn, 0)
     update = dot(total[...].astype(bf16), update_weight[...])
     normed, scale = normalise(update)
     update_normed[...] = normed
@@ -212,20 +230,19 @@
 
 
 def process_kernel(
-    live_ref,
     place_ref,
     slots,
     state,
-    near_left,
-    near_right,
+    near_close,
+    near_far,
     near_inner,
-    near_inner_corners,
     near_outer,
-    near_outer_corners,
-    senders,
-    receivers,
+    terms,
+    send_hot,
+    receive_hot,
+    place_hot,
+    sender_place_hot,
     edge_sender,
-    edge_receiver,
     edge_message,
     node_update,
     gain,
@@ -239,7 +256,6 @@
     mix_grad_out,
     receiver_grad,
     table,
-    terms,
     total,
     slope,
     normed_all,
@@ -255,44 +271,30 @@
 ):
     nodes = state.shape[0]
     reach = 256
-    live, core = live_ref[0], place_ref[0]
-    fill(
-        table,
-        state,
-        (near_left, near_right, near_inner, near_inner_corners, near_outer, near_outer_corners),
-    )
-    terms[0:nodes, :] = dot(state[...], edge_receiver[...]).astype(bf16)
-    terms[nodes:, :] = jnp.zeros_like(terms[nodes:, :])
+    fill(table, state, (near_close, near_far, near_inner, near_outer))
     total[...] = jnp.zeros_like(total)
     turn_rows = blocks_per_turn * lanes
-    turns = senders.shape[0] // blocks_per_turn
-
-    def forward(step, carry):
-        gathered, received, placed = [], [], []
-        for part in range(blocks_per_turn):
-            block = step * blocks_per_turn + part
-            start = window(slots, block, reach, core)
-            pick = lane_hot(senders[pl.ds(block, 1), :], reach)
+    turns = slots.shape[0] // blocks_per_turn
+
+    for step in range(turns):
+        here = pl.ds(step * turn_rows, turn_rows)
+        gathered = []
+        for block in range(step * blocks_per_turn, (step + 1) * blocks_per_turn):
+            start = window(slots, block, reach, place_ref)
+            pick = send_hot[block * lanes : (block + 1) * lanes, :]
             gathered.append(dot(pick, table[pl.ds(start, reach), :]).astype(bf16))
-            ends = live_row(receivers, block, live)
-            received.append(lane_hot(ends, reach))
-            placed.append(row_hot(ends, nodes))
-        here = pl.ds(pl.multiple_of(step * turn_rows, turn_rows), turn_rows)
         rows = jnp.concatenate(gathered, 0)
         sender_rows[here, :] = rows
         sent = dot(rows, edge_sender[...]).astype(bf16).astype(f32)
-        mix = sent + dot(jnp.concatenate(received, 0), terms[...])
+        mix = sent + dot(receive_hot[here, :], terms[...])
         gate = sigmoid(mix)
         slope[here, :] = gate * (1.0 + mix * (1.0 - gate))
         product = dot((mix * gate).astype(bf16), edge_message[...])
         normed, scale = normalise(product)
         normed_all[here, :] = normed
         scale_all[here, :] = jnp.broadcast_to(scale, (turn_rows, lanes))
-        total[...] += dot(jnp.concatenate(placed, 1), normed.astype(bf16))
+        total[...] += dot(place_hot[:, here], normed.astype(bf16))
         send(sender_rows.at[here, :], sender_rows_out.at[here, :], sems.at[0, step])
-        return carry
-
-    lax.fori_loop(0, turns, forward, 0)
     update = dot(total[...].astype(bf16), node_update[...])
     normed, scale = normalise(update)
     mesh_out[...] = (state[...].astype(f32) + normed * gain[...]).astype(bf16)
@@ -303,30 +305,22 @@
     table_grad[...] = jnp.zeros_like(table_grad)
     receiver_total[...] = jnp.zeros_like(receiver_total)
 
-    def backward(step, carry):
-        received, placed = [], []
-        for part in range(blocks_per_turn):
-            ends = live_row(receivers, step * blocks_per_turn + part, live)
-            received.append(lane_hot(ends, reach))
-            placed.append(row_hot(ends, nodes))
-        here = pl.ds(pl.multiple_of(step * turn_rows, turn_rows), turn_rows)
-        arriving = dot(jnp.concatenate(received, 0), upstream[...])
+    for step in range(turns):
+        here = pl.ds(step * turn_rows, turn_rows)
+        arriving = dot(receive_hot[here, :], upstream[...])
         product_grad = norm_back(normed_all[here, :], scale_all[here, 0:1], arriving)
         mix_grad = back_dot(product_grad.astype(bf16), edge_message[...]) * slope[here, :]
         mix_grad = mix_grad.astype(bf16)
         mix_grads[here, :] = mix_grad
         send(mix_grads.at[here, :], mix_grad_out.at[here, :], sems.at[1, step])
-        receiver_total[...] += dot(jnp.concatenate(placed, 1), mix_grad)
+        receiver_total[...] += dot(place_hot[:, here], mix_grad)
         for part in range(blocks_per_turn):
             block = step * blocks_per_turn + part
-            start = window(slots, block, reach, core)
-            place = row_hot(senders[pl.ds(block, 1), :], nodes)
+            start = window(slots, block, reach, place_ref)
             table_grad[pl.ds(start, nodes), :] += dot(
-                place, mix_grad[part * lanes : (part + 1) * lanes, :]
+                sender_place_hot[:, block * lanes : (block + 1) * lanes],
+                mix_grad[part * lanes : (part + 1) * lanes, :],
             )
-        return carry
-
-    lax.fori_loop(0, turns, backward, 0)
     send(table_grad.at[0:nodes, :], own_grad, last_sems.at[1])
     first = reach
     for part in (to_lon, to_inner, to_outer):
@@ -350,8 +344,8 @@
     own_grad,
     from_inner,
     from_outer,
-    from_left,
-    from_right,
+    from_close,
+    from_far,
     edge_sender,
     update_normed,
     update_scale,
@@ -372,8 +366,7 @@
     grads,
 ):
     nodes, width = state_part.shape
-    live = live_ref[0]
-    arrived = from_left[...].astype(f32) + from_right[...].astype(f32)
+    arrived = from_close[...].astype(f32) + from_far[...].astype(f32)
     copies = arrived.shape[0]
     arrived += from_inner[0:copies, :].astype(f32) + from_outer[0:copies, :].astype(f32)
     table_grad = own_grad[...] + dot(row_hot(export[...], nodes), arrived.astype(bf16))
@@ -387,12 +380,12 @@
     grads[width : 2 * width, :] = edge_grad[...].astype(f32)
     grads[2 * width :, :] = jnp.zeros_like(grads[2 * width :, :])
 
-    def turn(step, carry):
+    for step in range(receivers.shape[0] // blocks_per_turn):
+        here = pl.ds(step * turn_rows, turn_rows)
         received = [
-            lane_hot(live_row(receivers, step * blocks_per_turn + part, live), upstream.shape[0])
-            for part in range(blocks_per_turn)
+            lane_hot(jnp.where(block < live_ref[0], receivers[block : block + 1, :], -1), 256)
+            for block in range(step * blocks_per_turn, (step + 1) * blocks_per_turn)
         ]
-        here = pl.ds(pl.multiple_of(step * turn_rows, turn_rows), turn_rows)
         arriving = dot(jnp.concatenate(received, 0), upstream[...])
         product_grad = norm_back(
             normed_all[here, :].astype(f32), scale_all[here, 0:1], arriving
@@ -404,34 +397,34 @@
         grads[2 * width : 2 * width + variables, :] += cross_dot(
             inputs[here, :], pre_grad.astype(bf16)
         )
-        return carry
-
-    lax.fori_loop(0, receivers.shape[0] // blocks_per_turn, turn, 0)
-    core, near, far = place_ref[0], place_ref[1], place_ref[2]
-    piece = grads.shape[0] // 16
-    for block in range(16):
-        half, first, second = block // 4 % 2, block // 2 % 2, block % 2
-        bits = (first ^ near, second ^ far) if half == 0 else (first ^ far, second ^ near)
-        side = core ^ (1 - block // 8)
-        origin = (((side * 2 + half) * 2 + bits[0]) * 2 + bits[1]) * piece
-        rows = grads[pl.ds(pl.multiple_of(origin, 16), piece), :].astype(bf16)
-        target = given if block < 8 else kept
-        target[block % 8 * piece : (block % 8 + 1) * piece, :] = rows
+    arrange(place_ref, grads, given, kept)
+
+
+def origin(place_ref, side, turn, piece):
+    block = (place_ref[0] ^ side) * 4 + (place_ref[1 + side] ^ turn)
+    return pl.ds(pl.multiple_of(block * piece, piece), piece)
+
+
+def arrange(place_ref, grads, given, kept):
+    piece = grads.shape[0] // 8
+    for side, target in ((1, given), (0, kept)):
+        for turn in range(4):
+            rows = grads[origin(place_ref, side, turn, piece), :]
+            target[turn * piece : (turn + 1) * piece, :] = rows.astype(bf16)
+
+
+def order(place_ref, mine, other, grads):
+    piece = grads.shape[0] // 8
+    for side, source in ((0, mine), (1, other)):
+        for turn in range(4):
+            rows = source[turn * piece : (turn + 1) * piece, :].astype(f32)
+            grads[origin(place_ref, side, turn, piece), :] = rows
 
 
 def order_kernel(
     place_ref, mine, other, sender_grad, edge_grad, grid_grad, grads, last, sems
 ):
-    core, near, far = place_ref[0], place_ref[1], place_ref[2]
-    piece = grads.shape[0] // 16
-    for block in range(16):
-        half, first, second = block // 4 % 2, block // 2 % 2, block % 2
-        bits = (first ^ near, second ^ far) if half == 0 else (first ^ far, second ^ near)
-        side = core ^ (block // 8)
-        origin = (((side * 2 + half) * 2 + bits[0]) * 2 + bits[1]) * piece
-        source = mine if block < 8 else other
-        rows = source[block % 8 * piece : (block % 8 + 1) * piece, :].astype(f32)
-        grads[pl.ds(pl.multiple_of(origin, 16), piece), :] = rows
+    order(place_ref, mine, other, grads)
     width = sender_grad.shape[0]
     last[...] = grads[2 * width : 2 * width + last.shape[0], :]
     copies = (
@@ -448,23 +441,18 @@
 def call(kernel, operands, outs, scratch, scalars, mib):
     smem = pl.BlockSpec(memory_space=pltpu.SMEM)
     vmem = pl.BlockSpec(memory_space=pltpu.VMEM)
-    hbm = pl.BlockSpec(memory_space=pl.ANY)
+    free = pl.BlockSpec(memory_space=pl.ANY)
     return pl.pallas_call(
         kernel,
         out_shape=[jax.ShapeDtypeStruct(shape, dtype) for shape, dtype, _ in outs],
         in_specs=[smem] * scalars + [vmem] * (len(operands) - scalars),
-        out_specs=[hbm if kind else vmem for _, _, kind in outs],
+        out_specs=[free if kind else vmem for _, _, kind in outs],
         scratch_shapes=[pltpu.VMEM(*shape) if isinstance(shape, tuple) else shape for shape in scratch],
         compiler_params=pltpu.CompilerParams(vmem_limit_bytes=mib << 20),
         cost_estimate=pl.CostEstimate(flops=4 << 30, bytes_accessed=8 << 20, transcendentals=0),
     )(*operands)
 
 
-def shifted(x, step):
-    size = lax.axis_size("lon")
-    return lax.ppermute(x, "lon", [(i, (i + step) % size) for i in range(size)])
-
-
 def partner(x, axis, flip):
     return lax.ppermute(x, axis, [(i, i ^ flip) for i in range(lax.axis_size(axis))])
 
@@ -478,37 +466,58 @@
     return lax.ppermute(x, "lat", [(i, i + 1) for i in ends] + [(i + 1, i) for i in ends])
 
 
+def close(x):
+    return partner(x, "lon", 1)
+
+
+def far(x):
+    size = lax.axis_size("lon")
+    ends = range(1, size, 2)
+    return lax.ppermute(
+        x, "lon", [(i, (i + 1) % size) for i in ends] + [((i + 1) % size, i) for i in ends]
+    )
+
+
 def around(rows):
-    left, right = shifted(rows, 1), shifted(rows, -1)
-    above, below = inner(rows), outer(rows)
-    left, right, above, below = lax.optimization_barrier((left, right, above, below))
-    corners = jnp.concatenate([left, right], 0)
-    return left, right, above, inner(corners), below, outer(corners)
+    beside = close(rows), far(rows)
+    column = jnp.concatenate((rows,) + beside, 0)
+    return beside + (inner(column), outer(column))
 
 
 def add(left, right):
     return (left.astype(f32) + right.astype(f32)).astype(bf16)
 
 
-def half_chain(values, flips):
-    one, two = flips
-    for flip in flips:
-        half = values.shape[0] // 2
-        values = add(values[:half], partner(values[half:], "lat", 2 * flip))
-    for scale in (1, 4):
-        for flip in flips:
-            values = add(values, partner(values, "lon", scale * flip))
-    for flip in flips[::-1]:
-        values = jnp.concatenate([values, partner(values, "lat", 2 * flip)], 0)
-    return values
+flips = {"x1": 32, "x3": 96, "y1": 4, "y3": 12, "z1": 1, "z3": 3}
+stages = (
+    (("x1", "y1"), ("x3", "y3")),
+    (("z1", "x3"), ("z3", "x1")),
+    (("y3", "z3"), ("y1", "z1")),
+)
+
+
+def met(x, stage, turn):
+    pairs = []
+    for device in range(lax.axis_size("lat") * lax.axis_size("lon")):
+        first, second = stages[stage][device // 16 % 2]
+        flip = (turn & 1) * flips[first] ^ (turn >> 1) * flips[second]
+        pairs.append((device, device ^ flip))
+    return lax.ppermute(x, ("lat", "lon"), pairs)
+
+
+def added(own, one, two, three):
+    pair = own.astype(f32) + one.astype(f32)
+    return (pair + (two.astype(f32) + three.astype(f32))).astype(bf16)
 
 
 def summed(given, kept):
     values = add(kept, inner(given))
-    half = values.shape[0] // 2
-    values = jnp.concatenate(
-        [half_chain(values[:half], (1, 3)), half_chain(values[half:], (3, 1))], 0
-    )
+    piece = values.shape[0] // 4
+    own, *others = [values[turn * piece : (turn + 1) * piece] for turn in range(4)]
+    values = added(own, *[met(part, 0, turn) for turn, part in zip((1, 2, 3), others)])
+    for stage in (1, 2):
+        values = added(values, *[met(values, stage, turn) for turn in (1, 2, 3)])
+    values = jnp.concatenate([values] + [met(values, 0, turn) for turn in (1, 2, 3)], 0)
     return values, inner(values)
 
 
@@ -542,8 +551,19 @@
     nodes, width = mesh_init.shape
     copies = mesh_export.shape[0]
     edges = encode_senders.shape[0] * encode_senders.shape[1]
-    index = lax.axis_index("lat")
-    place = jnp.stack([index & 1, (index >> 1 ^ index >> 2) & 1, index >> 2 & 1]).astype(jnp.int32)
+    core, chip, row = [
+        part.astype(jnp.int32)
+        for part in (
+            lax.axis_index("lat") & 1,
+            lax.axis_index("lat") >> 1,
+            lax.axis_index("lon") >> 2,
+        )
+    ]
+    odd = lax.axis_index("lon").astype(jnp.int32) & 1
+    plain = (chip & 1 ^ chip >> 1) | (row & 1 ^ row >> 1) << 1
+    wrapped = chip >> 1 | row >> 1 << 1
+    first, second = jnp.where(core == 0, plain, wrapped), jnp.where(core == 0, wrapped, plain)
+    place = jnp.stack([core, first, second, odd])
     select = (grid_export[:, None] == jnp.arange(grid_count)[None, :]).astype(bf16)
     grid_near = around(dot(select, grid_in).astype(bf16))
     export = mesh_export[None]
@@ -571,23 +591,44 @@
             encode_senders,
             encode_receivers,
             export,
+            encode_gain,
+            receiver_weight,
             grid_weight,
             sender_weight,
-            receiver_weight,
             message_weight,
             update_weight,
-            encode_gain,
         ),
         [((nodes, width), bf16, 0), ((copies, width), bf16, 0)] + [each + (1,) for each in saved],
         [
             ((grid_count + 8 * lanes + grid_count - lanes, variables), bf16),
-            ((256, width), bf16),
             ((nodes, width), f32),
         ]
         + saved
-        + [pltpu.SemaphoreType.DMA((6, turns)), pltpu.SemaphoreType.DMA((2,))],
+        + [
+            ((256, width), bf16),
+            ((edges, grid_count), bf16),
+            ((edges, 256), bf16),
+            ((nodes, edges), bf16),
+            pltpu.SemaphoreType.DMA((6, turns)),
+            pltpu.SemaphoreType.DMA((2,)),
+        ],
         3,
-        20,
+        44,
+    )
+    prepared = [
+        ((256, width), bf16),
+        ((edges, 256), bf16),
+        ((edges, 256), bf16),
+        ((nodes, edges), bf16),
+        ((nodes, edges), bf16),
+    ]
+    terms, process_send, process_receive, process_place, process_sender_place = call(
+        prepare_kernel,
+        (process_live, process_senders, process_receivers, state, edge_receiver),
+        [each + (1,) for each in prepared],
+        prepared + [pltpu.SemaphoreType.DMA((5,))],
+        1,
+        16,
     )
     near = around(picked)
     (
@@ -602,15 +643,16 @@
     ) = call(
         process_kernel,
         (
-            process_live,
             place,
             process_slots,
             state,
             *near,
-            process_senders,
-            process_receivers,
+            terms,
+            process_send,
+            process_receive,
+            process_place,
+            process_sender_place,
             edge_sender,
-            edge_receiver,
             edge_message,
             node_update,
             node_gain,
@@ -628,7 +670,6 @@
         ],
         [
             ((256 + 8 * copies + 128, width), bf16),
-            ((256, width), bf16),
             ((nodes, width), f32),
             ((edges, width), f32),
             ((edges, width), f32),
@@ -642,11 +683,11 @@
             pltpu.SemaphoreType.DMA((2, turns)),
             pltpu.SemaphoreType.DMA((2,)),
         ],
-        3,
+        2,
         26,
     )
     from_inner, from_outer = inner(to_inner), outer(to_outer)
-    to_left, to_right = [
+    to_close, to_far = [
         (
             to_lon[side * copies : (side + 1) * copies].astype(f32)
             + from_inner[(side + 1) * copies : (side + 2) * copies].astype(f32)
@@ -654,7 +695,7 @@
         ).astype(bf16)
         for side in (0, 1)
     ]
-    from_right, from_left = shifted(to_left, -1), shifted(to_right, 1)
+    from_close, from_far = close(to_close), far(to_far)
     state_part = cotangent.astype(f32) + back_dot(receiver_grad, edge_receiver)
     edge_grad = cross_dot(sender_rows, mix_grad).astype(bf16)
     given, kept = call(
@@ -668,8 +709,8 @@
             own_grad,
             from_inner,
             from_outer,
-            from_left,
-            from_right,
+            from_close,
+            from_far,
             edge_sender,
             update[0],
             update[1],

time: 155 us -> 125 us (0.81)
  waiting for transfers between devices: 68.1 us -> 44.7 us
  starting transfers between devices: 52.7 us -> 48.4 us
    ppermute x23 -> x8, waiting for transfers between devices: 40.3 us -> 6.25 us  [partner(): lax.ppermute(x, axis, [(i, i ^ flip) for i in range(lax.axis_size(axis))])]
    ppermute x6 -> x15, starting transfers between devices: 9.34 us -> 30.8 us  [the longest x12 17.4 us: met(): return lax.ppermute(x, ('lat', 'lon'), pairs)]
    ppermute x23 -> x8, starting transfers between devices: 22.8 us -> 4.51 us  [partner(): lax.ppermute(x, axis, [(i, i ^ flip) for i in range(lax.axis_size(axis))])]
    ppermute x6 -> x15, waiting for transfers between devices: 17.7 us -> 27.8 us  [the longest x12 18.3 us: met(): return lax.ppermute(x, ('lat', 'lon'), pairs)]
    ppermute x5 -> x3, starting transfers between devices: 20.6 us -> 13.2 us  [outer(): lax.ppermute(x, 'lat', [(i, i + 1) for i in ends] + [(i + 1, i) for i in...]
    unnamed x50 -> x43, local copies, waits for them, and re-layouts: 5.13 us -> 4.2 us
    pallas_call x4 -> x5, Pallas kernels: 22.6 us -> 21.8 us  [call(): pl.pallas_call(kernel, out_shape=[jax.ShapeDtypeStruct(shape, dtype) for...]
    ppermute x5 -> x3, waiting for transfers between devices: 10 us -> 10.6 us  [outer(): lax.ppermute(x, 'lat', [(i, i + 1) for i in ends] + [(i + 1, i) for i in...]
  transfers between devices with their start and end apart: 34 -> 26, of which waited for: 26 -> 20; matrix products, arithmetic and copies ran while one was open for 2% -> 2% of each run, Pallas kernels for 0% -> 1%
where the time goes in v3:
time: 125 us
  starting transfers between devices  48.4 us (39%)
  waiting for transfers between devices  44.7 us (36%)
  Pallas kernels  21.8 us (17%)
  local copies, waits for them, and re-layouts  4.24 us (3%)
  between operations  2.58 us (2%)
  matrix products  2.31 us (2%)
    pallas_call x5, Pallas kernels, call(): pl.pallas_call(kernel, out_shape=[jax.ShapeDtypeStruct(shape, dtype) for...  21.8 us
    ppermute x12, waiting for transfers between devices, met(): return lax.ppermute(x, ('lat', 'lon'), pairs)  18.3 us
    ppermute x12, starting transfers between devices, met(): return lax.ppermute(x, ('lat', 'lon'), pairs)  17.4 us
    ppermute x3, starting transfers between devices, far(): lax.ppermute(x, 'lon', [(i, (i + 1) % size) for i in ends] + [((i + 1) %...  13.4 us
    ppermute x3, starting transfers between devices, outer(): lax.ppermute(x, 'lat', [(i, i + 1) for i in ends] + [(i + 1, i) for i in...  13.2 us
    ppermute x3, waiting for transfers between devices, outer(): lax.ppermute(x, 'lat', [(i, i + 1) for i in ends] + [(i + 1, i) for i in...  10.6 us
    ppermute x3, waiting for transfers between devices, far(): lax.ppermute(x, 'lon', [(i, (i + 1) % size) for i in ends] + [((i + 1) %...  9.46 us
    ppermute x8, waiting for transfers between devices, partner(): lax.ppermute(x, axis, [(i, i ^ flip) for i in range(lax.axis_size(axis))])  6.25 us
  transfers between devices with their start and end apart: 26, of which 20 were waited for; matrix products, arithmetic and copies ran while one was open for 2% of the time, Pallas kernels for 1%

profile of v3, /device:TPU:1, one launch (start us, length us, event | category | flops | bytes accessed | tf_op | source)
XLA Modules:
  0.0 124.7 jit_solution(17720187288163382738)
XLA Ops:
  2.0 7.1 %collective-permute-start.1 = (bf16[128,227]{1,0:T(8,128)(2,1)S(1)}, bf16[128,227]{1,0:T(8,128)(2,1)S(1)}, u32[]{:S(2)}, u32[]{:S(2)}) collective-permute-start(bf16[128,227]{1,0:T(8,128)(2,1)S(1)} %convolution_convert_fusion.1), channel_id=1, source_target_pairs={{1,2},{3,4},{5,6},{7,8},{9,10},{11,12},{13,14},{15,0},{2,1},{4,3},... | collective-permute-start | bytes 174344 | tf_op jit(solution)/shard_map/ppermute | solution.py:476
  12.2 5.1 %collective-permute-start.3 = (bf16[384,227]{1,0:T(8,128)(2,1)S(1)}, bf16[384,227]{1,0:T(8,128)(2,1)S(1)}, u32[]{:S(2)}, u32[]{:S(2)}) collective-permute-start(bf16[384,227]{1,0:T(8,128)(2,1)S(1)} %pad_maximum_fusion.1), channel_id=1, source_target_pairs={{16,32},{48,64},{80,96},{32,16},{64,48},{96,80},{17,33},{49,65},{8... | collective-permute-start | bytes 523016 | tf_op jit(solution)/shard_map/ppermute | solution.py:466
  23.8 6.3 %shard_map.255 = (bf16[160,512]{1,0:T(8,128)(2,1)S(1)}, bf16[128,512]{1,0:T(8,128)(2,1)S(1)}, bf16[1024,227]{1,0:T(8,128)(2,1)S(1)}, bf16[1024,512]{1,0:T(8,128)...) custom-call(s32[1]{0:T(128)S(6)} %copy.33.live_ref, ...), custom_call_target="tpu_custom_call" | custom-call | flops 4294967296 | bytes 8388608 | tf_op jit(solution)/shard_map/pallas_call | solution.py:445
  30.9 3.1 %collective-permute-start.5 = (bf16[128,512]{1,0:T(8,128)(2,1)S(1)}, bf16[128,512]{1,0:T(8,128)(2,1)S(1)}, u32[]{:S(2)}, u32[]{:S(2)}) collective-permute-start(bf16[128,512]{1,0:T(8,128)(2,1)S(1)} %get-tuple-element.33), channel_id=1, source_target_pairs={{1,2},{3,4},{5,6},{7,8},{9,10},{11,12},{13,14},{15,0},{2,1},{4,3},... | collective-permute-start | bytes 393224 | tf_op jit(solution)/shard_map/ppermute | solution.py:476
  35.0 4.0 %collective-permute-done.5.near_far = bf16[128,512]{1,0:T(8,128)(2,1)S(1)} collective-permute-done((bf16[128,512]{1,0:T(8,128)(2,1)S(1)}, bf16[128,512]{1,0:T(8,128)(2,1)S(1)}, u32[]{:S(2)}, u32[]{:S(2)}) %collective-permute-start.5) | collective-permute-done | bytes 131104 | tf_op jit(solution)/shard_map/ppermute | solution.py:476
  39.1 4.4 %collective-permute-start.7 = (bf16[384,512]{1,0:T(8,128)(2,1)S(1)}, bf16[384,512]{1,0:T(8,128)(2,1)S(1)}, u32[]{:S(2)}, u32[]{:S(2)}) collective-permute-start(bf16[384,512]{1,0:T(8,128)(2,1)S(1)} %constant_dynamic-update-slice_fusion), channel_id=1, source_target_pairs={{16,32},{48,64},{80,96},{32,16},{64,48},{96,80},{17,33},{49,65},{8... | collective-permute-start | bytes 1179656 | tf_op jit(solution)/shard_map/ppermute | solution.py:466
  44.7 4.2 %collective-permute-done.7.near_outer = bf16[384,512]{1,0:T(8,128)(2,1)S(1)} collective-permute-done((bf16[384,512]{1,0:T(8,128)(2,1)S(1)}, bf16[384,512]{1,0:T(8,128)(2,1)S(1)}, u32[]{:S(2)}, u32[]{:S(2)}) %collective-permute-start.7) | collective-permute-done | bytes 393248 | tf_op jit(solution)/shard_map/ppermute | solution.py:466
  49.0 7.7 %shard_map.257 = (bf16[160,512]{1,0:T(8,128)(2,1)}, f32[160,512]{1,0:T(8,128)S(1)}, bf16[256,512]{1,0:T(8,128)(2,1)S(1)}, bf16[384,512]{1,0:T(8,128)(2,1)S(1)}, ...) custom-call(s32[4]{0:T(128)S(1)} %pad_add_fusion.place_ref, ...), custom_call_target="tpu_custom_call" | custom-call | flops 4294967296 | bytes 8388608 | tf_op jit(solution)/shard_map/pallas_call | solution.py:445
  56.7 3.6 %collective-permute-start.9 = (bf16[384,512]{1,0:T(8,128)(2,1)S(1)}, bf16[384,512]{1,0:T(8,128)(2,1)S(1)}, u32[]{:S(2)}, u32[]{:S(2)}) collective-permute-start(bf16[384,512]{1,0:T(8,128)(2,1)S(1)} %get-tuple-element.43), channel_id=1, source_target_pairs={{16,32},{48,64},{80,96},{32,16},{64,48},{96,80},{17,33},{49,65},{8... | collective-permute-start | bytes 1179656 | tf_op jit(solution)/shard_map/ppermute | solution.py:466
  61.1 5.0 %collective-permute-done.9.from_outer = bf16[384,512]{1,0:T(8,128)(2,1)S(1)} collective-permute-done((bf16[384,512]{1,0:T(8,128)(2,1)S(1)}, bf16[384,512]{1,0:T(8,128)(2,1)S(1)}, u32[]{:S(2)}, u32[]{:S(2)}) %collective-permute-start.9) | collective-permute-done | bytes 393248 | tf_op jit(solution)/shard_map/ppermute | solution.py:466
  66.2 3.1 %collective-permute-start.11 = (bf16[128,512]{1,0:T(8,128)(2,1)S(1)}, bf16[128,512]{1,0:T(8,128)(2,1)S(1)}, u32[]{:S(2)}, u32[]{:S(2)}) collective-permute-start(bf16[128,512]{1,0:T(8,128)(2,1)S(1)} %get-tuple-element.60), channel_id=1, source_target_pairs={{1,2},{3,4},{5,6},{7,8},{9,10},{11,12},{13,14},{15,0},{2,1},{4,3},... | collective-permute-start | bytes 393224 | tf_op jit(solution)/shard_map/ppermute | solution.py:476
  69.7 3.8 %collective-permute-done.11.from_far = bf16[128,512]{1,0:T(8,128)(2,1)S(1)} collective-permute-done((bf16[128,512]{1,0:T(8,128)(2,1)S(1)}, bf16[128,512]{1,0:T(8,128)(2,1)S(1)}, u32[]{:S(2)}, u32[]{:S(2)}) %collective-permute-start.11) | collective-permute-done | bytes 131104 | tf_op jit(solution)/shard_map/ppermute | solution.py:476
  73.5 4.7 %shard_map.258 = (bf16[640,512]{1,0:T(8,128)(2,1)S(1)}, bf16[640,512]{1,0:T(8,128)(2,1)S(1)}) custom-call(s32[1]{0:T(128)S(6)} %copy.33.live_ref, s32[4]{0:T(128)S(1)} %pad_add_fusion.place_ref, s32[8,128]{1,0:T(8,128)S(1)} %copy-done.14, s32[1,128]{1,0:T(1,128)S(1)} %bitcast.16, f32[160,512]{1,0:T(8,128)S(1)} %convolution_add_fusion.state_part, ...), custom_call_target="tpu_custom_call" | custom-call | flops 4294967296 | bytes 8388608 | tf_op jit(solution)/shard_map/pallas_call | solution.py:445
  80.6 3.1 %collective-permute-start.13 = (bf16[160,512]{1,0:T(8,128)(2,1)S(1)}, bf16[160,512]{1,0:T(8,128)(2,1)S(1)}, u32[]{:S(2)}, u32[]{:S(2)}) collective-permute-start(bf16[160,512]{1,0:T(8,128)(2,1)S(1)} %get-tuple-element.62), channel_id=1, source_target_pairs={{0,32},{1,33},{2,34},{3,35},{4,36},{5,37},{6,38},{7,39},{8,40},{9,... | collective-permute-start | bytes 491528 | tf_op jit(solution)/shard_map/ppermute | solution.py:505
  83.8 2.5 %collective-permute-start.14 = (bf16[160,512]{1,0:T(8,128)(2,1)S(1)}, bf16[160,512]{1,0:T(8,128)(2,1)S(1)}, u32[]{:S(2)}, u32[]{:S(2)}) collective-permute-start(bf16[160,512]{1,0:T(8,128)(2,1)S(1)} %get-tuple-element.64), channel_id=1, source_target_pairs={{0,4},{1,5},{2,6},{3,7},{4,0},{5,1},{6,2},{7,3},{8,12},{9,13},{10,... | collective-permute-start | bytes 491528 | tf_op jit(solution)/shard_map/ppermute | solution.py:505
  86.5 4.8 %collective-permute-done.15 = bf16[160,512]{1,0:T(8,128)(2,1)S(1)} collective-permute-done((bf16[160,512]{1,0:T(8,128)(2,1)S(1)}, bf16[160,512]{1,0:T(8,128)(2,1)S(1)}, u32[]{:S(2)}, u32[]{:S(2)}) %collective-permute-start.15) | collective-permute-done | bytes 163872 | tf_op jit(solution)/shard_map/ppermute | solution.py:505
  91.3 3.2 %collective-permute-start.18 = (bf16[160,512]{1,0:T(8,128)(2,1)S(1)}, bf16[160,512]{1,0:T(8,128)(2,1)S(1)}, u32[]{:S(2)}, u32[]{:S(2)}) collective-permute-start(bf16[160,512]{1,0:T(8,128)(2,1)S(1)} %add_convert_fusion.3), channel_id=1, source_target_pairs={{0,97},{1,96},{2,99},{3,98},{4,101},{5,100},{6,103},{7,102},{8,105... | collective-permute-start | bytes 491528 | tf_op jit(solution)/shard_map/ppermute | solution.py:505
  95.3 2.7 %collective-permute-done.18 = bf16[160,512]{1,0:T(8,128)(2,1)S(1)} collective-permute-done((bf16[160,512]{1,0:T(8,128)(2,1)S(1)}, bf16[160,512]{1,0:T(8,128)(2,1)S(1)}, u32[]{:S(2)}, u32[]{:S(2)}) %collective-permute-start.18) | collective-permute-done | bytes 163872 | tf_op jit(solution)/shard_map/ppermute | solution.py:505
  100.2 2.5 %collective-permute-start.19 = (bf16[160,512]{1,0:T(8,128)(2,1)S(1)}, bf16[160,512]{1,0:T(8,128)(2,1)S(1)}, u32[]{:S(2)}, u32[]{:S(2)}) collective-permute-start(bf16[160,512]{1,0:T(8,128)(2,1)S(1)} %add_convert_fusion.2), channel_id=1, source_target_pairs={{0,12},{1,13},{2,14},{3,15},{4,8},{5,9},{6,10},{7,11},{8,4},{9,5},... | collective-permute-start | bytes 491528 | tf_op jit(solution)/shard_map/ppermute | solution.py:505
  102.7 2.5 %collective-permute-done.21 = bf16[160,512]{1,0:T(8,128)(2,1)S(1)} collective-permute-done((bf16[160,512]{1,0:T(8,128)(2,1)S(1)}, bf16[160,512]{1,0:T(8,128)(2,1)S(1)}, u32[]{:S(2)}, u32[]{:S(2)}) %collective-permute-start.21) | collective-permute-done | bytes 163872 | tf_op jit(solution)/shard_map/ppermute | solution.py:505
  106.2 3.4 %collective-permute-start.24 = (bf16[160,512]{1,0:T(8,128)(2,1)S(1)}, bf16[160,512]{1,0:T(8,128)(2,1)S(1)}, u32[]{:S(2)}, u32[]{:S(2)}) collective-permute-start(bf16[160,512]{1,0:T(8,128)(2,1)S(1)} %add_convert_fusion.1), channel_id=1, source_target_pairs={{0,36},{1,37},{2,38},{3,39},{4,32},{5,33},{6,34},{7,35},{8,44},{9,... | collective-permute-start | bytes 491528 | tf_op jit(solution)/shard_map/ppermute | solution.py:505
  111.4 2.5 %collective-permute-done.24 = bf16[160,512]{1,0:T(8,128)(2,1)S(1)} collective-permute-done((bf16[160,512]{1,0:T(8,128)(2,1)S(1)}, bf16[160,512]{1,0:T(8,128)(2,1)S(1)}, u32[]{:S(2)}, u32[]{:S(2)}) %collective-permute-start.24) | collective-permute-done | bytes 163872 | tf_op jit(solution)/shard_map/ppermute | solution.py:505
  116.7 3.9 %collective-permute-start.25 = (bf16[640,512]{1,0:T(8,128)(2,1)S(1)}, bf16[640,512]{1,0:T(8,128)(2,1)S(1)}, u32[]{:S(2)}, u32[]{:S(2)}) collective-permute-start(bf16[640,512]{1,0:T(8,128)(2,1)S(1)} %pad_maximum_fusion.mine), channel_id=1, source_target_pairs={{0,16},{16,0},{32,48},{48,32},{64,80},{80,64},{96,112},{112,96},{1... | collective-permute-start | bytes 1966088 | tf_op jit(solution)/shard_map/ppermute | solution.py:457
  122.3 2.2 %shard_map.259 = (f32[512,512]{1,0:T(8,128)}, f32[512,512]{1,0:T(8,128)}, f32[227,512]{1,0:T(8,128)}) custom-call(s32[4]{0:T(128)S(1)} %pad_add_fusion.place_ref, bf16[640,512]{1,0:T(8,128)(2,1)S(1)} %pad_maximum_fusion.mine, bf16[640,512]{1,0:T(8,128)(2,1)S(1)} %collective-permute-done.25.other), custom_call_target="tpu_custom_call" | custom-call | flops 4294967296 | bytes 8388608 | tf_op jit(solution)/shard_map/pallas_call | solution.py:445
  (89 shorter events, 26.5 us)
Async XLA Ops:
  2.0 8.8 %collective-permute-start.1 = (bf16[128,227]{1,0:T(8,128)(2,1)S(1)}, bf16[128,227]{1,0:T(8,128)(2,1)S(1)}, u32[]{:S(2)}, u32[]{:S(2)}) collective-permute-start(bf16[128,227]{1,0:T(8,128)(2,1)S(1)} %convolution_convert_fusion.1), channel_id=1, source_target_pairs={{1,2},{3,4},{5,6},{7,8},{9,10},{11,12},{13,14},{15,0},{2,1},{4,3},... | collective-permute-start | bytes 174344 | tf_op jit(solution)/shard_map/ppermute | solution.py:476
  12.2 8.5 %collective-permute-start.3 = (bf16[384,227]{1,0:T(8,128)(2,1)S(1)}, bf16[384,227]{1,0:T(8,128)(2,1)S(1)}, u32[]{:S(2)}, u32[]{:S(2)}) collective-permute-start(bf16[384,227]{1,0:T(8,128)(2,1)S(1)} %pad_maximum_fusion.1), channel_id=1, source_target_pairs={{16,32},{48,64},{80,96},{32,16},{64,48},{96,80},{17,33},{49,65},{8... | collective-permute-start | bytes 523016 | tf_op jit(solution)/shard_map/ppermute | solution.py:466
  17.4 3.3 %collective-permute-start.2 = (bf16[384,227]{1,0:T(8,128)(2,1)S(1)}, bf16[384,227]{1,0:T(8,128)(2,1)S(1)}, u32[]{:S(2)}, u32[]{:S(2)}) collective-permute-start(bf16[384,227]{1,0:T(8,128)(2,1)S(1)} %pad_maximum_fusion.1), channel_id=1, source_target_pairs={{0,16},{16,0},{32,48},{48,32},{64,80},{80,64},{96,112},{112,96},{1... | collective-permute-start | bytes 523016 | tf_op jit(solution)/shard_map/ppermute | solution.py:457
  30.1 4.8 %collective-permute-start.4 = (bf16[128,512]{1,0:T(8,128)(2,1)S(1)}, bf16[128,512]{1,0:T(8,128)(2,1)S(1)}, u32[]{:S(2)}, u32[]{:S(2)}) collective-permute-start(bf16[128,512]{1,0:T(8,128)(2,1)S(1)} %get-tuple-element.33), channel_id=1, source_target_pairs={{0,1},{1,0},{2,3},{3,2},{4,5},{5,4},{6,7},{7,6},{8,9},{9,8},{10,11... | collective-permute-start | bytes 393224 | tf_op jit(solution)/shard_map/ppermute | solution.py:457
  30.9 8.2 %collective-permute-start.5 = (bf16[128,512]{1,0:T(8,128)(2,1)S(1)}, bf16[128,512]{1,0:T(8,128)(2,1)S(1)}, u32[]{:S(2)}, u32[]{:S(2)}) collective-permute-start(bf16[128,512]{1,0:T(8,128)(2,1)S(1)} %get-tuple-element.33), channel_id=1, source_target_pairs={{1,2},{3,4},{5,6},{7,8},{9,10},{11,12},{13,14},{15,0},{2,1},{4,3},... | collective-permute-start | bytes 393224 | tf_op jit(solution)/shard_map/ppermute | solution.py:476
  39.1 9.9 %collective-permute-start.7 = (bf16[384,512]{1,0:T(8,128)(2,1)S(1)}, bf16[384,512]{1,0:T(8,128)(2,1)S(1)}, u32[]{:S(2)}, u32[]{:S(2)}) collective-permute-start(bf16[384,512]{1,0:T(8,128)(2,1)S(1)} %constant_dynamic-update-slice_fusion), channel_id=1, source_target_pairs={{16,32},{48,64},{80,96},{32,16},{64,48},{96,80},{17,33},{49,65},{8... | collective-permute-start | bytes 1179656 | tf_op jit(solution)/shard_map/ppermute | solution.py:466
  43.5 5.4 %collective-permute-start.6 = (bf16[384,512]{1,0:T(8,128)(2,1)S(1)}, bf16[384,512]{1,0:T(8,128)(2,1)S(1)}, u32[]{:S(2)}, u32[]{:S(2)}) collective-permute-start(bf16[384,512]{1,0:T(8,128)(2,1)S(1)} %constant_dynamic-update-slice_fusion), channel_id=1, source_target_pairs={{0,16},{16,0},{32,48},{48,32},{64,80},{80,64},{96,112},{112,96},{1... | collective-permute-start | bytes 1179656 | tf_op jit(solution)/shard_map/ppermute | solution.py:457
  56.7 4.5 %collective-permute-start.8 = (bf16[384,512]{1,0:T(8,128)(2,1)S(1)}, bf16[384,512]{1,0:T(8,128)(2,1)S(1)}, u32[]{:S(2)}, u32[]{:S(2)}) collective-permute-start(bf16[384,512]{1,0:T(8,128)(2,1)S(1)} %get-tuple-element.42), channel_id=1, source_target_pairs={{0,16},{16,0},{32,48},{48,32},{64,80},{80,64},{96,112},{112,96},{1... | collective-permute-start | bytes 1179656 | tf_op jit(solution)/shard_map/ppermute | solution.py:457
  56.7 9.4 %collective-permute-start.9 = (bf16[384,512]{1,0:T(8,128)(2,1)S(1)}, bf16[384,512]{1,0:T(8,128)(2,1)S(1)}, u32[]{:S(2)}, u32[]{:S(2)}) collective-permute-start(bf16[384,512]{1,0:T(8,128)(2,1)S(1)} %get-tuple-element.43), channel_id=1, source_target_pairs={{16,32},{48,64},{80,96},{32,16},{64,48},{96,80},{17,33},{49,65},{8... | collective-permute-start | bytes 1179656 | tf_op jit(solution)/shard_map/ppermute | solution.py:466
  66.2 7.2 %collective-permute-start.11 = (bf16[128,512]{1,0:T(8,128)(2,1)S(1)}, bf16[128,512]{1,0:T(8,128)(2,1)S(1)}, u32[]{:S(2)}, u32[]{:S(2)}) collective-permute-start(bf16[128,512]{1,0:T(8,128)(2,1)S(1)} %get-tuple-element.60), channel_id=1, source_target_pairs={{1,2},{3,4},{5,6},{7,8},{9,10},{11,12},{13,14},{15,0},{2,1},{4,3},... | collective-permute-start | bytes 393224 | tf_op jit(solution)/shard_map/ppermute | solution.py:476
  69.4 4.1 %collective-permute-start.10 = (bf16[128,512]{1,0:T(8,128)(2,1)S(1)}, bf16[128,512]{1,0:T(8,128)(2,1)S(1)}, u32[]{:S(2)}, u32[]{:S(2)}) collective-permute-start(bf16[128,512]{1,0:T(8,128)(2,1)S(1)} %get-tuple-element.61), channel_id=1, source_target_pairs={{0,1},{1,0},{2,3},{3,2},{4,5},{5,4},{6,7},{7,6},{8,9},{9,8},{10,11... | collective-permute-start | bytes 393224 | tf_op jit(solution)/shard_map/ppermute | solution.py:457
  80.6 5.9 %collective-permute-start.13 = (bf16[160,512]{1,0:T(8,128)(2,1)S(1)}, bf16[160,512]{1,0:T(8,128)(2,1)S(1)}, u32[]{:S(2)}, u32[]{:S(2)}) collective-permute-start(bf16[160,512]{1,0:T(8,128)(2,1)S(1)} %get-tuple-element.62), channel_id=1, source_target_pairs={{0,32},{1,33},{2,34},{3,35},{4,36},{5,37},{6,38},{7,39},{8,40},{9,... | collective-permute-start | bytes 491528 | tf_op jit(solution)/shard_map/ppermute | solution.py:505
  83.8 7.5 %collective-permute-start.15 = (bf16[160,512]{1,0:T(8,128)(2,1)S(1)}, bf16[160,512]{1,0:T(8,128)(2,1)S(1)}, u32[]{:S(2)}, u32[]{:S(2)}) collective-permute-start(bf16[160,512]{1,0:T(8,128)(2,1)S(1)} %get-tuple-element.63), channel_id=1, source_target_pairs={{0,36},{1,37},{2,38},{3,39},{4,32},{5,33},{6,34},{7,35},{8,44},{9,... | collective-permute-start | bytes 491528 | tf_op jit(solution)/shard_map/ppermute | solution.py:505
  83.8 7.5 %collective-permute-start.14 = (bf16[160,512]{1,0:T(8,128)(2,1)S(1)}, bf16[160,512]{1,0:T(8,128)(2,1)S(1)}, u32[]{:S(2)}, u32[]{:S(2)}) collective-permute-start(bf16[160,512]{1,0:T(8,128)(2,1)S(1)} %get-tuple-element.64), channel_id=1, source_target_pairs={{0,4},{1,5},{2,6},{3,7},{4,0},{5,1},{6,2},{7,3},{8,12},{9,13},{10,... | collective-permute-start | bytes 491528 | tf_op jit(solution)/shard_map/ppermute | solution.py:505
  91.3 6.7 %collective-permute-start.18 = (bf16[160,512]{1,0:T(8,128)(2,1)S(1)}, bf16[160,512]{1,0:T(8,128)(2,1)S(1)}, u32[]{:S(2)}, u32[]{:S(2)}) collective-permute-start(bf16[160,512]{1,0:T(8,128)(2,1)S(1)} %add_convert_fusion.3), channel_id=1, source_target_pairs={{0,97},{1,96},{2,99},{3,98},{4,101},{5,100},{6,103},{7,102},{8,105... | collective-permute-start | bytes 491528 | tf_op jit(solution)/shard_map/ppermute | solution.py:505
  94.5 4.6 %collective-permute-start.17 = (bf16[160,512]{1,0:T(8,128)(2,1)S(1)}, bf16[160,512]{1,0:T(8,128)(2,1)S(1)}, u32[]{:S(2)}, u32[]{:S(2)}) collective-permute-start(bf16[160,512]{1,0:T(8,128)(2,1)S(1)} %add_convert_fusion.3), channel_id=1, source_target_pairs={{0,96},{1,97},{2,98},{3,99},{4,100},{5,101},{6,102},{7,103},{8,104... | collective-permute-start | bytes 491528 | tf_op jit(solution)/shard_map/ppermute | solution.py:505
  94.6 5.4 %collective-permute-start.16 = (bf16[160,512]{1,0:T(8,128)(2,1)S(1)}, bf16[160,512]{1,0:T(8,128)(2,1)S(1)}, u32[]{:S(2)}, u32[]{:S(2)}) collective-permute-start(bf16[160,512]{1,0:T(8,128)(2,1)S(1)} %add_convert_fusion.3), channel_id=1, source_target_pairs={{0,1},{1,0},{2,3},{3,2},{4,5},{5,4},{6,7},{7,6},{8,9},{9,8},{10,11... | collective-permute-start | bytes 491528 | tf_op jit(solution)/shard_map/ppermute | solution.py:505
  100.0 5.3 %collective-permute-start.21 = (bf16[160,512]{1,0:T(8,128)(2,1)S(1)}, bf16[160,512]{1,0:T(8,128)(2,1)S(1)}, u32[]{:S(2)}, u32[]{:S(2)}) collective-permute-start(bf16[160,512]{1,0:T(8,128)(2,1)S(1)} %add_convert_fusion.2), channel_id=1, source_target_pairs={{0,15},{1,14},{2,13},{3,12},{4,11},{5,10},{6,9},{7,8},{8,7},{9,6},... | collective-permute-start | bytes 491528 | tf_op jit(solution)/shard_map/ppermute | solution.py:505
  100.1 6.0 %collective-permute-start.20 = (bf16[160,512]{1,0:T(8,128)(2,1)S(1)}, bf16[160,512]{1,0:T(8,128)(2,1)S(1)}, u32[]{:S(2)}, u32[]{:S(2)}) collective-permute-start(bf16[160,512]{1,0:T(8,128)(2,1)S(1)} %add_convert_fusion.2), channel_id=1, source_target_pairs={{0,3},{1,2},{2,1},{3,0},{4,7},{5,6},{6,5},{7,4},{8,11},{9,10},{10,... | collective-permute-start | bytes 491528 | tf_op jit(solution)/shard_map/ppermute | solution.py:505
  100.2 5.9 %collective-permute-start.19 = (bf16[160,512]{1,0:T(8,128)(2,1)S(1)}, bf16[160,512]{1,0:T(8,128)(2,1)S(1)}, u32[]{:S(2)}, u32[]{:S(2)}) collective-permute-start(bf16[160,512]{1,0:T(8,128)(2,1)S(1)} %add_convert_fusion.2), channel_id=1, source_target_pairs={{0,12},{1,13},{2,14},{3,15},{4,8},{5,9},{6,10},{7,11},{8,4},{9,5},... | collective-permute-start | bytes 491528 | tf_op jit(solution)/shard_map/ppermute | solution.py:505
  106.2 7.6 %collective-permute-start.24 = (bf16[160,512]{1,0:T(8,128)(2,1)S(1)}, bf16[160,512]{1,0:T(8,128)(2,1)S(1)}, u32[]{:S(2)}, u32[]{:S(2)}) collective-permute-start(bf16[160,512]{1,0:T(8,128)(2,1)S(1)} %add_convert_fusion.1), channel_id=1, source_target_pairs={{0,36},{1,37},{2,38},{3,39},{4,32},{5,33},{6,34},{7,35},{8,44},{9,... | collective-permute-start | bytes 491528 | tf_op jit(solution)/shard_map/ppermute | solution.py:505
  109.6 5.9 %collective-permute-start.23 = (bf16[160,512]{1,0:T(8,128)(2,1)S(1)}, bf16[160,512]{1,0:T(8,128)(2,1)S(1)}, u32[]{:S(2)}, u32[]{:S(2)}) collective-permute-start(bf16[160,512]{1,0:T(8,128)(2,1)S(1)} %add_convert_fusion.1), channel_id=1, source_target_pairs={{0,4},{1,5},{2,6},{3,7},{4,0},{5,1},{6,2},{7,3},{8,12},{9,13},{10,... | collective-permute-start | bytes 491528 | tf_op jit(solution)/shard_map/ppermute | solution.py:505
  111.2 5.5 %collective-permute-start.22 = (bf16[160,512]{1,0:T(8,128)(2,1)S(1)}, bf16[160,512]{1,0:T(8,128)(2,1)S(1)}, u32[]{:S(2)}, u32[]{:S(2)}) collective-permute-start(bf16[160,512]{1,0:T(8,128)(2,1)S(1)} %add_convert_fusion.1), channel_id=1, source_target_pairs={{0,32},{1,33},{2,34},{3,35},{4,36},{5,37},{6,38},{7,39},{8,40},{9,... | collective-permute-start | bytes 491528 | tf_op jit(solution)/shard_map/ppermute | solution.py:505
  116.7 5.6 %collective-permute-start.25 = (bf16[640,512]{1,0:T(8,128)(2,1)S(1)}, bf16[640,512]{1,0:T(8,128)(2,1)S(1)}, u32[]{:S(2)}, u32[]{:S(2)}) collective-permute-start(bf16[640,512]{1,0:T(8,128)(2,1)S(1)} %pad_maximum_fusion.mine), channel_id=1, source_target_pairs={{0,16},{16,0},{32,48},{48,32},{64,80},{80,64},{96,112},{112,96},{1... | collective-permute-start | bytes 1966088 | tf_op jit(solution)/shard_map/ppermute | solution.py:457
  (22 other events, 259.5 us)

commit v4 on v3

v4 whole, which is shorter than its diff:
```python
import jax
import jax.numpy as jnp
from jax import lax
from jax.experimental import pallas as pl
from jax.experimental.pallas import tpu as pltpu
from jax.sharding import PartitionSpec as P

norm_epsilon = 1e-05
lanes = 128
f32 = jnp.float32
bf16 = jnp.bfloat16


def dot(left, right):
    return jnp.dot(left, right, preferred_element_type=f32)


def back_dot(left, weight):
    return lax.dot_general(left, weight, (((1,), (1,)), ((), ())), preferred_element_type=f32)


def cross_dot(left, right):
    return lax.dot_general(left, right, (((0,), (0,)), ((), ())), preferred_element_type=f32)


def sigmoid(values):
    return 0.5 * jnp.tanh(0.5 * values) + 0.5


def row_mean(values):
    return jnp.mean(values, axis=-1, keepdims=True)


def normalise(values):
    center = values - row_mean(values)
    scale = lax.rsqrt(row_mean(center * center) + norm_epsilon)
    return center * scale, scale


def norm_back(normed, scale, upstream):
    inner = row_mean(upstream * normed)
    return scale * (upstream - row_mean(upstream) - normed * inner)


def lane_hot(row, width):
    spread = jnp.transpose(jnp.broadcast_to(row.astype(f32), (lanes, lanes)))
    column = lax.broadcasted_iota(jnp.int32, (lanes, lanes), 1).astype(f32)
    parts = [
        jnp.where(spread == column + float(start), 1.0, 0.0).astype(bf16)
        for start in range(0, width, lanes)
    ]
    return jnp.concatenate(parts, 1)


def row_hot(row, count):
    index = lax.broadcasted_iota(jnp.int32, (count, lanes), 0)
    return jnp.where(index == row, 1.0, 0.0).astype(bf16)


def window(slots, block, own_rows, place_ref):
    core, odd = place_ref[0], place_ref[3]
    slot = slots[block]
    band = jnp.where(slot >= 6, 2, jnp.where(slot >= 3, 1, 0))
    sector = slot - 3 * band
    close = (sector == 2) == (odd == 0)
    side = jnp.where(sector == 1, 0, jnp.where(close, 1, 2))
    inside = (band == 2) == (core == 0)
    place = jnp.where(band == 1, -1, jnp.where(inside, 2, 5)) + side
    return pl.multiple_of(jnp.where(slot == 4, 0, own_rows + lanes * place), lanes)


def fill(table, own, near):
    table[0 : own.shape[0], :] = own[...]
    first = own.shape[0] + -own.shape[0] % lanes
    if first > own.shape[0]:
        table[own.shape[0] : first, :] = jnp.zeros_like(table[own.shape[0] : first, :])
    for part in near:
        table[first : first + part.shape[0], :] = part[...]
        first += part.shape[0]
    table[first:, :] = jnp.zeros_like(table[first:, :])


def send(source, target, sem):
    pltpu.make_async_copy(source, target, sem).start()


def finish(source, target, sem):
    pltpu.make_async_copy(source, target, sem).wait()


def prepare_kernel(live_ref, senders, receivers, state, weight, terms, *hots):
    nodes = state.shape[0]
    terms[0:nodes, :] = dot(state[...], weight[...]).astype(bf16)
    terms[nodes:, :] = jnp.zeros_like(terms[nodes:, :])
    block = lax.broadcasted_iota(jnp.int32, receivers.shape, 0)
    hot_rows(senders, jnp.where(block < live_ref[0], receivers[...], -1), *hots)


def hot_rows(senders, ends, send_hot, receive_hot, place_hot, sender_place_hot=None):
    for block in range(senders.shape[0]):
        here = slice(block * lanes, (block + 1) * lanes)
        begin_row, end_row = senders[block : block + 1, :], ends[block : block + 1, :]
        send_hot[here, :] = lane_hot(begin_row, send_hot.shape[1])
        receive_hot[here, :] = lane_hot(end_row, receive_hot.shape[1])
        place_hot[:, here] = row_hot(end_row, place_hot.shape[0])
        if sender_place_hot is not None:
            sender_place_hot[:, here] = row_hot(begin_row, sender_place_hot.shape[0])


def ends_kernel(live_ref, receivers, ends):
    block = lax.broadcasted_iota(jnp.int32, ends.shape, 0)
    ends[...] = jnp.where(block < live_ref[0], receivers[...], -1)


def encode_kernel(
    place_ref,
    slots,
    grid_columns,
    near_close,
    near_far,
    near_inner,
    near_inner_sides,
    near_outer,
    near_outer_sides,
    senders,
    ends,
    export,
    gain,
    base,
    receiver_weight,
    grid_weight,
    sender_weight,
    message_weight,
    update_weight,
    state,
    picked,
    inputs,
    hidden,
    pre_slope,
    mix_slope,
    normed_all,
    scale_all,
    update_normed,
    update_scale,
    table,
    projected,
    send_hot,
    receive_hot,
    place_hot,
):
    own = grid_columns.shape[1]
    nodes, width = base.shape
    projected[0:nodes, :] = dot(base[...], receiver_weight[...]).astype(bf16)
    projected[nodes:, :] = jnp.zeros_like(projected[nodes:, :])
    hot_rows(senders, ends, send_hot, receive_hot, place_hot)
    equal = lax.broadcasted_iota(jnp.int32, (own, own), 0) == lax.broadcasted_iota(
        jnp.int32, (own, own), 1
    )
    identity = jnp.where(equal, 1.0, 0.0).astype(bf16)
    grid_own = back_dot(identity, grid_columns[...]).astype(bf16)
    near = near_close, near_far, near_inner, near_inner_sides, near_outer, near_outer_sides
    fill(table, grid_own, near)
    for block in range(senders.shape[0]):
        here = slice(block * lanes, (block + 1) * lanes)
        start = window(slots, block, own, place_ref)
        inputs[here, :] = dot(send_hot[here, :], table[pl.ds(start, own), :]).astype(bf16)
    pre = dot(inputs[...], grid_weight[...])
    gate = sigmoid(pre)
    pre_slope[...] = (gate * (1.0 + pre * (1.0 - gate))).astype(bf16)
    hidden[...] = (pre * gate).astype(bf16)
    mix = dot(hidden[...], sender_weight[...]) + dot(receive_hot[...], projected[...])
    gate = sigmoid(mix)
    mix_slope[...] = (gate * (1.0 + mix * (1.0 - gate))).astype(bf16)
    product = dot((mix * gate).astype(bf16), message_weight[...])
    normed, scale = normalise(product)
    normed_all[...] = normed.astype(bf16)
    scale_all[...] = jnp.broadcast_to(scale, scale_all.shape)
    total = dot(place_hot[...], normed_all[...])
    update = dot(total.astype(bf16), update_weight[...])
    normed, scale = normalise(update)
    update_normed[...] = normed
    update_scale[...] = jnp.broadcast_to(scale, update_scale.shape)
    new_state = (base[...].astype(f32) + normed * gain[...]).astype(bf16)
    state[...] = new_state
    padded_state = jnp.concatenate([new_state, jnp.zeros((256 - nodes, width), bf16)], 0)
    picked[...] = dot(lane_hot(export[...], 256), padded_state).astype(bf16)


def process_kernel(
    place_ref,
    slots,
    state,
    near_close,
    near_far,
    near_inner,
    near_inner_sides,
    near_outer,
    near_outer_sides,
    terms,
    send_hot,
    receive_hot,
    place_hot,
    sender_place_hot,
    edge_sender,
    edge_message,
    node_update,
    gain,
    cotangent,
    mesh_far,
    own_grad,
    to_lon,
    to_inner,
    to_outer,
    to_outer_sides,
    sender_rows,
    mix_grads,
    table,
    slope,
    normed_all,
    upstream,
    table_grad,
    mesh_out,
    sem,
):
    nodes = state.shape[0]
    reach = 256
    near = near_close, near_far, near_inner, near_inner_sides, near_outer, near_outer_sides
    fill(table, state, near)
    blocks = slots.shape[0]
    starts = [window(slots, block, reach, place_ref) for block in range(blocks)]
    for block in range(blocks):
        here = slice(block * lanes, (block + 1) * lanes)
        picked = dot(send_hot[here, :], table[pl.ds(starts[block], reach), :])
        sender_rows[here, :] = picked.astype(bf16)
    mix = dot(sender_rows[...], edge_sender[...]) + dot(receive_hot[...], terms[...])
    gate = sigmoid(mix)
    slope[...] = (gate * (1.0 + mix * (1.0 - gate))).astype(bf16)
    product = dot((mix * gate).astype(bf16), edge_message[...])
    normed, edge_scale = normalise(product)
    normed_all[...] = normed.astype(bf16)
    total = dot(place_hot[...], normed_all[...])
    update = dot(total.astype(bf16), node_update[...])
    normed, scale = normalise(update)
    update_grad = norm_back(normed, scale, cotangent[...].astype(f32) * gain[...])
    upstream[0:nodes, :] = back_dot(update_grad.astype(bf16), node_update[...]).astype(bf16)
    upstream[nodes:, :] = jnp.zeros_like(upstream[nodes:, :])
    mesh_out[...] = (state[...].astype(f32) + normed * gain[...]).astype(bf16)
    send(mesh_out, mesh_far, sem)
    table_grad[...] = jnp.zeros_like(table_grad)
    arriving = dot(receive_hot[...], upstream[...])
    product_grad = norm_back(normed_all[...].astype(f32), edge_scale, arriving)
    mix_grad = back_dot(product_grad.astype(bf16), edge_message[...]) * slope[...].astype(f32)
    mix_grads[...] = mix_grad.astype(bf16)
    for block in range(blocks):
        here = slice(block * lanes, (block + 1) * lanes)
        table_grad[pl.ds(starts[block], nodes), :] += dot(
            sender_place_hot[:, here], mix_grads[here, :]
        )
    own_grad[...] = table_grad[0:nodes, :]
    first = reach
    for part in (to_lon, to_inner, to_outer, to_outer_sides):
        part[...] = table_grad[first : first + part.shape[0], :].astype(bf16)
        first += part.shape[0]
    finish(mesh_out, mesh_far, sem)


def edge_kernel(
    sender_rows, mix_grads, place_hot, edge_receiver, cotangent, edge_grad, state_part
):
    edge_grad[...] = cross_dot(sender_rows[...], mix_grads[...]).astype(bf16)
    receiver_grad = dot(place_hot[...], mix_grads[...]).astype(bf16)
    state_part[...] = cotangent[...].astype(f32) + back_dot(receiver_grad, edge_receiver[...])


def encode_back_kernel(
    place_ref,
    ends,
    export,
    state_part,
    own_grad,
    from_inner,
    from_close,
    from_far,
    from_outer,
    edge_sender,
    update_normed,
    update_scale,
    gain,
    update_weight,
    normed_all,
    scale_all,
    mix_slope,
    pre_slope,
    inputs,
    hidden,
    message_weight,
    sender_weight,
    edge_grad,
    given,
    kept,
    upstream,
    grads,
):
    nodes, width = state_part.shape
    arrived = from_close[...].astype(f32) + from_far[...].astype(f32)
    copies = arrived.shape[0]
    arrived += from_inner[0:copies, :].astype(f32) + from_outer[0:copies, :].astype(f32)
    table_grad = own_grad[...] + dot(row_hot(export[...], nodes), arrived.astype(bf16))
    state_grad = state_part[...] + back_dot(table_grad.astype(bf16), edge_sender[...])
    update_grad = norm_back(update_normed[...], update_scale[:, 0:1], state_grad * gain[...])
    upstream[0:nodes, :] = back_dot(update_grad.astype(bf16), update_weight[...]).astype(bf16)
    upstream[nodes:, :] = jnp.zeros_like(upstream[nodes:, :])
    variables = inputs.shape[1]
    grads[width : 2 * width, :] = edge_grad[...].astype(f32)
    grads[2 * width :, :] = jnp.zeros_like(grads[2 * width :, :])

    received = [lane_hot(ends[block : block + 1, :], 256) for block in range(ends.shape[0])]
    arriving = dot(jnp.concatenate(received, 0), upstream[...])
    product_grad = norm_back(
        normed_all[...].astype(f32), scale_all[:, 0:1], arriving
    ).astype(bf16)
    mix_grad = back_dot(product_grad, message_weight[...]) * mix_slope[...].astype(f32)
    mix_grad = mix_grad.astype(bf16)
    grads[0:width, :] = cross_dot(hidden[...], mix_grad)
    pre_grad = back_dot(mix_grad, sender_weight[...]) * pre_slope[...].astype(f32)
    grads[2 * width : 2 * width + variables, :] = cross_dot(
        inputs[...], pre_grad.astype(bf16)
    )
    arrange(place_ref, grads, given, kept)


def origin(place_ref, side, turn, piece):
    block = (place_ref[0] ^ side) * 4 + (place_ref[1 + side] ^ turn)
    return pl.ds(pl.multiple_of(block * piece, piece), piece)


def arrange(place_ref, grads, given, kept):
    piece = grads.shape[0] // 8
    for side, target in ((1, given), (0, kept)):
        for turn in range(4):
            rows = grads[origin(place_ref, side, turn, piece), :]
            target[turn * piece : (turn + 1) * piece, :] = rows.astype(bf16)


def order(place_ref, mine, other, grads):
    piece = grads.shape[0] // 8
    for side, source in ((0, mine), (1, other)):
        for turn in range(4):
            rows = source[turn * piece : (turn + 1) * piece, :].astype(f32)
            grads[origin(place_ref, side, turn, piece), :] = rows


def order_kernel(
    place_ref, mine, other, sender_grad, edge_grad, grid_grad, grads, last, sems
):
    order(place_ref, mine, other, grads)
    width = sender_grad.shape[0]
    last[...] = grads[2 * width : 2 * width + last.shape[0], :]
    copies = (
        (grads.at[0:width, :], sender_grad, sems.at[0]),
        (grads.at[width : 2 * width, :], edge_grad, sems.at[1]),
        (last, grid_grad, sems.at[2]),
    )
    for copy in copies:
        send(*copy)
    for copy in copies:
        finish(*copy)


def call(kernel, operands, outs, scratch, scalars, mib, work=4):
    smem = pl.BlockSpec(memory_space=pltpu.SMEM)
    vmem = pl.BlockSpec(memory_space=pltpu.VMEM)
    free = pl.BlockSpec(memory_space=pl.ANY)
    return pl.pallas_call(
        kernel,
        out_shape=[jax.ShapeDtypeStruct(shape, dtype) for shape, dtype, _ in outs],
        in_specs=[smem] * scalars + [vmem] * (len(operands) - scalars),
        out_specs=[free if kind else vmem for _, _, kind in outs],
        scratch_shapes=[pltpu.VMEM(*shape) if isinstance(shape, tuple) else shape for shape in scratch],
        compiler_params=pltpu.CompilerParams(vmem_limit_bytes=mib << 20),
        cost_estimate=pl.CostEstimate(flops=work << 30, bytes_accessed=8 << 20, transcendentals=0),
    )(*operands)


def partner(x, axis, flip):
    return lax.ppermute(x, axis, [(i, i ^ flip) for i in range(lax.axis_size(axis))])


def inner(x):
    return partner(x, "lat", 1)


def outer(x):
    ends = range(1, lax.axis_size("lat") - 1, 2)
    return lax.ppermute(x, "lat", [(i, i + 1) for i in ends] + [(i + 1, i) for i in ends])


def close(x):
    return partner(x, "lon", 1)


def far(x):
    size = lax.axis_size("lon")
    ends = range(1, size, 2)
    return lax.ppermute(
        x, "lon", [(i, (i + 1) % size) for i in ends] + [((i + 1) % size, i) for i in ends]
    )


def around(rows):
    lat, lon = (inner(rows), outer(rows)), (close(rows), far(rows))
    *lat, near_close, near_far = lax.optimization_barrier(lat + lon)
    sides = jnp.concatenate([near_close, near_far], 0)
    return near_close, near_far, lat[0], inner(sides), lat[1], outer(sides)


def add(left, right):
    return (left.astype(f32) + right.astype(f32)).astype(bf16)


flips = {"x1": 32, "x3": 96, "y1": 4, "y3": 12, "z1": 1, "z3": 3}
stages = (
    (("x1", "y3"), ("x3", "y1")),
    (("z1", "x3"), ("z3", "x1")),
    (("y1", "z3"), ("y3", "z1")),
)


def met(x, stage, turn):
    pairs = []
    for device in range(lax.axis_size("lat") * lax.axis_size("lon")):
        first, second = stages[stage][device // 16 % 2]
        flip = (turn & 1) * flips[first] ^ (turn >> 1) * flips[second]
        pairs.append((device, device ^ flip))
    return lax.ppermute(x, ("lat", "lon"), pairs)


def added(own, one, two, three):
    pair = own.astype(f32) + one.astype(f32)
    return (pair + (two.astype(f32) + three.astype(f32))).astype(bf16)


def summed(given, kept):
    values = add(kept, inner(given))
    piece = values.shape[0] // 4
    own, *others = [values[turn * piece : (turn + 1) * piece] for turn in range(4)]
    values = added(own, *[met(part, 0, turn) for turn, part in zip((1, 2, 3), others)])
    for stage in (1, 2):
        values = added(values, *[met(values, stage, turn) for turn in (1, 2, 3)])
    values = jnp.concatenate([values] + [met(values, 0, turn) for turn in (1, 2, 3)], 0)
    return values, inner(values)


def local(
    grid_in,
    grid_export,
    mesh_init,
    encode_senders,
    encode_slots,
    encode_receivers,
    encode_live,
    mesh_export,
    process_senders,
    process_slots,
    process_receivers,
    process_live,
    grid_weight,
    sender_weight,
    receiver_weight,
    message_weight,
    update_weight,
    encode_gain,
    edge_sender,
    edge_receiver,
    edge_message,
    node_update,
    node_gain,
    cotangent,
):
    grid_count, variables = grid_in.shape
    nodes, width = mesh_init.shape
    copies = mesh_export.shape[0]
    edges = encode_senders.shape[0] * encode_senders.shape[1]
    core, chip, row = [
        part.astype(jnp.int32)
        for part in (
            lax.axis_index("lat") & 1,
            lax.axis_index("lat") >> 1,
            lax.axis_index("lon") >> 2,
        )
    ]
    odd = lax.axis_index("lon").astype(jnp.int32) & 1
    even = (chip & 1 ^ chip >> 1) | row >> 1 << 1
    uneven = chip >> 1 | (row & 1 ^ row >> 1) << 1
    first, second = jnp.where(core == 0, even, uneven), jnp.where(core == 0, uneven, even)
    place = jnp.stack([core, first, second, odd])
    select = (grid_export[:, None] == jnp.arange(grid_count)[None, :]).astype(bf16)
    grid_near = around(dot(select, grid_in).astype(bf16))
    export = mesh_export[None]
    encode_gain, node_gain = encode_gain[None], node_gain[None]
    saved = [
        ((edges, variables), bf16, 0),
        ((edges, width), bf16, 0),
        ((edges, width), bf16, 0),
        ((edges, width), bf16, 0),
        ((edges, width), bf16, 0),
        ((edges, lanes), f32, 0),
        ((nodes, width), f32, 0),
        ((nodes, lanes), f32, 0),
    ]
    (ends,) = call(
        ends_kernel,
        (encode_live, encode_receivers),
        [(encode_receivers.shape, jnp.int32, 0)],
        [],
        1,
        16,
        30,
    )
    state, picked, inputs, hidden, pre_slope, mix_slope, normed, scale, *update = call(
        encode_kernel,
        (
            place,
            encode_slots,
            jnp.transpose(grid_in),
            *grid_near,
            encode_senders,
            ends,
            export,
            encode_gain,
            mesh_init,
            receiver_weight,
            grid_weight,
            sender_weight,
            message_weight,
            update_weight,
        ),
        [((nodes, width), bf16, 0), ((copies, width), bf16, 0)] + saved,
        [
            ((grid_count + 8 * lanes + grid_count - lanes, variables), bf16),
            ((256, width), bf16),
            ((edges, grid_count), bf16),
            ((edges, 256), bf16),
            ((nodes, edges), bf16),
        ],
        2,
        20,
    )
    terms, process_send, process_receive, process_place, process_sender_place = call(
        prepare_kernel,
        (process_live, process_senders, process_receivers, state, edge_receiver),
        [
            ((256, width), bf16, 0),
            ((edges, 256), bf16, 0),
            ((edges, 256), bf16, 0),
            ((nodes, edges), bf16, 0),
            ((nodes, edges), bf16, 0),
        ],
        [],
        1,
        16,
    )
    near = around(picked)
    (
        mesh_out,
        own_grad,
        to_lon,
        to_inner,
        to_outer,
        to_outer_sides,
        sender_rows,
        mix_grad,
    ) = call(
        process_kernel,
        (
            place,
            process_slots,
            state,
            *near,
            terms,
            process_send,
            process_receive,
            process_place,
            process_sender_place,
            edge_sender,
            edge_message,
            node_update,
            node_gain,
            cotangent,
        ),
        [
            ((nodes, width), bf16, 1),
            ((nodes, width), f32, 0),
            ((2 * copies, width), bf16, 0),
            ((3 * copies, width), bf16, 0),
            ((copies, width), bf16, 0),
            ((2 * copies, width), bf16, 0),
            ((edges, width), bf16, 0),
            ((edges, width), bf16, 0),
        ],
        [
            ((256 + 8 * copies + 128, width), bf16),
            ((edges, width), bf16),
            ((edges, width), bf16),
            ((256, width), bf16),
            ((256 + 8 * copies + 128, width), f32),
            ((nodes, width), bf16),
            pltpu.SemaphoreType.DMA,
        ],
        2,
        26,
    )
    from_outer_sides = outer(to_outer_sides)
    from_outer, from_inner = outer(to_outer), inner(to_inner)
    to_close, to_far = [
        (
            to_lon[side * copies : (side + 1) * copies].astype(f32)
            + from_inner[(side + 1) * copies : (side + 2) * copies].astype(f32)
            + from_outer_sides[side * copies : (side + 1) * copies].astype(f32)
        ).astype(bf16)
        for side in (0, 1)
    ]
    from_close, from_far = close(to_close), far(to_far)
    edge_grad, state_part = call(
        edge_kernel,
        (sender_rows, mix_grad, process_place, edge_receiver, cotangent),
        [((width, width), bf16, 0), ((nodes, width), f32, 0)],
        [],
        0,
        16,
    )
    given, kept = call(
        encode_back_kernel,
        (
            place,
            ends,
            export,
            state_part,
            own_grad,
            from_inner,
            from_close,
            from_far,
            from_outer,
            edge_sender,
            update[0],
            update[1],
            encode_gain,
            update_weight,
            normed,
            scale,
            mix_slope,
            pre_slope,
            inputs,
            hidden,
            message_weight,
            sender_weight,
            edge_grad,
        ),
        [((640, width), bf16, 0)] * 2,
        [((256, width), bf16), ((1280, width), f32)],
        1,
        16,
    )
    mine, other = summed(given, kept)
    sender_grad, edge_grad, grid_grad = call(
        order_kernel,
        (place, mine, other),
        [((width, width), f32, 1), ((width, width), f32, 1), ((variables, width), f32, 1)],
        [((1280, width), f32), ((variables, width), f32), pltpu.SemaphoreType.DMA((3,))],
        1,
        8,
    )
    return mesh_out, grid_grad, sender_grad, edge_grad


def solution(mesh):
    tiles, shared = P(("lat", "lon")), P()
    wide = P(("lat", "lon"), None)
    return jax.shard_map(
        local,
        mesh=mesh,
        in_specs=(
            (wide, tiles, wide, wide, tiles, wide, tiles, tiles, wide, tiles, wide, tiles)
            + (shared,) * 11
            + (wide,)
        ),
        out_specs=(wide, shared, shared, shared),
        check_vma=False,
    )
```

time: 125 us -> 117 us (0.936)
  waiting for transfers between devices: 44.7 us -> 36.5 us
  starting transfers between devices: 48.4 us -> 54.6 us
  local copies, waits for them, and re-layouts: 4.24 us -> 0.88 us
  Pallas kernels: 21.8 us -> 19.3 us
    ppermute x3 -> x6, starting transfers between devices: 13.2 us -> 21.7 us  [outer(): lax.ppermute(x, 'lat', [(i, i + 1) for i in ends] + [(i + 1, i) for i in...]
    ppermute x3, waiting for transfers between devices: 9.46 us -> 4.63 us  [far(): lax.ppermute(x, 'lon', [(i, (i + 1) % size) for i in ends] + [((i + 1) %...]
    unnamed x43 -> x44, local copies, waits for them, and re-layouts: 4.2 us -> 0.82 us
    pallas_call x5 -> x7, Pallas kernels: 21.8 us -> 19.3 us  [call(): pl.pallas_call(kernel, out_shape=[jax.ShapeDtypeStruct(shape, dtype) for...]
    ppermute x8 -> x10, waiting for transfers between devices: 6.25 us -> 3.83 us  [partner(): lax.ppermute(x, axis, [(i, i ^ flip) for i in range(lax.axis_size(axis))])]
    ppermute x3 -> x6, waiting for transfers between devices: 10.6 us -> 8.67 us  [outer(): lax.ppermute(x, 'lat', [(i, i + 1) for i in ends] + [(i + 1, i) for i in...]
    ppermute x3, starting transfers between devices: 13.4 us -> 11.8 us  [far(): lax.ppermute(x, 'lon', [(i, (i + 1) % size) for i in ends] + [((i + 1) %...]
    ppermute x8 -> x10, starting transfers between devices: 4.51 us -> 4.57 us  [partner(): lax.ppermute(x, axis, [(i, i ^ flip) for i in range(lax.axis_size(axis))])]
  transfers between devices with their start and end apart: 26 -> 31, of which waited for: 20 -> 20; matrix products, arithmetic and copies ran while one was open for 2% -> 0% of each run, Pallas kernels for 1% -> 1%
where the time goes in v4:
time: 117 us; the launch traced here: 116 us
  starting transfers between devices  54.6 us (47%)
  waiting for transfers between devices  36.5 us (31%)
  Pallas kernels  19.3 us (16%)
  between operations  2.63 us (2%)
  matrix products  1.19 us (1%)
    ppermute x6, starting transfers between devices, outer(): lax.ppermute(x, 'lat', [(i, i + 1) for i in ends] + [(i + 1, i) for i in...  21.7 us
    ppermute x12, waiting for transfers between devices, met(): return lax.ppermute(x, ('lat', 'lon'), pairs)  19.4 us
    pallas_call x7, Pallas kernels, call(): pl.pallas_call(kernel, out_shape=[jax.ShapeDtypeStruct(shape, dtype) for...  19.3 us
    ppermute x12, starting transfers between devices, met(): return lax.ppermute(x, ('lat', 'lon'), pairs)  16.5 us
    ppermute x3, starting transfers between devices, far(): lax.ppermute(x, 'lon', [(i, (i + 1) % size) for i in ends] + [((i + 1) %...  11.8 us
    ppermute x6, waiting for transfers between devices, outer(): lax.ppermute(x, 'lat', [(i, i + 1) for i in ends] + [(i + 1, i) for i in...  8.67 us
    ppermute x3, waiting for transfers between devices, far(): lax.ppermute(x, 'lon', [(i, (i + 1) % size) for i in ends] + [((i + 1) %...  4.63 us
    ppermute x10, starting transfers between devices, partner(): lax.ppermute(x, axis, [(i, i ^ flip) for i in range(lax.axis_size(axis))])  4.57 us
  transfers between devices with their start and end apart: 31, of which 20 were waited for; matrix products, arithmetic and copies ran while one was open for 0% of the time, Pallas kernels for 1%

profile of v4, /device:TPU:1, one launch (start us, length us, event | category | flops | bytes accessed | tf_op | source)
XLA Modules:
  0.0 115.7 jit_solution(17793079296165971184)
XLA Ops:
  1.8 7.1 %collective-permute-start.3 = (bf16[128,227]{1,0:T(8,128)(2,1)S(1)}, bf16[128,227]{1,0:T(8,128)(2,1)S(1)}, u32[]{:S(2)}, u32[]{:S(2)}) collective-permute-start(bf16[128,227]{1,0:T(8,128)(2,1)S(1)} %convolution_convert_fusion), channel_id=1, source_target_pairs={{1,2},{3,4},{5,6},{7,8},{9,10},{11,12},{13,14},{15,0},{2,1},{4,3},... | collective-permute-start | bytes 174344 | tf_op jit(solution)/shard_map/ppermute | solution.py:405
  8.9 3.9 %collective-permute-start.1 = (bf16[128,227]{1,0:T(8,128)(2,1)S(1)}, bf16[128,227]{1,0:T(8,128)(2,1)S(1)}, u32[]{:S(2)}, u32[]{:S(2)}) collective-permute-start(bf16[128,227]{1,0:T(8,128)(2,1)S(1)} %convolution_convert_fusion), channel_id=1, source_target_pairs={{16,32},{48,64},{80,96},{32,16},{64,48},{96,80},{17,33},{49,65},{8... | collective-permute-start | bytes 174344 | tf_op jit(solution)/shard_map/ppermute | solution.py:395
  15.0 3.9 %collective-permute-start.5 = (bf16[256,227]{1,0:T(8,128)(2,1)S(1)}, bf16[256,227]{1,0:T(8,128)(2,1)S(1)}, u32[]{:S(2)}, u32[]{:S(2)}) collective-permute-start(bf16[256,227]{1,0:T(8,128)(2,1)S(1)} %constant_dynamic-update-slice_fusion), channel_id=1, source_target_pairs={{16,32},{48,64},{80,96},{32,16},{64,48},{96,80},{17,33},{49,65},{8... | collective-permute-start | bytes 348680 | tf_op jit(solution)/shard_map/ppermute | solution.py:395
  21.7 5.0 %shard_map.256 = (bf16[160,512]{1,0:T(8,128)(2,1)S(1)}, bf16[128,512]{1,0:T(8,128)(2,1)S(1)}, bf16[1024,227]{1,0:T(8,128)(2,1)S(1)}, bf16[1024,512]{1,0:T(8,128)...) custom-call(s32[4]{0:T(128)S(1)} %pad_add_fusion.place_ref, ...), custom_call_target="tpu_custom_call" | custom-call | flops 4294967296 | bytes 8388608 | tf_op jit(solution)/shard_map/pallas_call | solution.py:374
  28.6 3.9 %collective-permute-start.7 = (bf16[128,512]{1,0:T(8,128)(2,1)S(1)}, bf16[128,512]{1,0:T(8,128)(2,1)S(1)}, u32[]{:S(2)}, u32[]{:S(2)}) collective-permute-start(bf16[128,512]{1,0:T(8,128)(2,1)S(1)} %get-tuple-element.47), channel_id=1, source_target_pairs={{16,32},{48,64},{80,96},{32,16},{64,48},{96,80},{17,33},{49,65},{8... | collective-permute-start | bytes 393224 | tf_op jit(solution)/shard_map/ppermute | solution.py:395
  35.2 4.1 %collective-permute-start.11 = (bf16[256,512]{1,0:T(8,128)(2,1)S(1)}, bf16[256,512]{1,0:T(8,128)(2,1)S(1)}, u32[]{:S(2)}, u32[]{:S(2)}) collective-permute-start(bf16[256,512]{1,0:T(8,128)(2,1)S(1)} %constant_dynamic-update-slice_fusion.2), channel_id=1, source_target_pairs={{16,32},{48,64},{80,96},{32,16},{64,48},{96,80},{17,33},{49,65},{8... | collective-permute-start | bytes 786440 | tf_op jit(solution)/shard_map/ppermute | solution.py:395
  40.0 3.3 %collective-permute-done.11.near_outer_sides = bf16[256,512]{1,0:T(8,128)(2,1)S(1)} collective-permute-done((bf16[256,512]{1,0:T(8,128)(2,1)S(1)}, bf16[256,512]{1,0:T(8,128)(2,1)S(1)}, u32[]{:S(2)}, u32[]{:S(2)}) %collective-permute-start.11) | collective-permute-done | bytes 262176 | tf_op jit(solution)/shard_map/ppermute | solution.py:395
  43.4 6.3 %shard_map.258 = (bf16[160,512]{1,0:T(8,128)(2,1)}, f32[160,512]{1,0:T(8,128)S(1)}, bf16[256,512]{1,0:T(8,128)(2,1)S(1)}, bf16[384,512]{1,0:T(8,128)(2,1)S(1)}, ...) custom-call(s32[4]{0:T(128)S(1)} %pad_add_fusion.place_ref, ...), custom_call_target="tpu_custom_call" | custom-call | flops 4294967296 | bytes 8388608 | tf_op jit(solution)/shard_map/pallas_call | solution.py:374
  49.7 3.7 %collective-permute-start.13 = (bf16[256,512]{1,0:T(8,128)(2,1)S(1)}, bf16[256,512]{1,0:T(8,128)(2,1)S(1)}, u32[]{:S(2)}, u32[]{:S(2)}) collective-permute-start(bf16[256,512]{1,0:T(8,128)(2,1)S(1)} %get-tuple-element.64), channel_id=1, source_target_pairs={{16,32},{48,64},{80,96},{32,16},{64,48},{96,80},{17,33},{49,65},{8... | collective-permute-start | bytes 786440 | tf_op jit(solution)/shard_map/ppermute | solution.py:395
  53.5 2.1 %collective-permute-start.16 = (bf16[128,512]{1,0:T(8,128)(2,1)S(1)}, bf16[128,512]{1,0:T(8,128)(2,1)S(1)}, u32[]{:S(2)}, u32[]{:S(2)}) collective-permute-start(bf16[128,512]{1,0:T(8,128)(2,1)S(1)} %get-tuple-element.65), channel_id=1, source_target_pairs={{16,32},{48,64},{80,96},{32,16},{64,48},{96,80},{17,33},{49,65},{8... | collective-permute-start | bytes 393224 | tf_op jit(solution)/shard_map/ppermute | solution.py:395
  55.6 1.9 %collective-permute-done.13 = bf16[256,512]{1,0:T(8,128)(2,1)S(1)} collective-permute-done((bf16[256,512]{1,0:T(8,128)(2,1)S(1)}, bf16[256,512]{1,0:T(8,128)(2,1)S(1)}, u32[]{:S(2)}, u32[]{:S(2)}) %collective-permute-start.13) | collective-permute-done | bytes 262176 | tf_op jit(solution)/shard_map/ppermute | solution.py:395
  57.6 2.9 %collective-permute-start.15 = (bf16[128,512]{1,0:T(8,128)(2,1)S(1)}, bf16[128,512]{1,0:T(8,128)(2,1)S(1)}, u32[]{:S(2)}, u32[]{:S(2)}) collective-permute-start(bf16[128,512]{1,0:T(8,128)(2,1)S(1)} %get-tuple-element.80), channel_id=1, source_target_pairs={{1,2},{3,4},{5,6},{7,8},{9,10},{11,12},{13,14},{15,0},{2,1},{4,3},... | collective-permute-start | bytes 393224 | tf_op jit(solution)/shard_map/ppermute | solution.py:405
  61.7 3.2 %collective-permute-done.15.from_far = bf16[128,512]{1,0:T(8,128)(2,1)S(1)} collective-permute-done((bf16[128,512]{1,0:T(8,128)(2,1)S(1)}, bf16[128,512]{1,0:T(8,128)(2,1)S(1)}, u32[]{:S(2)}, u32[]{:S(2)}) %collective-permute-start.15) | collective-permute-done | bytes 131104 | tf_op jit(solution)/shard_map/ppermute | solution.py:405
  64.9 4.2 %shard_map.260 = (bf16[640,512]{1,0:T(8,128)(2,1)S(1)}, bf16[640,512]{1,0:T(8,128)(2,1)S(1)}) custom-call(s32[4]{0:T(128)S(1)} %pad_add_fusion.place_ref, s32[8,128]{1,0:T(8,128)S(1)} %shard_map.255.ends, s32[1,128]{1,0:T(1,128)S(1)} %bitcast.14, f32[160,512]{1,0:T(8,128)S(1)} %get-tuple-element.60.state_part, f32[160,512]{1,0:T(8,128)S(1)} %get-tuple-element.61.own_grad, ...), custom_call_target="tpu_custom_call" | custom-call | flops 4294967296 | bytes 8388608 | tf_op jit(solution)/shard_map/pallas_call | solution.py:374
  69.2 2.1 %collective-permute-done.17 = bf16[640,512]{1,0:T(8,128)(2,1)S(1)} collective-permute-done((bf16[640,512]{1,0:T(8,128)(2,1)S(1)}, bf16[640,512]{1,0:T(8,128)(2,1)S(1)}, u32[]{:S(2)}, u32[]{:S(2)}) %collective-permute-start.17) | collective-permute-done | bytes 655392 | tf_op jit(solution)/shard_map/ppermute | solution.py:386
  71.5 3.4 %collective-permute-start.18 = (bf16[160,512]{1,0:T(8,128)(2,1)S(1)}, bf16[160,512]{1,0:T(8,128)(2,1)S(1)}, u32[]{:S(2)}, u32[]{:S(2)}) collective-permute-start(bf16[160,512]{1,0:T(8,128)(2,1)S(1)} %get-tuple-element.82), channel_id=1, source_target_pairs={{0,32},{1,33},{2,34},{3,35},{4,36},{5,37},{6,38},{7,39},{8,40},{9,... | collective-permute-start | bytes 491528 | tf_op jit(solution)/shard_map/ppermute | solution.py:435
  77.6 3.9 %collective-permute-done.20 = bf16[160,512]{1,0:T(8,128)(2,1)S(1)} collective-permute-done((bf16[160,512]{1,0:T(8,128)(2,1)S(1)}, bf16[160,512]{1,0:T(8,128)(2,1)S(1)}, u32[]{:S(2)}, u32[]{:S(2)}) %collective-permute-start.20) | collective-permute-done | bytes 163872 | tf_op jit(solution)/shard_map/ppermute | solution.py:435
  85.5 2.5 %collective-permute-done.23 = bf16[160,512]{1,0:T(8,128)(2,1)S(1)} collective-permute-done((bf16[160,512]{1,0:T(8,128)(2,1)S(1)}, bf16[160,512]{1,0:T(8,128)(2,1)S(1)}, u32[]{:S(2)}, u32[]{:S(2)}) %collective-permute-start.23) | collective-permute-done | bytes 163872 | tf_op jit(solution)/shard_map/ppermute | solution.py:435
  90.2 2.9 %collective-permute-start.25 = (bf16[160,512]{1,0:T(8,128)(2,1)S(1)}, bf16[160,512]{1,0:T(8,128)(2,1)S(1)}, u32[]{:S(2)}, u32[]{:S(2)}) collective-permute-start(bf16[160,512]{1,0:T(8,128)(2,1)S(1)} %add_convert_fusion.2), channel_id=1, source_target_pairs={{0,3},{1,2},{2,1},{3,0},{4,7},{5,6},{6,5},{7,4},{8,11},{9,10},{10,... | collective-permute-start | bytes 491528 | tf_op jit(solution)/shard_map/ppermute | solution.py:435
  94.0 2.5 %collective-permute-done.26 = bf16[160,512]{1,0:T(8,128)(2,1)S(1)} collective-permute-done((bf16[160,512]{1,0:T(8,128)(2,1)S(1)}, bf16[160,512]{1,0:T(8,128)(2,1)S(1)}, u32[]{:S(2)}, u32[]{:S(2)}) %collective-permute-start.26) | collective-permute-done | bytes 163872 | tf_op jit(solution)/shard_map/ppermute | solution.py:435
  100.0 1.9 %collective-permute-start.28 = (bf16[160,512]{1,0:T(8,128)(2,1)S(1)}, bf16[160,512]{1,0:T(8,128)(2,1)S(1)}, u32[]{:S(2)}, u32[]{:S(2)}) collective-permute-start(bf16[160,512]{1,0:T(8,128)(2,1)S(1)} %add_convert_fusion.1), channel_id=1, source_target_pairs={{0,12},{1,13},{2,14},{3,15},{4,8},{5,9},{6,10},{7,11},{8,4},{9,5},... | collective-permute-start | bytes 491528 | tf_op jit(solution)/shard_map/ppermute | solution.py:435
  102.8 2.5 %collective-permute-done.29 = bf16[160,512]{1,0:T(8,128)(2,1)S(1)} collective-permute-done((bf16[160,512]{1,0:T(8,128)(2,1)S(1)}, bf16[160,512]{1,0:T(8,128)(2,1)S(1)}, u32[]{:S(2)}, u32[]{:S(2)}) %collective-permute-start.29) | collective-permute-done | bytes 163872 | tf_op jit(solution)/shard_map/ppermute | solution.py:435
  107.7 4.0 %collective-permute-start.30 = (bf16[640,512]{1,0:T(8,128)(2,1)S(1)}, bf16[640,512]{1,0:T(8,128)(2,1)S(1)}, u32[]{:S(2)}, u32[]{:S(2)}) collective-permute-start(bf16[640,512]{1,0:T(8,128)(2,1)S(1)} %pad_maximum_fusion.mine), channel_id=1, source_target_pairs={{0,16},{16,0},{32,48},{48,32},{64,80},{80,64},{96,112},{112,96},{1... | collective-permute-start | bytes 1966088 | tf_op jit(solution)/shard_map/ppermute | solution.py:386
  113.4 2.2 %shard_map.261 = (f32[512,512]{1,0:T(8,128)}, f32[512,512]{1,0:T(8,128)}, f32[227,512]{1,0:T(8,128)}) custom-call(s32[4]{0:T(128)S(1)} %pad_add_fusion.place_ref, bf16[640,512]{1,0:T(8,128)(2,1)S(1)} %pad_maximum_fusion.mine, bf16[640,512]{1,0:T(8,128)(2,1)S(1)} %collective-permute-done.30.other), custom_call_target="tpu_custom_call" | custom-call | flops 4294967296 | bytes 8388608 | tf_op jit(solution)/shard_map/pallas_call | solution.py:374
  (100 shorter events, 29.6 us)
Async XLA Ops:
  1.8 11.8 %collective-permute-start.3 = (bf16[128,227]{1,0:T(8,128)(2,1)S(1)}, bf16[128,227]{1,0:T(8,128)(2,1)S(1)}, u32[]{:S(2)}, u32[]{:S(2)}) collective-permute-start(bf16[128,227]{1,0:T(8,128)(2,1)S(1)} %convolution_convert_fusion), channel_id=1, source_target_pairs={{1,2},{3,4},{5,6},{7,8},{9,10},{11,12},{13,14},{15,0},{2,1},{4,3},... | collective-permute-start | bytes 174344 | tf_op jit(solution)/shard_map/ppermute | solution.py:405
  8.9 5.9 %collective-permute-start.1 = (bf16[128,227]{1,0:T(8,128)(2,1)S(1)}, bf16[128,227]{1,0:T(8,128)(2,1)S(1)}, u32[]{:S(2)}, u32[]{:S(2)}) collective-permute-start(bf16[128,227]{1,0:T(8,128)(2,1)S(1)} %convolution_convert_fusion), channel_id=1, source_target_pairs={{16,32},{48,64},{80,96},{32,16},{64,48},{96,80},{17,33},{49,65},{8... | collective-permute-start | bytes 174344 | tf_op jit(solution)/shard_map/ppermute | solution.py:395
  15.0 6.5 %collective-permute-start.5 = (bf16[256,227]{1,0:T(8,128)(2,1)S(1)}, bf16[256,227]{1,0:T(8,128)(2,1)S(1)}, u32[]{:S(2)}, u32[]{:S(2)}) collective-permute-start(bf16[256,227]{1,0:T(8,128)(2,1)S(1)} %constant_dynamic-update-slice_fusion), channel_id=1, source_target_pairs={{16,32},{48,64},{80,96},{32,16},{64,48},{96,80},{17,33},{49,65},{8... | collective-permute-start | bytes 348680 | tf_op jit(solution)/shard_map/ppermute | solution.py:395
  26.7 8.0 %collective-permute-start.9 = (bf16[128,512]{1,0:T(8,128)(2,1)S(1)}, bf16[128,512]{1,0:T(8,128)(2,1)S(1)}, u32[]{:S(2)}, u32[]{:S(2)}) collective-permute-start(bf16[128,512]{1,0:T(8,128)(2,1)S(1)} %get-tuple-element.47), channel_id=1, source_target_pairs={{1,2},{3,4},{5,6},{7,8},{9,10},{11,12},{13,14},{15,0},{2,1},{4,3},... | collective-permute-start | bytes 393224 | tf_op jit(solution)/shard_map/ppermute | solution.py:405
  28.5 6.2 %collective-permute-start.8 = (bf16[128,512]{1,0:T(8,128)(2,1)S(1)}, bf16[128,512]{1,0:T(8,128)(2,1)S(1)}, u32[]{:S(2)}, u32[]{:S(2)}) collective-permute-start(bf16[128,512]{1,0:T(8,128)(2,1)S(1)} %get-tuple-element.47), channel_id=1, source_target_pairs={{0,1},{1,0},{2,3},{3,2},{4,5},{5,4},{6,7},{7,6},{8,9},{9,8},{10,11... | collective-permute-start | bytes 393224 | tf_op jit(solution)/shard_map/ppermute | solution.py:386
  28.6 6.6 %collective-permute-start.7 = (bf16[128,512]{1,0:T(8,128)(2,1)S(1)}, bf16[128,512]{1,0:T(8,128)(2,1)S(1)}, u32[]{:S(2)}, u32[]{:S(2)}) collective-permute-start(bf16[128,512]{1,0:T(8,128)(2,1)S(1)} %get-tuple-element.47), channel_id=1, source_target_pairs={{16,32},{48,64},{80,96},{32,16},{64,48},{96,80},{17,33},{49,65},{8... | collective-permute-start | bytes 393224 | tf_op jit(solution)/shard_map/ppermute | solution.py:395
  35.2 8.1 %collective-permute-start.11 = (bf16[256,512]{1,0:T(8,128)(2,1)S(1)}, bf16[256,512]{1,0:T(8,128)(2,1)S(1)}, u32[]{:S(2)}, u32[]{:S(2)}) collective-permute-start(bf16[256,512]{1,0:T(8,128)(2,1)S(1)} %constant_dynamic-update-slice_fusion.2), channel_id=1, source_target_pairs={{16,32},{48,64},{80,96},{32,16},{64,48},{96,80},{17,33},{49,65},{8... | collective-permute-start | bytes 786440 | tf_op jit(solution)/shard_map/ppermute | solution.py:395
  49.6 7.9 %collective-permute-start.12 = (bf16[384,512]{1,0:T(8,128)(2,1)S(1)}, bf16[384,512]{1,0:T(8,128)(2,1)S(1)}, u32[]{:S(2)}, u32[]{:S(2)}) collective-permute-start(bf16[384,512]{1,0:T(8,128)(2,1)S(1)} %get-tuple-element.62), channel_id=1, source_target_pairs={{0,16},{16,0},{32,48},{48,32},{64,80},{80,64},{96,112},{112,96},{1... | collective-permute-start | bytes 1179656 | tf_op jit(solution)/shard_map/ppermute | solution.py:386
  49.7 7.8 %collective-permute-start.13 = (bf16[256,512]{1,0:T(8,128)(2,1)S(1)}, bf16[256,512]{1,0:T(8,128)(2,1)S(1)}, u32[]{:S(2)}, u32[]{:S(2)}) collective-permute-start(bf16[256,512]{1,0:T(8,128)(2,1)S(1)} %get-tuple-element.64), channel_id=1, source_target_pairs={{16,32},{48,64},{80,96},{32,16},{64,48},{96,80},{17,33},{49,65},{8... | collective-permute-start | bytes 786440 | tf_op jit(solution)/shard_map/ppermute | solution.py:395
  53.5 8.2 %collective-permute-start.16 = (bf16[128,512]{1,0:T(8,128)(2,1)S(1)}, bf16[128,512]{1,0:T(8,128)(2,1)S(1)}, u32[]{:S(2)}, u32[]{:S(2)}) collective-permute-start(bf16[128,512]{1,0:T(8,128)(2,1)S(1)} %get-tuple-element.65), channel_id=1, source_target_pairs={{16,32},{48,64},{80,96},{32,16},{64,48},{96,80},{17,33},{49,65},{8... | collective-permute-start | bytes 393224 | tf_op jit(solution)/shard_map/ppermute | solution.py:395
  57.6 7.2 %collective-permute-start.15 = (bf16[128,512]{1,0:T(8,128)(2,1)S(1)}, bf16[128,512]{1,0:T(8,128)(2,1)S(1)}, u32[]{:S(2)}, u32[]{:S(2)}) collective-permute-start(bf16[128,512]{1,0:T(8,128)(2,1)S(1)} %get-tuple-element.80), channel_id=1, source_target_pairs={{1,2},{3,4},{5,6},{7,8},{9,10},{11,12},{13,14},{15,0},{2,1},{4,3},... | collective-permute-start | bytes 393224 | tf_op jit(solution)/shard_map/ppermute | solution.py:405
  71.5 6.1 %collective-permute-start.18 = (bf16[160,512]{1,0:T(8,128)(2,1)S(1)}, bf16[160,512]{1,0:T(8,128)(2,1)S(1)}, u32[]{:S(2)}, u32[]{:S(2)}) collective-permute-start(bf16[160,512]{1,0:T(8,128)(2,1)S(1)} %get-tuple-element.82), channel_id=1, source_target_pairs={{0,32},{1,33},{2,34},{3,35},{4,36},{5,37},{6,38},{7,39},{8,40},{9,... | collective-permute-start | bytes 491528 | tf_op jit(solution)/shard_map/ppermute | solution.py:435
  74.9 6.6 %collective-permute-start.20 = (bf16[160,512]{1,0:T(8,128)(2,1)S(1)}, bf16[160,512]{1,0:T(8,128)(2,1)S(1)}, u32[]{:S(2)}, u32[]{:S(2)}) collective-permute-start(bf16[160,512]{1,0:T(8,128)(2,1)S(1)} %get-tuple-element.83), channel_id=1, source_target_pairs={{0,44},{1,45},{2,46},{3,47},{4,40},{5,41},{6,42},{7,43},{8,36},{9,... | collective-permute-start | bytes 491528 | tf_op jit(solution)/shard_map/ppermute | solution.py:435
  75.1 6.4 %collective-permute-start.19 = (bf16[160,512]{1,0:T(8,128)(2,1)S(1)}, bf16[160,512]{1,0:T(8,128)(2,1)S(1)}, u32[]{:S(2)}, u32[]{:S(2)}) collective-permute-start(bf16[160,512]{1,0:T(8,128)(2,1)S(1)} %get-tuple-element.84), channel_id=1, source_target_pairs={{0,12},{1,13},{2,14},{3,15},{4,8},{5,9},{6,10},{7,11},{8,4},{9,5},... | collective-permute-start | bytes 491528 | tf_op jit(solution)/shard_map/ppermute | solution.py:435
  81.6 6.4 %collective-permute-start.23 = (bf16[160,512]{1,0:T(8,128)(2,1)S(1)}, bf16[160,512]{1,0:T(8,128)(2,1)S(1)}, u32[]{:S(2)}, u32[]{:S(2)}) collective-permute-start(bf16[160,512]{1,0:T(8,128)(2,1)S(1)} %add_convert_fusion.3), channel_id=1, source_target_pairs={{0,97},{1,96},{2,99},{3,98},{4,101},{5,100},{6,103},{7,102},{8,105... | collective-permute-start | bytes 491528 | tf_op jit(solution)/shard_map/ppermute | solution.py:435
  83.2 5.1 %collective-permute-start.22 = (bf16[160,512]{1,0:T(8,128)(2,1)S(1)}, bf16[160,512]{1,0:T(8,128)(2,1)S(1)}, u32[]{:S(2)}, u32[]{:S(2)}) collective-permute-start(bf16[160,512]{1,0:T(8,128)(2,1)S(1)} %add_convert_fusion.3), channel_id=1, source_target_pairs={{0,96},{1,97},{2,98},{3,99},{4,100},{5,101},{6,102},{7,103},{8,104... | collective-permute-start | bytes 491528 | tf_op jit(solution)/shard_map/ppermute | solution.py:435
  83.9 6.1 %collective-permute-start.21 = (bf16[160,512]{1,0:T(8,128)(2,1)S(1)}, bf16[160,512]{1,0:T(8,128)(2,1)S(1)}, u32[]{:S(2)}, u32[]{:S(2)}) collective-permute-start(bf16[160,512]{1,0:T(8,128)(2,1)S(1)} %add_convert_fusion.3), channel_id=1, source_target_pairs={{0,1},{1,0},{2,3},{3,2},{4,5},{5,4},{6,7},{7,6},{8,9},{9,8},{10,11... | collective-permute-start | bytes 491528 | tf_op jit(solution)/shard_map/ppermute | solution.py:435
  90.1 6.5 %collective-permute-start.26 = (bf16[160,512]{1,0:T(8,128)(2,1)S(1)}, bf16[160,512]{1,0:T(8,128)(2,1)S(1)}, u32[]{:S(2)}, u32[]{:S(2)}) collective-permute-start(bf16[160,512]{1,0:T(8,128)(2,1)S(1)} %add_convert_fusion.2), channel_id=1, source_target_pairs={{0,7},{1,6},{2,5},{3,4},{4,3},{5,2},{6,1},{7,0},{8,15},{9,14},{10,... | collective-permute-start | bytes 491528 | tf_op jit(solution)/shard_map/ppermute | solution.py:435
  90.2 7.4 %collective-permute-start.25 = (bf16[160,512]{1,0:T(8,128)(2,1)S(1)}, bf16[160,512]{1,0:T(8,128)(2,1)S(1)}, u32[]{:S(2)}, u32[]{:S(2)}) collective-permute-start(bf16[160,512]{1,0:T(8,128)(2,1)S(1)} %add_convert_fusion.2), channel_id=1, source_target_pairs={{0,3},{1,2},{2,1},{3,0},{4,7},{5,6},{6,5},{7,4},{8,11},{9,10},{10,... | collective-permute-start | bytes 491528 | tf_op jit(solution)/shard_map/ppermute | solution.py:435
  93.1 5.7 %collective-permute-start.24 = (bf16[160,512]{1,0:T(8,128)(2,1)S(1)}, bf16[160,512]{1,0:T(8,128)(2,1)S(1)}, u32[]{:S(2)}, u32[]{:S(2)}) collective-permute-start(bf16[160,512]{1,0:T(8,128)(2,1)S(1)} %add_convert_fusion.2), channel_id=1, source_target_pairs={{0,4},{1,5},{2,6},{3,7},{4,0},{5,1},{6,2},{7,3},{8,12},{9,13},{10,... | collective-permute-start | bytes 491528 | tf_op jit(solution)/shard_map/ppermute | solution.py:435
  98.8 6.5 %collective-permute-start.29 = (bf16[160,512]{1,0:T(8,128)(2,1)S(1)}, bf16[160,512]{1,0:T(8,128)(2,1)S(1)}, u32[]{:S(2)}, u32[]{:S(2)}) collective-permute-start(bf16[160,512]{1,0:T(8,128)(2,1)S(1)} %add_convert_fusion.1), channel_id=1, source_target_pairs={{0,44},{1,45},{2,46},{3,47},{4,40},{5,41},{6,42},{7,43},{8,36},{9,... | collective-permute-start | bytes 491528 | tf_op jit(solution)/shard_map/ppermute | solution.py:435
  100.0 6.4 %collective-permute-start.28 = (bf16[160,512]{1,0:T(8,128)(2,1)S(1)}, bf16[160,512]{1,0:T(8,128)(2,1)S(1)}, u32[]{:S(2)}, u32[]{:S(2)}) collective-permute-start(bf16[160,512]{1,0:T(8,128)(2,1)S(1)} %add_convert_fusion.1), channel_id=1, source_target_pairs={{0,12},{1,13},{2,14},{3,15},{4,8},{5,9},{6,10},{7,11},{8,4},{9,5},... | collective-permute-start | bytes 491528 | tf_op jit(solution)/shard_map/ppermute | solution.py:435
  101.9 5.7 %collective-permute-start.27 = (bf16[160,512]{1,0:T(8,128)(2,1)S(1)}, bf16[160,512]{1,0:T(8,128)(2,1)S(1)}, u32[]{:S(2)}, u32[]{:S(2)}) collective-permute-start(bf16[160,512]{1,0:T(8,128)(2,1)S(1)} %add_convert_fusion.1), channel_id=1, source_target_pairs={{0,32},{1,33},{2,34},{3,35},{4,36},{5,37},{6,38},{7,39},{8,40},{9,... | collective-permute-start | bytes 491528 | tf_op jit(solution)/shard_map/ppermute | solution.py:435
  107.7 5.7 %collective-permute-start.30 = (bf16[640,512]{1,0:T(8,128)(2,1)S(1)}, bf16[640,512]{1,0:T(8,128)(2,1)S(1)}, u32[]{:S(2)}, u32[]{:S(2)}) collective-permute-start(bf16[640,512]{1,0:T(8,128)(2,1)S(1)} %pad_maximum_fusion.mine), channel_id=1, source_target_pairs={{0,16},{16,0},{32,48},{48,32},{64,80},{80,64},{96,112},{112,96},{1... | collective-permute-start | bytes 1966088 | tf_op jit(solution)/shard_map/ppermute | solution.py:386
  (28 other events, 173.2 us)

commit v5 on v4

--- a/solution.py
+++ b/solution.py
@@ -329,52 +329,85 @@
     arrange(place_ref, grads, given, kept)
 
 
-def origin(place_ref, side, turn, piece):
-    block = (place_ref[0] ^ side) * 4 + (place_ref[1 + side] ^ turn)
-    return pl.ds(pl.multiple_of(block * piece, piece), piece)
+def owner(place_ref, side, turn):
+    return (place_ref[0] ^ side) * 4 + (place_ref[1 + side] ^ turn)
+
+
+def rows_of(block, count, first=0):
+    return pl.ds(pl.multiple_of(first + block * count, 32), count)
 
 
 def arrange(place_ref, grads, given, kept):
-    piece = grads.shape[0] // 8
+    width = grads.shape[1]
     for side, target in ((1, given), (0, kept)):
         for turn in range(4):
-            rows = grads[origin(place_ref, side, turn, piece), :]
-            target[turn * piece : (turn + 1) * piece, :] = rows.astype(bf16)
-
-
-def order(place_ref, mine, other, grads):
-    piece = grads.shape[0] // 8
+            block = owner(place_ref, side, turn)
+            first = turn * 160
+            for count, base in ((64, 0), (64, width), (32, 2 * width)):
+                rows = grads[rows_of(block, count, base), :]
+                target[first : first + count, :] = rows.astype(bf16)
+                first += count
+
+
+def order(place_ref, side, source, sender_grad, edge_grad, parts, sems):
+    copies = []
+    for turn in range(4):
+        block = owner(place_ref, side, turn)
+        parts[turn] = source[turn * 160 : turn * 160 + 128, :].astype(f32)
+        for index, target in enumerate((sender_grad, edge_grad)):
+            copies.append(
+                (
+                    parts.at[turn, index * 64 : index * 64 + 64, :],
+                    target.at[rows_of(block, 64), :],
+                    sems.at[turn, index],
+                )
+            )
+            send(*copies[-1])
+    return copies
+
+
+def order_mine_kernel(place_ref, mine, sender_grad, edge_grad, parts, sems):
+    for copy in order(place_ref, 0, mine, sender_grad, edge_grad, parts, sems):
+        finish(*copy)
+
+
+def order_other_kernel(
+    place_ref,
+    mine,
+    other,
+    sender_in,
+    edge_in,
+    sender_grad,
+    edge_grad,
+    grid_grad,
+    parts,
+    grid_rows,
+    last,
+    sems,
+    last_sem,
+):
+    copies = order(place_ref, 1, other, sender_grad, edge_grad, parts, sems)
     for side, source in ((0, mine), (1, other)):
         for turn in range(4):
-            rows = source[turn * piece : (turn + 1) * piece, :].astype(f32)
-            grads[origin(place_ref, side, turn, piece), :] = rows
-
-
-def order_kernel(
-    place_ref, mine, other, sender_grad, edge_grad, grid_grad, grads, last, sems
-):
-    order(place_ref, mine, other, grads)
-    width = sender_grad.shape[0]
-    last[...] = grads[2 * width : 2 * width + last.shape[0], :]
-    copies = (
-        (grads.at[0:width, :], sender_grad, sems.at[0]),
-        (grads.at[width : 2 * width, :], edge_grad, sems.at[1]),
-        (last, grid_grad, sems.at[2]),
-    )
-    for copy in copies:
-        send(*copy)
+            rows = source[turn * 160 + 128 : (turn + 1) * 160, :].astype(f32)
+            grid_rows[rows_of(owner(place_ref, side, turn), 32), :] = rows
+    last[...] = grid_rows[0 : last.shape[0], :]
+    send(last, grid_grad, last_sem)
     for copy in copies:
         finish(*copy)
-
-
-def call(kernel, operands, outs, scratch, scalars, mib, work=4):
+    finish(last, grid_grad, last_sem)
+
+
+def call(kernel, operands, outs, scratch, scalars, mib, work=4, kept_places={}):
     smem = pl.BlockSpec(memory_space=pltpu.SMEM)
     vmem = pl.BlockSpec(memory_space=pltpu.VMEM)
     free = pl.BlockSpec(memory_space=pl.ANY)
     return pl.pallas_call(
         kernel,
         out_shape=[jax.ShapeDtypeStruct(shape, dtype) for shape, dtype, _ in outs],
-        in_specs=[smem] * scalars + [vmem] * (len(operands) - scalars),
+        in_specs=[smem] * scalars
+        + [free if index in kept_places else vmem for index in range(scalars, len(operands))],
+        input_output_aliases=kept_places,
         out_specs=[free if kind else vmem for _, _, kind in outs],
         scratch_shapes=[pltpu.VMEM(*shape) if isinstance(shape, tuple) else shape for shape in scratch],
         compiler_params=pltpu.CompilerParams(vmem_limit_bytes=mib << 20),
@@ -408,10 +441,10 @@
 
 
 def around(rows):
-    lat, lon = (inner(rows), outer(rows)), (close(rows), far(rows))
-    *lat, near_close, near_far = lax.optimization_barrier(lat + lon)
+    near_outer, near_inner, near_close, near_far = outer(rows), inner(rows), close(rows), far(rows)
+    near_inner, near_close, near_far = lax.optimization_barrier((near_inner, near_close, near_far))
     sides = jnp.concatenate([near_close, near_far], 0)
-    return near_close, near_far, lat[0], inner(sides), lat[1], outer(sides)
+    return near_close, near_far, near_inner, inner(sides), near_outer, outer(sides)
 
 
 def add(left, right):
@@ -420,9 +453,9 @@
 
 flips = {"x1": 32, "x3": 96, "y1": 4, "y3": 12, "z1": 1, "z3": 3}
 stages = (
-    (("x1", "y3"), ("x3", "y1")),
+    (("x1", "y1"), ("x3", "y3")),
     (("z1", "x3"), ("z3", "x1")),
-    (("y1", "z3"), ("y3", "z1")),
+    (("y3", "z3"), ("y1", "z1")),
 )
 
 
@@ -448,7 +481,7 @@
     for stage in (1, 2):
         values = added(values, *[met(values, stage, turn) for turn in (1, 2, 3)])
     values = jnp.concatenate([values] + [met(values, 0, turn) for turn in (1, 2, 3)], 0)
-    return values, inner(values)
+    return values
 
 
 def local(
@@ -490,9 +523,9 @@
         )
     ]
     odd = lax.axis_index("lon").astype(jnp.int32) & 1
-    even = (chip & 1 ^ chip >> 1) | row >> 1 << 1
-    uneven = chip >> 1 | (row & 1 ^ row >> 1) << 1
-    first, second = jnp.where(core == 0, even, uneven), jnp.where(core == 0, uneven, even)
+    plain = (chip & 1 ^ chip >> 1) | (row & 1 ^ row >> 1) << 1
+    wrapped = chip >> 1 | row >> 1 << 1
+    first, second = jnp.where(core == 0, plain, wrapped), jnp.where(core == 0, wrapped, plain)
     place = jnp.stack([core, first, second, odd])
     select = (grid_export[:, None] == jnp.arange(grid_count)[None, :]).astype(bf16)
     grid_near = around(dot(select, grid_in).astype(bf16))
@@ -661,14 +694,22 @@
         1,
         16,
     )
-    mine, other = summed(given, kept)
+    mine = summed(given, kept)
+    other = inner(mine)
+    halves = [((width, width), f32, 1)] * 2
+    scratch = [((4, 128, width), f32), pltpu.SemaphoreType.DMA((4, 2))]
+    parts = call(order_mine_kernel, (place, mine), halves, scratch, 1, 8)
     sender_grad, edge_grad, grid_grad = call(
-        order_kernel,
-        (place, mine, other),
-        [((width, width), f32, 1), ((width, width), f32, 1), ((variables, width), f32, 1)],
-        [((1280, width), f32), ((variables, width), f32), pltpu.SemaphoreType.DMA((3,))],
+        order_other_kernel,
+        (place, mine, other, *parts),
+        halves + [((variables, width), f32, 1)],
+        scratch[:1]
+        + [((256, width), f32), ((variables, width), f32)]
+        + scratch[1:]
+        + [pltpu.SemaphoreType.DMA],
         1,
         8,
+        kept_places={3: 0, 4: 1},
     )
     return mesh_out, grid_grad, sender_grad, edge_grad
 

time: 117 us -> 115 us (0.983)
  waiting for transfers between devices: 36.5 us -> 30.6 us
  starting transfers between devices: 54.6 us -> 58.2 us
    ppermute x3, starting transfers between devices: 11.8 us -> 13.6 us  [far(): lax.ppermute(x, 'lon', [(i, (i + 1) % size) for i in ends] + [((i + 1) %...]
    ppermute x3, waiting for transfers between devices: 4.63 us -> 2.93 us  [far(): lax.ppermute(x, 'lon', [(i, (i + 1) % size) for i in ends] + [((i + 1) %...]
    ppermute x6, waiting for transfers between devices: 8.67 us -> 7.09 us  [outer(): lax.ppermute(x, 'lat', [(i, i + 1) for i in ends] + [(i + 1, i) for i in...]
    ppermute x10, waiting for transfers between devices: 3.83 us -> 2.27 us  [partner(): lax.ppermute(x, axis, [(i, i ^ flip) for i in range(lax.axis_size(axis))])]
    ppermute x10, starting transfers between devices: 4.57 us -> 5.83 us  [partner(): lax.ppermute(x, axis, [(i, i ^ flip) for i in range(lax.axis_size(axis))])]
    ppermute x12, starting transfers between devices: 16.5 us -> 17.7 us  [met(): return lax.ppermute(x, ('lat', 'lon'), pairs)]
    pallas_call x7 -> x8, Pallas kernels: 19.3 us -> 20.4 us  [call(): pl.pallas_call(kernel, out_shape=[jax.ShapeDtypeStruct(shape, dtype) for...]
  transfers between devices with their start and end apart: 31 -> 31, of which waited for: 20 -> 17; matrix products, arithmetic and copies ran while one was open for 0% -> 0% of each run, Pallas kernels for 1% -> 3%
where the time goes in v5:
time: 115 us
  starting transfers between devices  58.2 us (51%)
  waiting for transfers between devices  30.6 us (27%)
  Pallas kernels  20.4 us (18%)
  between operations  2.65 us (2%)
  matrix products  1.19 us (1%)
    ppermute x6, starting transfers between devices, outer(): lax.ppermute(x, 'lat', [(i, i + 1) for i in ends] + [(i + 1, i) for i in...  21.1 us
    pallas_call x8, Pallas kernels, call(): pl.pallas_call(kernel, out_shape=[jax.ShapeDtypeStruct(shape, dtype) for...  20.4 us
    ppermute x12, waiting for transfers between devices, met(): return lax.ppermute(x, ('lat', 'lon'), pairs)  18.4 us
    ppermute x12, starting transfers between devices, met(): return lax.ppermute(x, ('lat', 'lon'), pairs)  17.7 us
    ppermute x3, starting transfers between devices, far(): lax.ppermute(x, 'lon', [(i, (i + 1) % size) for i in ends] + [((i + 1) %...  13.6 us
    ppermute x6, waiting for transfers between devices, outer(): lax.ppermute(x, 'lat', [(i, i + 1) for i in ends] + [(i + 1, i) for i in...  7.09 us
    ppermute x10, starting transfers between devices, partner(): lax.ppermute(x, axis, [(i, i ^ flip) for i in range(lax.axis_size(axis))])  5.83 us
    ppermute x3, waiting for transfers between devices, far(): lax.ppermute(x, 'lon', [(i, (i + 1) % size) for i in ends] + [((i + 1) %...  2.93 us
  transfers between devices with their start and end apart: 31, of which 17 were waited for; matrix products, arithmetic and copies ran while one was open for 0% of the time, Pallas kernels for 3%

profile of v5, /device:TPU:1, one launch (start us, length us, event | category | flops | bytes accessed | tf_op | source)
XLA Modules:
  0.0 114.6 jit_solution(8995802205395277449)
XLA Ops:
  1.8 7.1 %collective-permute-start.2 = (bf16[128,227]{1,0:T(8,128)(2,1)S(1)}, bf16[128,227]{1,0:T(8,128)(2,1)S(1)}, u32[]{:S(2)}, u32[]{:S(2)}) collective-permute-start(bf16[128,227]{1,0:T(8,128)(2,1)S(1)} %convolution_convert_fusion), channel_id=1, source_target_pairs={{1,2},{3,4},{5,6},{7,8},{9,10},{11,12},{13,14},{15,0},{2,1},{4,3},... | collective-permute-start | bytes 174344 | tf_op jit(solution)/shard_map/ppermute | solution.py:438
  9.9 3.0 %collective-permute-start.4 = (bf16[128,227]{1,0:T(8,128)(2,1)S(1)}, bf16[128,227]{1,0:T(8,128)(2,1)S(1)}, u32[]{:S(2)}, u32[]{:S(2)}) collective-permute-start(bf16[128,227]{1,0:T(8,128)(2,1)S(1)} %convolution_convert_fusion), channel_id=1, source_target_pairs={{16,32},{48,64},{80,96},{32,16},{64,48},{96,80},{17,33},{49,65},{8... | collective-permute-start | bytes 174344 | tf_op jit(solution)/shard_map/ppermute | solution.py:428
  13.7 3.8 %collective-permute-start.5 = (bf16[256,227]{1,0:T(8,128)(2,1)S(1)}, bf16[256,227]{1,0:T(8,128)(2,1)S(1)}, u32[]{:S(2)}, u32[]{:S(2)}) collective-permute-start(bf16[256,227]{1,0:T(8,128)(2,1)S(1)} %constant_dynamic-update-slice_fusion), channel_id=1, source_target_pairs={{16,32},{48,64},{80,96},{32,16},{64,48},{96,80},{17,33},{49,65},{8... | collective-permute-start | bytes 348680 | tf_op jit(solution)/shard_map/ppermute | solution.py:428
  20.4 5.0 %shard_map.256 = (bf16[160,512]{1,0:T(8,128)(2,1)S(1)}, bf16[128,512]{1,0:T(8,128)(2,1)S(1)}, bf16[1024,227]{1,0:T(8,128)(2,1)S(1)}, bf16[1024,512]{1,0:T(8,128)...) custom-call(s32[4]{0:T(128)S(1)} %pad_add_fusion.place_ref, ...), custom_call_target="tpu_custom_call" | custom-call | flops 4294967296 | bytes 8388608 | tf_op jit(solution)/shard_map/pallas_call | solution.py:405
  25.4 3.1 %collective-permute-start.8 = (bf16[128,512]{1,0:T(8,128)(2,1)S(1)}, bf16[128,512]{1,0:T(8,128)(2,1)S(1)}, u32[]{:S(2)}, u32[]{:S(2)}) collective-permute-start(bf16[128,512]{1,0:T(8,128)(2,1)S(1)} %get-tuple-element.46), channel_id=1, source_target_pairs={{1,2},{3,4},{5,6},{7,8},{9,10},{11,12},{13,14},{15,0},{2,1},{4,3},... | collective-permute-start | bytes 393224 | tf_op jit(solution)/shard_map/ppermute | solution.py:438
  29.1 3.9 %collective-permute-start.10 = (bf16[128,512]{1,0:T(8,128)(2,1)S(1)}, bf16[128,512]{1,0:T(8,128)(2,1)S(1)}, u32[]{:S(2)}, u32[]{:S(2)}) collective-permute-start(bf16[128,512]{1,0:T(8,128)(2,1)S(1)} %get-tuple-element.46), channel_id=1, source_target_pairs={{16,32},{48,64},{80,96},{32,16},{64,48},{96,80},{17,33},{49,65},{8... | collective-permute-start | bytes 393224 | tf_op jit(solution)/shard_map/ppermute | solution.py:428
  33.4 4.6 %collective-permute-start.11 = (bf16[256,512]{1,0:T(8,128)(2,1)S(1)}, bf16[256,512]{1,0:T(8,128)(2,1)S(1)}, u32[]{:S(2)}, u32[]{:S(2)}) collective-permute-start(bf16[256,512]{1,0:T(8,128)(2,1)S(1)} %constant_dynamic-update-slice_fusion.2), channel_id=1, source_target_pairs={{16,32},{48,64},{80,96},{32,16},{64,48},{96,80},{17,33},{49,65},{8... | collective-permute-start | bytes 786440 | tf_op jit(solution)/shard_map/ppermute | solution.py:428
  38.7 3.3 %collective-permute-done.11.near_outer_sides = bf16[256,512]{1,0:T(8,128)(2,1)S(1)} collective-permute-done((bf16[256,512]{1,0:T(8,128)(2,1)S(1)}, bf16[256,512]{1,0:T(8,128)(2,1)S(1)}, u32[]{:S(2)}, u32[]{:S(2)}) %collective-permute-start.11) | collective-permute-done | bytes 262176 | tf_op jit(solution)/shard_map/ppermute | solution.py:428
  42.0 6.3 %shard_map.258 = (bf16[160,512]{1,0:T(8,128)(2,1)}, f32[160,512]{1,0:T(8,128)S(1)}, bf16[256,512]{1,0:T(8,128)(2,1)S(1)}, bf16[384,512]{1,0:T(8,128)(2,1)S(1)}, ...) custom-call(s32[4]{0:T(128)S(1)} %pad_add_fusion.place_ref, ...), custom_call_target="tpu_custom_call" | custom-call | flops 4294967296 | bytes 8388608 | tf_op jit(solution)/shard_map/pallas_call | solution.py:405
  48.4 3.6 %collective-permute-start.13 = (bf16[256,512]{1,0:T(8,128)(2,1)S(1)}, bf16[256,512]{1,0:T(8,128)(2,1)S(1)}, u32[]{:S(2)}, u32[]{:S(2)}) collective-permute-start(bf16[256,512]{1,0:T(8,128)(2,1)S(1)} %get-tuple-element.62), channel_id=1, source_target_pairs={{16,32},{48,64},{80,96},{32,16},{64,48},{96,80},{17,33},{49,65},{8... | collective-permute-start | bytes 786440 | tf_op jit(solution)/shard_map/ppermute | solution.py:428
  52.1 2.1 %collective-permute-start.16 = (bf16[128,512]{1,0:T(8,128)(2,1)S(1)}, bf16[128,512]{1,0:T(8,128)(2,1)S(1)}, u32[]{:S(2)}, u32[]{:S(2)}) collective-permute-start(bf16[128,512]{1,0:T(8,128)(2,1)S(1)} %get-tuple-element.63), channel_id=1, source_target_pairs={{16,32},{48,64},{80,96},{32,16},{64,48},{96,80},{17,33},{49,65},{8... | collective-permute-start | bytes 393224 | tf_op jit(solution)/shard_map/ppermute | solution.py:428
  56.2 3.4 %collective-permute-start.15 = (bf16[128,512]{1,0:T(8,128)(2,1)S(1)}, bf16[128,512]{1,0:T(8,128)(2,1)S(1)}, u32[]{:S(2)}, u32[]{:S(2)}) collective-permute-start(bf16[128,512]{1,0:T(8,128)(2,1)S(1)} %get-tuple-element.80), channel_id=1, source_target_pairs={{1,2},{3,4},{5,6},{7,8},{9,10},{11,12},{13,14},{15,0},{2,1},{4,3},... | collective-permute-start | bytes 393224 | tf_op jit(solution)/shard_map/ppermute | solution.py:438
  60.8 2.6 %collective-permute-done.15.from_far = bf16[128,512]{1,0:T(8,128)(2,1)S(1)} collective-permute-done((bf16[128,512]{1,0:T(8,128)(2,1)S(1)}, bf16[128,512]{1,0:T(8,128)(2,1)S(1)}, u32[]{:S(2)}, u32[]{:S(2)}) %collective-permute-start.15) | collective-permute-done | bytes 131104 | tf_op jit(solution)/shard_map/ppermute | solution.py:438
  63.5 4.2 %shard_map.260 = (bf16[640,512]{1,0:T(8,128)(2,1)S(1)}, bf16[640,512]{1,0:T(8,128)(2,1)S(1)}) custom-call(s32[4]{0:T(128)S(1)} %pad_add_fusion.place_ref, s32[8,128]{1,0:T(8,128)S(1)} %shard_map.255.ends, s32[1,128]{1,0:T(1,128)S(1)} %bitcast.14, f32[160,512]{1,0:T(8,128)S(1)} %get-tuple-element.58.state_part, f32[160,512]{1,0:T(8,128)S(1)} %get-tuple-element.59.own_grad, ...), custom_call_target="tpu_custom_call" | custom-call | flops 4294967296 | bytes 8388608 | tf_op jit(solution)/shard_map/pallas_call | solution.py:405
  70.1 3.4 %collective-permute-start.18 = (bf16[160,512]{1,0:T(8,128)(2,1)S(1)}, bf16[160,512]{1,0:T(8,128)(2,1)S(1)}, u32[]{:S(2)}, u32[]{:S(2)}) collective-permute-start(bf16[160,512]{1,0:T(8,128)(2,1)S(1)} %get-tuple-element.82), channel_id=1, source_target_pairs={{0,32},{1,33},{2,34},{3,35},{4,36},{5,37},{6,38},{7,39},{8,40},{9,... | collective-permute-start | bytes 491528 | tf_op jit(solution)/shard_map/ppermute | solution.py:468
  73.5 2.5 %collective-permute-start.19 = (bf16[160,512]{1,0:T(8,128)(2,1)S(1)}, bf16[160,512]{1,0:T(8,128)(2,1)S(1)}, u32[]{:S(2)}, u32[]{:S(2)}) collective-permute-start(bf16[160,512]{1,0:T(8,128)(2,1)S(1)} %get-tuple-element.84), channel_id=1, source_target_pairs={{0,4},{1,5},{2,6},{3,7},{4,0},{5,1},{6,2},{7,3},{8,12},{9,13},{10,... | collective-permute-start | bytes 491528 | tf_op jit(solution)/shard_map/ppermute | solution.py:468
  76.2 4.8 %collective-permute-done.20 = bf16[160,512]{1,0:T(8,128)(2,1)S(1)} collective-permute-done((bf16[160,512]{1,0:T(8,128)(2,1)S(1)}, bf16[160,512]{1,0:T(8,128)(2,1)S(1)}, u32[]{:S(2)}, u32[]{:S(2)}) %collective-permute-start.20) | collective-permute-done | bytes 163872 | tf_op jit(solution)/shard_map/ppermute | solution.py:468
  81.1 3.5 %collective-permute-start.23 = (bf16[160,512]{1,0:T(8,128)(2,1)S(1)}, bf16[160,512]{1,0:T(8,128)(2,1)S(1)}, u32[]{:S(2)}, u32[]{:S(2)}) collective-permute-start(bf16[160,512]{1,0:T(8,128)(2,1)S(1)} %add_convert_fusion.3), channel_id=1, source_target_pairs={{0,97},{1,96},{2,99},{3,98},{4,101},{5,100},{6,103},{7,102},{8,105... | collective-permute-start | bytes 491528 | tf_op jit(solution)/shard_map/ppermute | solution.py:468
  85.0 2.7 %collective-permute-done.23 = bf16[160,512]{1,0:T(8,128)(2,1)S(1)} collective-permute-done((bf16[160,512]{1,0:T(8,128)(2,1)S(1)}, bf16[160,512]{1,0:T(8,128)(2,1)S(1)}, u32[]{:S(2)}, u32[]{:S(2)}) %collective-permute-start.23) | collective-permute-done | bytes 163872 | tf_op jit(solution)/shard_map/ppermute | solution.py:468
  90.2 2.5 %collective-permute-start.24 = (bf16[160,512]{1,0:T(8,128)(2,1)S(1)}, bf16[160,512]{1,0:T(8,128)(2,1)S(1)}, u32[]{:S(2)}, u32[]{:S(2)}) collective-permute-start(bf16[160,512]{1,0:T(8,128)(2,1)S(1)} %add_convert_fusion.2), channel_id=1, source_target_pairs={{0,12},{1,13},{2,14},{3,15},{4,8},{5,9},{6,10},{7,11},{8,4},{9,5},... | collective-permute-start | bytes 491528 | tf_op jit(solution)/shard_map/ppermute | solution.py:468
  92.8 2.5 %collective-permute-done.26 = bf16[160,512]{1,0:T(8,128)(2,1)S(1)} collective-permute-done((bf16[160,512]{1,0:T(8,128)(2,1)S(1)}, bf16[160,512]{1,0:T(8,128)(2,1)S(1)}, u32[]{:S(2)}, u32[]{:S(2)}) %collective-permute-start.26) | collective-permute-done | bytes 163872 | tf_op jit(solution)/shard_map/ppermute | solution.py:468
  96.2 2.8 %collective-permute-start.29 = (bf16[160,512]{1,0:T(8,128)(2,1)S(1)}, bf16[160,512]{1,0:T(8,128)(2,1)S(1)}, u32[]{:S(2)}, u32[]{:S(2)}) collective-permute-start(bf16[160,512]{1,0:T(8,128)(2,1)S(1)} %add_convert_fusion.1), channel_id=1, source_target_pairs={{0,36},{1,37},{2,38},{3,39},{4,32},{5,33},{6,34},{7,35},{8,44},{9,... | collective-permute-start | bytes 491528 | tf_op jit(solution)/shard_map/ppermute | solution.py:468
  101.4 2.5 %collective-permute-done.29 = bf16[160,512]{1,0:T(8,128)(2,1)S(1)} collective-permute-done((bf16[160,512]{1,0:T(8,128)(2,1)S(1)}, bf16[160,512]{1,0:T(8,128)(2,1)S(1)}, u32[]{:S(2)}, u32[]{:S(2)}) %collective-permute-start.29) | collective-permute-done | bytes 163872 | tf_op jit(solution)/shard_map/ppermute | solution.py:468
  106.5 4.5 %collective-permute-start.30 = (bf16[640,512]{1,0:T(8,128)(2,1)S(1)}, bf16[640,512]{1,0:T(8,128)(2,1)S(1)}, u32[]{:S(2)}, u32[]{:S(2)}) collective-permute-start(bf16[640,512]{1,0:T(8,128)(2,1)S(1)} %pad_maximum_fusion.mine), channel_id=1, source_target_pairs={{0,16},{16,0},{32,48},{48,32},{64,80},{80,64},{96,112},{112,96},{1... | collective-permute-start | bytes 1966088 | tf_op jit(solution)/shard_map/ppermute | solution.py:419
  (101 shorter events, 24.1 us)
Async XLA Ops:
  1.8 11.7 %collective-permute-start.2 = (bf16[128,227]{1,0:T(8,128)(2,1)S(1)}, bf16[128,227]{1,0:T(8,128)(2,1)S(1)}, u32[]{:S(2)}, u32[]{:S(2)}) collective-permute-start(bf16[128,227]{1,0:T(8,128)(2,1)S(1)} %convolution_convert_fusion), channel_id=1, source_target_pairs={{1,2},{3,4},{5,6},{7,8},{9,10},{11,12},{13,14},{15,0},{2,1},{4,3},... | collective-permute-start | bytes 174344 | tf_op jit(solution)/shard_map/ppermute | solution.py:438
  9.9 8.6 %collective-permute-start.4 = (bf16[128,227]{1,0:T(8,128)(2,1)S(1)}, bf16[128,227]{1,0:T(8,128)(2,1)S(1)}, u32[]{:S(2)}, u32[]{:S(2)}) collective-permute-start(bf16[128,227]{1,0:T(8,128)(2,1)S(1)} %convolution_convert_fusion), channel_id=1, source_target_pairs={{16,32},{48,64},{80,96},{32,16},{64,48},{96,80},{17,33},{49,65},{8... | collective-permute-start | bytes 174344 | tf_op jit(solution)/shard_map/ppermute | solution.py:428
  13.7 6.5 %collective-permute-start.5 = (bf16[256,227]{1,0:T(8,128)(2,1)S(1)}, bf16[256,227]{1,0:T(8,128)(2,1)S(1)}, u32[]{:S(2)}, u32[]{:S(2)}) collective-permute-start(bf16[256,227]{1,0:T(8,128)(2,1)S(1)} %constant_dynamic-update-slice_fusion), channel_id=1, source_target_pairs={{16,32},{48,64},{80,96},{32,16},{64,48},{96,80},{17,33},{49,65},{8... | collective-permute-start | bytes 348680 | tf_op jit(solution)/shard_map/ppermute | solution.py:428
  25.4 7.9 %collective-permute-start.8 = (bf16[128,512]{1,0:T(8,128)(2,1)S(1)}, bf16[128,512]{1,0:T(8,128)(2,1)S(1)}, u32[]{:S(2)}, u32[]{:S(2)}) collective-permute-start(bf16[128,512]{1,0:T(8,128)(2,1)S(1)} %get-tuple-element.46), channel_id=1, source_target_pairs={{1,2},{3,4},{5,6},{7,8},{9,10},{11,12},{13,14},{15,0},{2,1},{4,3},... | collective-permute-start | bytes 393224 | tf_op jit(solution)/shard_map/ppermute | solution.py:438
  28.5 4.9 %collective-permute-start.7 = (bf16[128,512]{1,0:T(8,128)(2,1)S(1)}, bf16[128,512]{1,0:T(8,128)(2,1)S(1)}, u32[]{:S(2)}, u32[]{:S(2)}) collective-permute-start(bf16[128,512]{1,0:T(8,128)(2,1)S(1)} %get-tuple-element.46), channel_id=1, source_target_pairs={{0,1},{1,0},{2,3},{3,2},{4,5},{5,4},{6,7},{7,6},{8,9},{9,8},{10,11... | collective-permute-start | bytes 393224 | tf_op jit(solution)/shard_map/ppermute | solution.py:419
  28.5 4.9 %collective-permute-start.6 = (bf16[128,512]{1,0:T(8,128)(2,1)S(1)}, bf16[128,512]{1,0:T(8,128)(2,1)S(1)}, u32[]{:S(2)}, u32[]{:S(2)}) collective-permute-start(bf16[128,512]{1,0:T(8,128)(2,1)S(1)} %get-tuple-element.46), channel_id=1, source_target_pairs={{0,16},{16,0},{32,48},{48,32},{64,80},{80,64},{96,112},{112,96},{1... | collective-permute-start | bytes 393224 | tf_op jit(solution)/shard_map/ppermute | solution.py:419
  29.1 9.5 %collective-permute-start.10 = (bf16[128,512]{1,0:T(8,128)(2,1)S(1)}, bf16[128,512]{1,0:T(8,128)(2,1)S(1)}, u32[]{:S(2)}, u32[]{:S(2)}) collective-permute-start(bf16[128,512]{1,0:T(8,128)(2,1)S(1)} %get-tuple-element.46), channel_id=1, source_target_pairs={{16,32},{48,64},{80,96},{32,16},{64,48},{96,80},{17,33},{49,65},{8... | collective-permute-start | bytes 393224 | tf_op jit(solution)/shard_map/ppermute | solution.py:428
  33.4 8.6 %collective-permute-start.11 = (bf16[256,512]{1,0:T(8,128)(2,1)S(1)}, bf16[256,512]{1,0:T(8,128)(2,1)S(1)}, u32[]{:S(2)}, u32[]{:S(2)}) collective-permute-start(bf16[256,512]{1,0:T(8,128)(2,1)S(1)} %constant_dynamic-update-slice_fusion.2), channel_id=1, source_target_pairs={{16,32},{48,64},{80,96},{32,16},{64,48},{96,80},{17,33},{49,65},{8... | collective-permute-start | bytes 786440 | tf_op jit(solution)/shard_map/ppermute | solution.py:428
  48.3 7.8 %collective-permute-start.12 = (bf16[384,512]{1,0:T(8,128)(2,1)S(1)}, bf16[384,512]{1,0:T(8,128)(2,1)S(1)}, u32[]{:S(2)}, u32[]{:S(2)}) collective-permute-start(bf16[384,512]{1,0:T(8,128)(2,1)S(1)} %get-tuple-element.60), channel_id=1, source_target_pairs={{0,16},{16,0},{32,48},{48,32},{64,80},{80,64},{96,112},{112,96},{1... | collective-permute-start | bytes 1179656 | tf_op jit(solution)/shard_map/ppermute | solution.py:419
  48.4 7.7 %collective-permute-start.13 = (bf16[256,512]{1,0:T(8,128)(2,1)S(1)}, bf16[256,512]{1,0:T(8,128)(2,1)S(1)}, u32[]{:S(2)}, u32[]{:S(2)}) collective-permute-start(bf16[256,512]{1,0:T(8,128)(2,1)S(1)} %get-tuple-element.62), channel_id=1, source_target_pairs={{16,32},{48,64},{80,96},{32,16},{64,48},{96,80},{17,33},{49,65},{8... | collective-permute-start | bytes 786440 | tf_op jit(solution)/shard_map/ppermute | solution.py:428
  52.1 8.7 %collective-permute-start.16 = (bf16[128,512]{1,0:T(8,128)(2,1)S(1)}, bf16[128,512]{1,0:T(8,128)(2,1)S(1)}, u32[]{:S(2)}, u32[]{:S(2)}) collective-permute-start(bf16[128,512]{1,0:T(8,128)(2,1)S(1)} %get-tuple-element.63), channel_id=1, source_target_pairs={{16,32},{48,64},{80,96},{32,16},{64,48},{96,80},{17,33},{49,65},{8... | collective-permute-start | bytes 393224 | tf_op jit(solution)/shard_map/ppermute | solution.py:428
  56.2 7.2 %collective-permute-start.15 = (bf16[128,512]{1,0:T(8,128)(2,1)S(1)}, bf16[128,512]{1,0:T(8,128)(2,1)S(1)}, u32[]{:S(2)}, u32[]{:S(2)}) collective-permute-start(bf16[128,512]{1,0:T(8,128)(2,1)S(1)} %get-tuple-element.80), channel_id=1, source_target_pairs={{1,2},{3,4},{5,6},{7,8},{9,10},{11,12},{13,14},{15,0},{2,1},{4,3},... | collective-permute-start | bytes 393224 | tf_op jit(solution)/shard_map/ppermute | solution.py:438
  70.1 6.1 %collective-permute-start.18 = (bf16[160,512]{1,0:T(8,128)(2,1)S(1)}, bf16[160,512]{1,0:T(8,128)(2,1)S(1)}, u32[]{:S(2)}, u32[]{:S(2)}) collective-permute-start(bf16[160,512]{1,0:T(8,128)(2,1)S(1)} %get-tuple-element.82), channel_id=1, source_target_pairs={{0,32},{1,33},{2,34},{3,35},{4,36},{5,37},{6,38},{7,39},{8,40},{9,... | collective-permute-start | bytes 491528 | tf_op jit(solution)/shard_map/ppermute | solution.py:468
  73.5 7.5 %collective-permute-start.20 = (bf16[160,512]{1,0:T(8,128)(2,1)S(1)}, bf16[160,512]{1,0:T(8,128)(2,1)S(1)}, u32[]{:S(2)}, u32[]{:S(2)}) collective-permute-start(bf16[160,512]{1,0:T(8,128)(2,1)S(1)} %get-tuple-element.83), channel_id=1, source_target_pairs={{0,36},{1,37},{2,38},{3,39},{4,32},{5,33},{6,34},{7,35},{8,44},{9,... | collective-permute-start | bytes 491528 | tf_op jit(solution)/shard_map/ppermute | solution.py:468
  73.5 7.5 %collective-permute-start.19 = (bf16[160,512]{1,0:T(8,128)(2,1)S(1)}, bf16[160,512]{1,0:T(8,128)(2,1)S(1)}, u32[]{:S(2)}, u32[]{:S(2)}) collective-permute-start(bf16[160,512]{1,0:T(8,128)(2,1)S(1)} %get-tuple-element.84), channel_id=1, source_target_pairs={{0,4},{1,5},{2,6},{3,7},{4,0},{5,1},{6,2},{7,3},{8,12},{9,13},{10,... | collective-permute-start | bytes 491528 | tf_op jit(solution)/shard_map/ppermute | solution.py:468
  81.1 6.7 %collective-permute-start.23 = (bf16[160,512]{1,0:T(8,128)(2,1)S(1)}, bf16[160,512]{1,0:T(8,128)(2,1)S(1)}, u32[]{:S(2)}, u32[]{:S(2)}) collective-permute-start(bf16[160,512]{1,0:T(8,128)(2,1)S(1)} %add_convert_fusion.3), channel_id=1, source_target_pairs={{0,97},{1,96},{2,99},{3,98},{4,101},{5,100},{6,103},{7,102},{8,105... | collective-permute-start | bytes 491528 | tf_op jit(solution)/shard_map/ppermute | solution.py:468
  84.6 5.4 %collective-permute-start.21 = (bf16[160,512]{1,0:T(8,128)(2,1)S(1)}, bf16[160,512]{1,0:T(8,128)(2,1)S(1)}, u32[]{:S(2)}, u32[]{:S(2)}) collective-permute-start(bf16[160,512]{1,0:T(8,128)(2,1)S(1)} %add_convert_fusion.3), channel_id=1, source_target_pairs={{0,1},{1,0},{2,3},{3,2},{4,5},{5,4},{6,7},{7,6},{8,9},{9,8},{10,11... | collective-permute-start | bytes 491528 | tf_op jit(solution)/shard_map/ppermute | solution.py:468
  90.1 5.3 %collective-permute-start.26 = (bf16[160,512]{1,0:T(8,128)(2,1)S(1)}, bf16[160,512]{1,0:T(8,128)(2,1)S(1)}, u32[]{:S(2)}, u32[]{:S(2)}) collective-permute-start(bf16[160,512]{1,0:T(8,128)(2,1)S(1)} %add_convert_fusion.2), channel_id=1, source_target_pairs={{0,15},{1,14},{2,13},{3,12},{4,11},{5,10},{6,9},{7,8},{8,7},{9,6},... | collective-permute-start | bytes 491528 | tf_op jit(solution)/shard_map/ppermute | solution.py:468
  90.2 6.0 %collective-permute-start.25 = (bf16[160,512]{1,0:T(8,128)(2,1)S(1)}, bf16[160,512]{1,0:T(8,128)(2,1)S(1)}, u32[]{:S(2)}, u32[]{:S(2)}) collective-permute-start(bf16[160,512]{1,0:T(8,128)(2,1)S(1)} %add_convert_fusion.2), channel_id=1, source_target_pairs={{0,3},{1,2},{2,1},{3,0},{4,7},{5,6},{6,5},{7,4},{8,11},{9,10},{10,... | collective-permute-start | bytes 491528 | tf_op jit(solution)/shard_map/ppermute | solution.py:468
  90.2 5.9 %collective-permute-start.24 = (bf16[160,512]{1,0:T(8,128)(2,1)S(1)}, bf16[160,512]{1,0:T(8,128)(2,1)S(1)}, u32[]{:S(2)}, u32[]{:S(2)}) collective-permute-start(bf16[160,512]{1,0:T(8,128)(2,1)S(1)} %add_convert_fusion.2), channel_id=1, source_target_pairs={{0,12},{1,13},{2,14},{3,15},{4,8},{5,9},{6,10},{7,11},{8,4},{9,5},... | collective-permute-start | bytes 491528 | tf_op jit(solution)/shard_map/ppermute | solution.py:468
  96.2 7.7 %collective-permute-start.29 = (bf16[160,512]{1,0:T(8,128)(2,1)S(1)}, bf16[160,512]{1,0:T(8,128)(2,1)S(1)}, u32[]{:S(2)}, u32[]{:S(2)}) collective-permute-start(bf16[160,512]{1,0:T(8,128)(2,1)S(1)} %add_convert_fusion.1), channel_id=1, source_target_pairs={{0,36},{1,37},{2,38},{3,39},{4,32},{5,33},{6,34},{7,35},{8,44},{9,... | collective-permute-start | bytes 491528 | tf_op jit(solution)/shard_map/ppermute | solution.py:468
  99.1 6.5 %collective-permute-start.28 = (bf16[160,512]{1,0:T(8,128)(2,1)S(1)}, bf16[160,512]{1,0:T(8,128)(2,1)S(1)}, u32[]{:S(2)}, u32[]{:S(2)}) collective-permute-start(bf16[160,512]{1,0:T(8,128)(2,1)S(1)} %add_convert_fusion.1), channel_id=1, source_target_pairs={{0,4},{1,5},{2,6},{3,7},{4,0},{5,1},{6,2},{7,3},{8,12},{9,13},{10,... | collective-permute-start | bytes 491528 | tf_op jit(solution)/shard_map/ppermute | solution.py:468
  100.9 5.5 %collective-permute-start.27 = (bf16[160,512]{1,0:T(8,128)(2,1)S(1)}, bf16[160,512]{1,0:T(8,128)(2,1)S(1)}, u32[]{:S(2)}, u32[]{:S(2)}) collective-permute-start(bf16[160,512]{1,0:T(8,128)(2,1)S(1)} %add_convert_fusion.1), channel_id=1, source_target_pairs={{0,32},{1,33},{2,34},{3,35},{4,36},{5,37},{6,38},{7,39},{8,40},{9,... | collective-permute-start | bytes 491528 | tf_op jit(solution)/shard_map/ppermute | solution.py:468
  106.5 6.2 %collective-permute-start.30 = (bf16[640,512]{1,0:T(8,128)(2,1)S(1)}, bf16[640,512]{1,0:T(8,128)(2,1)S(1)}, u32[]{:S(2)}, u32[]{:S(2)}) collective-permute-start(bf16[640,512]{1,0:T(8,128)(2,1)S(1)} %pad_maximum_fusion.mine), channel_id=1, source_target_pairs={{0,16},{16,0},{32,48},{48,32},{64,80},{80,64},{96,112},{112,96},{1... | collective-permute-start | bytes 1966088 | tf_op jit(solution)/shard_map/ppermute | solution.py:419
  (28 other events, 177.0 us)

commit v6 on v5

--- a/solution.py
+++ b/solution.py
@@ -136,8 +136,8 @@
     picked,
     inputs,
     hidden,
-    pre_slope,
-    mix_slope,
+    pre_kept,
+    mix_kept,
     normed_all,
     scale_all,
     update_normed,
@@ -166,11 +166,11 @@
         inputs[here, :] = dot(send_hot[here, :], table[pl.ds(start, own), :]).astype(bf16)
     pre = dot(inputs[...], grid_weight[...])
     gate = sigmoid(pre)
-    pre_slope[...] = (gate * (1.0 + pre * (1.0 - gate))).astype(bf16)
+    pre_kept[...] = pre.astype(bf16)
     hidden[...] = (pre * gate).astype(bf16)
     mix = dot(hidden[...], sender_weight[...]) + dot(receive_hot[...], projected[...])
     gate = sigmoid(mix)
-    mix_slope[...] = (gate * (1.0 + mix * (1.0 - gate))).astype(bf16)
+    mix_kept[...] = mix.astype(bf16)
     product = dot((mix * gate).astype(bf16), message_weight[...])
     normed, scale = normalise(product)
     normed_all[...] = normed.astype(bf16)
@@ -265,16 +265,35 @@
 
 
 def edge_kernel(
-    sender_rows, mix_grads, place_hot, edge_receiver, cotangent, edge_grad, state_part
+    sender_rows,
+    mix_grads,
+    place_hot,
+    edge_receiver,
+    cotangent,
+    ends,
+    pre_kept,
+    mix_kept,
+    edge_grad,
+    state_part,
+    receive_hot,
+    pre_slope,
+    mix_slope,
 ):
+    for block in range(ends.shape[0]):
+        here = slice(block * lanes, (block + 1) * lanes)
+        receive_hot[here, :] = lane_hot(ends[block : block + 1, :], receive_hot.shape[1])
     edge_grad[...] = cross_dot(sender_rows[...], mix_grads[...]).astype(bf16)
     receiver_grad = dot(place_hot[...], mix_grads[...]).astype(bf16)
     state_part[...] = cotangent[...].astype(f32) + back_dot(receiver_grad, edge_receiver[...])
+    for kept, slope in ((pre_kept, pre_slope), (mix_kept, mix_slope)):
+        value = kept[...].astype(f32)
+        gate = sigmoid(value)
+        slope[...] = (gate * (1.0 + value * (1.0 - gate))).astype(bf16)
 
 
 def encode_back_kernel(
     place_ref,
-    ends,
+    receive_hot,
     export,
     state_part,
     own_grad,
@@ -311,11 +330,8 @@
     upstream[0:nodes, :] = back_dot(update_grad.astype(bf16), update_weight[...]).astype(bf16)
     upstream[nodes:, :] = jnp.zeros_like(upstream[nodes:, :])
     variables = inputs.shape[1]
-    grads[width : 2 * width, :] = edge_grad[...].astype(f32)
-    grads[2 * width :, :] = jnp.zeros_like(grads[2 * width :, :])
-
-    received = [lane_hot(ends[block : block + 1, :], 256) for block in range(ends.shape[0])]
-    arriving = dot(jnp.concatenate(received, 0), upstream[...])
+    grads[width:, :] = jnp.zeros_like(grads[width:, :])
+    arriving = dot(receive_hot[...], upstream[...])
     product_grad = norm_back(
         normed_all[...].astype(f32), scale_all[:, 0:1], arriving
     ).astype(bf16)
@@ -323,10 +339,10 @@
     mix_grad = mix_grad.astype(bf16)
     grads[0:width, :] = cross_dot(hidden[...], mix_grad)
     pre_grad = back_dot(mix_grad, sender_weight[...]) * pre_slope[...].astype(f32)
-    grads[2 * width : 2 * width + variables, :] = cross_dot(
+    grads[width : width + variables, :] = cross_dot(
         inputs[...], pre_grad.astype(bf16)
     )
-    arrange(place_ref, grads, given, kept)
+    arrange(place_ref, grads, edge_grad, given, kept)
 
 
 def owner(place_ref, side, turn):
@@ -337,14 +353,14 @@
     return pl.ds(pl.multiple_of(first + block * count, 32), count)
 
 
-def arrange(place_ref, grads, given, kept):
+def arrange(place_ref, grads, edge_grad, given, kept):
     width = grads.shape[1]
     for side, target in ((1, given), (0, kept)):
         for turn in range(4):
             block = owner(place_ref, side, turn)
             first = turn * 160
-            for count, base in ((64, 0), (64, width), (32, 2 * width)):
-                rows = grads[rows_of(block, count, base), :]
+            for count, source, base in ((64, grads, 0), (64, edge_grad, 0), (32, grads, width)):
+                rows = source[rows_of(block, count, base), :]
                 target[first : first + count, :] = rows.astype(bf16)
                 first += count
 
@@ -550,7 +566,7 @@
         16,
         30,
     )
-    state, picked, inputs, hidden, pre_slope, mix_slope, normed, scale, *update = call(
+    state, picked, inputs, hidden, pre_kept, mix_kept, normed, scale, *update = call(
         encode_kernel,
         (
             place,
@@ -654,10 +670,11 @@
         for side in (0, 1)
     ]
     from_close, from_far = close(to_close), far(to_far)
-    edge_grad, state_part = call(
+    edge_grad, state_part, receive_hot, pre_slope, mix_slope = call(
         edge_kernel,
-        (sender_rows, mix_grad, process_place, edge_receiver, cotangent),
-        [((width, width), bf16, 0), ((nodes, width), f32, 0)],
+        (sender_rows, mix_grad, process_place, edge_receiver, cotangent, ends, pre_kept, mix_kept),
+        [((width, width), bf16, 0), ((nodes, width), f32, 0), ((edges, 256), bf16, 0)]
+        + [((edges, width), bf16, 0)] * 2,
         [],
         0,
         16,
@@ -666,7 +683,7 @@
         encode_back_kernel,
         (
             place,
-            ends,
+            receive_hot,
             export,
             state_part,
             own_grad,
@@ -690,7 +707,7 @@
             edge_grad,
         ),
         [((640, width), bf16, 0)] * 2,
-        [((256, width), bf16), ((1280, width), f32)],
+        [((256, width), bf16), ((768, width), f32)],
         1,
         16,
     )

time: 115 us -> 115 us (level)
  waiting for transfers between devices: 30.6 us -> 28.5 us
  Pallas kernels: 20.4 us -> 22.3 us
    ppermute x3, waiting for transfers between devices: 2.93 us -> 0.68 us  [far(): lax.ppermute(x, 'lon', [(i, (i + 1) % size) for i in ends] + [((i + 1) %...]
    pallas_call x8, Pallas kernels: 20.4 us -> 22.3 us  [call(): pl.pallas_call(kernel, out_shape=[jax.ShapeDtypeStruct(shape, dtype) for...]
  transfers between devices with their start and end apart: 31 -> 31, of which waited for: 17 -> 17; matrix products, arithmetic and copies ran while one was open for 0% -> 0% of each run, Pallas kernels for 3% -> 5%
where the time goes in v6:
time: 115 us
  starting transfers between devices  58.2 us (51%)
  waiting for transfers between devices  28.5 us (25%)
  Pallas kernels  22.3 us (19%)
  between operations  2.66 us (2%)
  matrix products  1.19 us (1%)
    pallas_call x8, Pallas kernels, call(): pl.pallas_call(kernel, out_shape=[jax.ShapeDtypeStruct(shape, dtype) for...  22.3 us
    ppermute x6, starting transfers between devices, outer(): lax.ppermute(x, 'lat', [(i, i + 1) for i in ends] + [(i + 1, i) for i in...  20.9 us
    ppermute x12, waiting for transfers between devices, met(): return lax.ppermute(x, ('lat', 'lon'), pairs)  18.3 us
    ppermute x12, starting transfers between devices, met(): return lax.ppermute(x, ('lat', 'lon'), pairs)  17.7 us
    ppermute x3, starting transfers between devices, far(): lax.ppermute(x, 'lon', [(i, (i + 1) % size) for i in ends] + [((i + 1) %...  13.8 us
    ppermute x6, waiting for transfers between devices, outer(): lax.ppermute(x, 'lat', [(i, i + 1) for i in ends] + [(i + 1, i) for i in...  7.27 us
    ppermute x10, starting transfers between devices, partner(): lax.ppermute(x, axis, [(i, i ^ flip) for i in range(lax.axis_size(axis))])  5.87 us
  transfers between devices with their start and end apart: 31, of which 17 were waited for; matrix products, arithmetic and copies ran while one was open for 0% of the time, Pallas kernels for 5%

profile of v6, /device:TPU:1, one launch (start us, length us, event | category | flops | bytes accessed | tf_op | source)
XLA Modules:
  0.0 114.5 jit_solution(13228157257900751711)
XLA Ops:
  1.8 7.1 %collective-permute-start.2 = (bf16[128,227]{1,0:T(8,128)(2,1)S(1)}, bf16[128,227]{1,0:T(8,128)(2,1)S(1)}, u32[]{:S(2)}, u32[]{:S(2)}) collective-permute-start(bf16[128,227]{1,0:T(8,128)(2,1)S(1)} %convolution_convert_fusion), channel_id=1, source_target_pairs={{1,2},{3,4},{5,6},{7,8},{9,10},{11,12},{13,14},{15,0},{2,1},{4,3},... | collective-permute-start | bytes 174344 | tf_op jit(solution)/shard_map/ppermute | solution.py:454
  9.9 3.0 %collective-permute-start.4 = (bf16[128,227]{1,0:T(8,128)(2,1)S(1)}, bf16[128,227]{1,0:T(8,128)(2,1)S(1)}, u32[]{:S(2)}, u32[]{:S(2)}) collective-permute-start(bf16[128,227]{1,0:T(8,128)(2,1)S(1)} %convolution_convert_fusion), channel_id=1, source_target_pairs={{16,32},{48,64},{80,96},{32,16},{64,48},{96,80},{17,33},{49,65},{8... | collective-permute-start | bytes 174344 | tf_op jit(solution)/shard_map/ppermute | solution.py:444
  13.7 3.8 %collective-permute-start.5 = (bf16[256,227]{1,0:T(8,128)(2,1)S(1)}, bf16[256,227]{1,0:T(8,128)(2,1)S(1)}, u32[]{:S(2)}, u32[]{:S(2)}) collective-permute-start(bf16[256,227]{1,0:T(8,128)(2,1)S(1)} %constant_dynamic-update-slice_fusion), channel_id=1, source_target_pairs={{16,32},{48,64},{80,96},{32,16},{64,48},{96,80},{17,33},{49,65},{8... | collective-permute-start | bytes 348680 | tf_op jit(solution)/shard_map/ppermute | solution.py:444
  20.4 4.6 %shard_map.256 = (bf16[160,512]{1,0:T(8,128)(2,1)S(1)}, bf16[128,512]{1,0:T(8,128)(2,1)S(1)}, bf16[1024,227]{1,0:T(8,128)(2,1)S(1)}, bf16[1024,512]{1,0:T(8,128)...) custom-call(s32[4]{0:T(128)S(1)} %pad_add_fusion.place_ref, ...), custom_call_target="tpu_custom_call" | custom-call | flops 4294967296 | bytes 8388608 | tf_op jit(solution)/shard_map/pallas_call | solution.py:421
  25.0 3.1 %collective-permute-start.8 = (bf16[128,512]{1,0:T(8,128)(2,1)S(1)}, bf16[128,512]{1,0:T(8,128)(2,1)S(1)}, u32[]{:S(2)}, u32[]{:S(2)}) collective-permute-start(bf16[128,512]{1,0:T(8,128)(2,1)S(1)} %get-tuple-element.49), channel_id=1, source_target_pairs={{1,2},{3,4},{5,6},{7,8},{9,10},{11,12},{13,14},{15,0},{2,1},{4,3},... | collective-permute-start | bytes 393224 | tf_op jit(solution)/shard_map/ppermute | solution.py:454
  28.8 3.9 %collective-permute-start.10 = (bf16[128,512]{1,0:T(8,128)(2,1)S(1)}, bf16[128,512]{1,0:T(8,128)(2,1)S(1)}, u32[]{:S(2)}, u32[]{:S(2)}) collective-permute-start(bf16[128,512]{1,0:T(8,128)(2,1)S(1)} %get-tuple-element.49), channel_id=1, source_target_pairs={{16,32},{48,64},{80,96},{32,16},{64,48},{96,80},{17,33},{49,65},{8... | collective-permute-start | bytes 393224 | tf_op jit(solution)/shard_map/ppermute | solution.py:444
  33.0 4.6 %collective-permute-start.11 = (bf16[256,512]{1,0:T(8,128)(2,1)S(1)}, bf16[256,512]{1,0:T(8,128)(2,1)S(1)}, u32[]{:S(2)}, u32[]{:S(2)}) collective-permute-start(bf16[256,512]{1,0:T(8,128)(2,1)S(1)} %constant_dynamic-update-slice_fusion.2), channel_id=1, source_target_pairs={{16,32},{48,64},{80,96},{32,16},{64,48},{96,80},{17,33},{49,65},{8... | collective-permute-start | bytes 786440 | tf_op jit(solution)/shard_map/ppermute | solution.py:444
  38.3 3.3 %collective-permute-done.11.near_outer_sides = bf16[256,512]{1,0:T(8,128)(2,1)S(1)} collective-permute-done((bf16[256,512]{1,0:T(8,128)(2,1)S(1)}, bf16[256,512]{1,0:T(8,128)(2,1)S(1)}, u32[]{:S(2)}, u32[]{:S(2)}) %collective-permute-start.11) | collective-permute-done | bytes 262176 | tf_op jit(solution)/shard_map/ppermute | solution.py:444
  41.7 6.3 %shard_map.258 = (bf16[160,512]{1,0:T(8,128)(2,1)}, f32[160,512]{1,0:T(8,128)S(1)}, bf16[256,512]{1,0:T(8,128)(2,1)S(1)}, bf16[384,512]{1,0:T(8,128)(2,1)S(1)}, ...) custom-call(s32[4]{0:T(128)S(1)} %pad_add_fusion.place_ref, ...), custom_call_target="tpu_custom_call" | custom-call | flops 4294967296 | bytes 8388608 | tf_op jit(solution)/shard_map/pallas_call | solution.py:421
  48.1 3.7 %collective-permute-start.13 = (bf16[256,512]{1,0:T(8,128)(2,1)S(1)}, bf16[256,512]{1,0:T(8,128)(2,1)S(1)}, u32[]{:S(2)}, u32[]{:S(2)}) collective-permute-start(bf16[256,512]{1,0:T(8,128)(2,1)S(1)} %get-tuple-element.68), channel_id=1, source_target_pairs={{16,32},{48,64},{80,96},{32,16},{64,48},{96,80},{17,33},{49,65},{8... | collective-permute-start | bytes 786440 | tf_op jit(solution)/shard_map/ppermute | solution.py:444
  53.7 2.1 %collective-permute-done.13 = bf16[256,512]{1,0:T(8,128)(2,1)S(1)} collective-permute-done((bf16[256,512]{1,0:T(8,128)(2,1)S(1)}, bf16[256,512]{1,0:T(8,128)(2,1)S(1)}, u32[]{:S(2)}, u32[]{:S(2)}) %collective-permute-start.13) | collective-permute-done | bytes 262176 | tf_op jit(solution)/shard_map/ppermute | solution.py:444
  55.9 3.6 %collective-permute-start.15 = (bf16[128,512]{1,0:T(8,128)(2,1)S(1)}, bf16[128,512]{1,0:T(8,128)(2,1)S(1)}, u32[]{:S(2)}, u32[]{:S(2)}) collective-permute-start(bf16[128,512]{1,0:T(8,128)(2,1)S(1)} %get-tuple-element.86), channel_id=1, source_target_pairs={{1,2},{3,4},{5,6},{7,8},{9,10},{11,12},{13,14},{15,0},{2,1},{4,3},... | collective-permute-start | bytes 393224 | tf_op jit(solution)/shard_map/ppermute | solution.py:454
  59.5 3.4 %shard_map.259 = (bf16[512,512]{1,0:T(8,128)(2,1)S(1)}, f32[160,512]{1,0:T(8,128)S(1)}, bf16[1024,256]{1,0:T(8,128)(2,1)S(1)}, bf16[1024,512]{1,0:T(8,128)(2,1)S(1)}, bf16[1024,512]{1,0:T(8,128)(2,1)S(1)}) custom-call(bf16[1024,512]{1,0:T(8,128)(2,1)S(1)} %get-tuple-element.59.sender_rows, bf16[1024,512]{1,0:T(8,128)(2,1)S(1)} %get-tuple-element.60.mix_grads, ...), custom_call_target="tpu_custom_call" | custom-call | flops 4294967296 | bytes 8388608 | tf_op jit(solution)/shard_map/pallas_call | solution.py:421
  63.3 4.2 %shard_map.260 = (bf16[640,512]{1,0:T(8,128)(2,1)S(1)}, bf16[640,512]{1,0:T(8,128)(2,1)S(1)}) custom-call(s32[4]{0:T(128)S(1)} %pad_add_fusion.place_ref, bf16[1024,256]{1,0:T(8,128)(2,1)S(1)} %get-tuple-element.63.receive_hot, s32[1,128]{1,0:T(1,128)S(1)} %bitcast.14, f32[160,512]{1,0:T(8,128)S(1)} %get-tuple-element.64.state_part, ...), custom_call_target="tpu_custom_call" | custom-call | flops 4294967296 | bytes 8388608 | tf_op jit(solution)/shard_map/pallas_call | solution.py:421
  69.9 3.4 %collective-permute-start.18 = (bf16[160,512]{1,0:T(8,128)(2,1)S(1)}, bf16[160,512]{1,0:T(8,128)(2,1)S(1)}, u32[]{:S(2)}, u32[]{:S(2)}) collective-permute-start(bf16[160,512]{1,0:T(8,128)(2,1)S(1)} %get-tuple-element.88), channel_id=1, source_target_pairs={{0,32},{1,33},{2,34},{3,35},{4,36},{5,37},{6,38},{7,39},{8,40},{9,... | collective-permute-start | bytes 491528 | tf_op jit(solution)/shard_map/ppermute | solution.py:484
  73.3 2.5 %collective-permute-start.19 = (bf16[160,512]{1,0:T(8,128)(2,1)S(1)}, bf16[160,512]{1,0:T(8,128)(2,1)S(1)}, u32[]{:S(2)}, u32[]{:S(2)}) collective-permute-start(bf16[160,512]{1,0:T(8,128)(2,1)S(1)} %get-tuple-element.90), channel_id=1, source_target_pairs={{0,4},{1,5},{2,6},{3,7},{4,0},{5,1},{6,2},{7,3},{8,12},{9,13},{10,... | collective-permute-start | bytes 491528 | tf_op jit(solution)/shard_map/ppermute | solution.py:484
  76.1 4.8 %collective-permute-done.20 = bf16[160,512]{1,0:T(8,128)(2,1)S(1)} collective-permute-done((bf16[160,512]{1,0:T(8,128)(2,1)S(1)}, bf16[160,512]{1,0:T(8,128)(2,1)S(1)}, u32[]{:S(2)}, u32[]{:S(2)}) %collective-permute-start.20) | collective-permute-done | bytes 163872 | tf_op jit(solution)/shard_map/ppermute | solution.py:484
  80.9 3.5 %collective-permute-start.23 = (bf16[160,512]{1,0:T(8,128)(2,1)S(1)}, bf16[160,512]{1,0:T(8,128)(2,1)S(1)}, u32[]{:S(2)}, u32[]{:S(2)}) collective-permute-start(bf16[160,512]{1,0:T(8,128)(2,1)S(1)} %add_convert_fusion.3), channel_id=1, source_target_pairs={{0,97},{1,96},{2,99},{3,98},{4,101},{5,100},{6,103},{7,102},{8,105... | collective-permute-start | bytes 491528 | tf_op jit(solution)/shard_map/ppermute | solution.py:484
  84.9 2.7 %collective-permute-done.23 = bf16[160,512]{1,0:T(8,128)(2,1)S(1)} collective-permute-done((bf16[160,512]{1,0:T(8,128)(2,1)S(1)}, bf16[160,512]{1,0:T(8,128)(2,1)S(1)}, u32[]{:S(2)}, u32[]{:S(2)}) %collective-permute-start.23) | collective-permute-done | bytes 163872 | tf_op jit(solution)/shard_map/ppermute | solution.py:484
  90.1 2.5 %collective-permute-start.24 = (bf16[160,512]{1,0:T(8,128)(2,1)S(1)}, bf16[160,512]{1,0:T(8,128)(2,1)S(1)}, u32[]{:S(2)}, u32[]{:S(2)}) collective-permute-start(bf16[160,512]{1,0:T(8,128)(2,1)S(1)} %add_convert_fusion.2), channel_id=1, source_target_pairs={{0,12},{1,13},{2,14},{3,15},{4,8},{5,9},{6,10},{7,11},{8,4},{9,5},... | collective-permute-start | bytes 491528 | tf_op jit(solution)/shard_map/ppermute | solution.py:484
  92.6 2.5 %collective-permute-done.26 = bf16[160,512]{1,0:T(8,128)(2,1)S(1)} collective-permute-done((bf16[160,512]{1,0:T(8,128)(2,1)S(1)}, bf16[160,512]{1,0:T(8,128)(2,1)S(1)}, u32[]{:S(2)}, u32[]{:S(2)}) %collective-permute-start.26) | collective-permute-done | bytes 163872 | tf_op jit(solution)/shard_map/ppermute | solution.py:484
  96.1 2.8 %collective-permute-start.29 = (bf16[160,512]{1,0:T(8,128)(2,1)S(1)}, bf16[160,512]{1,0:T(8,128)(2,1)S(1)}, u32[]{:S(2)}, u32[]{:S(2)}) collective-permute-start(bf16[160,512]{1,0:T(8,128)(2,1)S(1)} %add_convert_fusion.1), channel_id=1, source_target_pairs={{0,36},{1,37},{2,38},{3,39},{4,32},{5,33},{6,34},{7,35},{8,44},{9,... | collective-permute-start | bytes 491528 | tf_op jit(solution)/shard_map/ppermute | solution.py:484
  101.2 2.5 %collective-permute-done.29 = bf16[160,512]{1,0:T(8,128)(2,1)S(1)} collective-permute-done((bf16[160,512]{1,0:T(8,128)(2,1)S(1)}, bf16[160,512]{1,0:T(8,128)(2,1)S(1)}, u32[]{:S(2)}, u32[]{:S(2)}) %collective-permute-start.29) | collective-permute-done | bytes 163872 | tf_op jit(solution)/shard_map/ppermute | solution.py:484
  106.3 4.6 %collective-permute-start.30 = (bf16[640,512]{1,0:T(8,128)(2,1)S(1)}, bf16[640,512]{1,0:T(8,128)(2,1)S(1)}, u32[]{:S(2)}, u32[]{:S(2)}) collective-permute-start(bf16[640,512]{1,0:T(8,128)(2,1)S(1)} %pad_maximum_fusion.mine), channel_id=1, source_target_pairs={{0,16},{16,0},{32,48},{48,32},{64,80},{80,64},{96,112},{112,96},{1... | collective-permute-start | bytes 1966088 | tf_op jit(solution)/shard_map/ppermute | solution.py:435
  (101 shorter events, 23.3 us)
Async XLA Ops:
  1.8 11.7 %collective-permute-start.2 = (bf16[128,227]{1,0:T(8,128)(2,1)S(1)}, bf16[128,227]{1,0:T(8,128)(2,1)S(1)}, u32[]{:S(2)}, u32[]{:S(2)}) collective-permute-start(bf16[128,227]{1,0:T(8,128)(2,1)S(1)} %convolution_convert_fusion), channel_id=1, source_target_pairs={{1,2},{3,4},{5,6},{7,8},{9,10},{11,12},{13,14},{15,0},{2,1},{4,3},... | collective-permute-start | bytes 174344 | tf_op jit(solution)/shard_map/ppermute | solution.py:454
  9.9 8.6 %collective-permute-start.4 = (bf16[128,227]{1,0:T(8,128)(2,1)S(1)}, bf16[128,227]{1,0:T(8,128)(2,1)S(1)}, u32[]{:S(2)}, u32[]{:S(2)}) collective-permute-start(bf16[128,227]{1,0:T(8,128)(2,1)S(1)} %convolution_convert_fusion), channel_id=1, source_target_pairs={{16,32},{48,64},{80,96},{32,16},{64,48},{96,80},{17,33},{49,65},{8... | collective-permute-start | bytes 174344 | tf_op jit(solution)/shard_map/ppermute | solution.py:444
  13.7 6.5 %collective-permute-start.5 = (bf16[256,227]{1,0:T(8,128)(2,1)S(1)}, bf16[256,227]{1,0:T(8,128)(2,1)S(1)}, u32[]{:S(2)}, u32[]{:S(2)}) collective-permute-start(bf16[256,227]{1,0:T(8,128)(2,1)S(1)} %constant_dynamic-update-slice_fusion), channel_id=1, source_target_pairs={{16,32},{48,64},{80,96},{32,16},{64,48},{96,80},{17,33},{49,65},{8... | collective-permute-start | bytes 348680 | tf_op jit(solution)/shard_map/ppermute | solution.py:444
  25.0 7.9 %collective-permute-start.8 = (bf16[128,512]{1,0:T(8,128)(2,1)S(1)}, bf16[128,512]{1,0:T(8,128)(2,1)S(1)}, u32[]{:S(2)}, u32[]{:S(2)}) collective-permute-start(bf16[128,512]{1,0:T(8,128)(2,1)S(1)} %get-tuple-element.49), channel_id=1, source_target_pairs={{1,2},{3,4},{5,6},{7,8},{9,10},{11,12},{13,14},{15,0},{2,1},{4,3},... | collective-permute-start | bytes 393224 | tf_op jit(solution)/shard_map/ppermute | solution.py:454
  28.1 4.9 %collective-permute-start.7 = (bf16[128,512]{1,0:T(8,128)(2,1)S(1)}, bf16[128,512]{1,0:T(8,128)(2,1)S(1)}, u32[]{:S(2)}, u32[]{:S(2)}) collective-permute-start(bf16[128,512]{1,0:T(8,128)(2,1)S(1)} %get-tuple-element.49), channel_id=1, source_target_pairs={{0,1},{1,0},{2,3},{3,2},{4,5},{5,4},{6,7},{7,6},{8,9},{9,8},{10,11... | collective-permute-start | bytes 393224 | tf_op jit(solution)/shard_map/ppermute | solution.py:435
  28.1 4.9 %collective-permute-start.6 = (bf16[128,512]{1,0:T(8,128)(2,1)S(1)}, bf16[128,512]{1,0:T(8,128)(2,1)S(1)}, u32[]{:S(2)}, u32[]{:S(2)}) collective-permute-start(bf16[128,512]{1,0:T(8,128)(2,1)S(1)} %get-tuple-element.49), channel_id=1, source_target_pairs={{0,16},{16,0},{32,48},{48,32},{64,80},{80,64},{96,112},{112,96},{1... | collective-permute-start | bytes 393224 | tf_op jit(solution)/shard_map/ppermute | solution.py:435
  28.8 9.5 %collective-permute-start.10 = (bf16[128,512]{1,0:T(8,128)(2,1)S(1)}, bf16[128,512]{1,0:T(8,128)(2,1)S(1)}, u32[]{:S(2)}, u32[]{:S(2)}) collective-permute-start(bf16[128,512]{1,0:T(8,128)(2,1)S(1)} %get-tuple-element.49), channel_id=1, source_target_pairs={{16,32},{48,64},{80,96},{32,16},{64,48},{96,80},{17,33},{49,65},{8... | collective-permute-start | bytes 393224 | tf_op jit(solution)/shard_map/ppermute | solution.py:444
  33.0 8.6 %collective-permute-start.11 = (bf16[256,512]{1,0:T(8,128)(2,1)S(1)}, bf16[256,512]{1,0:T(8,128)(2,1)S(1)}, u32[]{:S(2)}, u32[]{:S(2)}) collective-permute-start(bf16[256,512]{1,0:T(8,128)(2,1)S(1)} %constant_dynamic-update-slice_fusion.2), channel_id=1, source_target_pairs={{16,32},{48,64},{80,96},{32,16},{64,48},{96,80},{17,33},{49,65},{8... | collective-permute-start | bytes 786440 | tf_op jit(solution)/shard_map/ppermute | solution.py:444
  48.0 7.8 %collective-permute-start.12 = (bf16[384,512]{1,0:T(8,128)(2,1)S(1)}, bf16[384,512]{1,0:T(8,128)(2,1)S(1)}, u32[]{:S(2)}, u32[]{:S(2)}) collective-permute-start(bf16[384,512]{1,0:T(8,128)(2,1)S(1)} %get-tuple-element.66), channel_id=1, source_target_pairs={{0,16},{16,0},{32,48},{48,32},{64,80},{80,64},{96,112},{112,96},{1... | collective-permute-start | bytes 1179656 | tf_op jit(solution)/shard_map/ppermute | solution.py:435
  48.1 7.7 %collective-permute-start.13 = (bf16[256,512]{1,0:T(8,128)(2,1)S(1)}, bf16[256,512]{1,0:T(8,128)(2,1)S(1)}, u32[]{:S(2)}, u32[]{:S(2)}) collective-permute-start(bf16[256,512]{1,0:T(8,128)(2,1)S(1)} %get-tuple-element.68), channel_id=1, source_target_pairs={{16,32},{48,64},{80,96},{32,16},{64,48},{96,80},{17,33},{49,65},{8... | collective-permute-start | bytes 786440 | tf_op jit(solution)/shard_map/ppermute | solution.py:444
  51.7 11.2 %collective-permute-start.16 = (bf16[128,512]{1,0:T(8,128)(2,1)S(1)}, bf16[128,512]{1,0:T(8,128)(2,1)S(1)}, u32[]{:S(2)}, u32[]{:S(2)}) collective-permute-start(bf16[128,512]{1,0:T(8,128)(2,1)S(1)} %get-tuple-element.69), channel_id=1, source_target_pairs={{16,32},{48,64},{80,96},{32,16},{64,48},{96,80},{17,33},{49,65},{8... | collective-permute-start | bytes 393224 | tf_op jit(solution)/shard_map/ppermute | solution.py:444
  55.9 7.4 %collective-permute-start.15 = (bf16[128,512]{1,0:T(8,128)(2,1)S(1)}, bf16[128,512]{1,0:T(8,128)(2,1)S(1)}, u32[]{:S(2)}, u32[]{:S(2)}) collective-permute-start(bf16[128,512]{1,0:T(8,128)(2,1)S(1)} %get-tuple-element.86), channel_id=1, source_target_pairs={{1,2},{3,4},{5,6},{7,8},{9,10},{11,12},{13,14},{15,0},{2,1},{4,3},... | collective-permute-start | bytes 393224 | tf_op jit(solution)/shard_map/ppermute | solution.py:454
  69.9 6.1 %collective-permute-start.18 = (bf16[160,512]{1,0:T(8,128)(2,1)S(1)}, bf16[160,512]{1,0:T(8,128)(2,1)S(1)}, u32[]{:S(2)}, u32[]{:S(2)}) collective-permute-start(bf16[160,512]{1,0:T(8,128)(2,1)S(1)} %get-tuple-element.88), channel_id=1, source_target_pairs={{0,32},{1,33},{2,34},{3,35},{4,36},{5,37},{6,38},{7,39},{8,40},{9,... | collective-permute-start | bytes 491528 | tf_op jit(solution)/shard_map/ppermute | solution.py:484
  73.3 7.5 %collective-permute-start.20 = (bf16[160,512]{1,0:T(8,128)(2,1)S(1)}, bf16[160,512]{1,0:T(8,128)(2,1)S(1)}, u32[]{:S(2)}, u32[]{:S(2)}) collective-permute-start(bf16[160,512]{1,0:T(8,128)(2,1)S(1)} %get-tuple-element.89), channel_id=1, source_target_pairs={{0,36},{1,37},{2,38},{3,39},{4,32},{5,33},{6,34},{7,35},{8,44},{9,... | collective-permute-start | bytes 491528 | tf_op jit(solution)/shard_map/ppermute | solution.py:484
  73.3 7.5 %collective-permute-start.19 = (bf16[160,512]{1,0:T(8,128)(2,1)S(1)}, bf16[160,512]{1,0:T(8,128)(2,1)S(1)}, u32[]{:S(2)}, u32[]{:S(2)}) collective-permute-start(bf16[160,512]{1,0:T(8,128)(2,1)S(1)} %get-tuple-element.90), channel_id=1, source_target_pairs={{0,4},{1,5},{2,6},{3,7},{4,0},{5,1},{6,2},{7,3},{8,12},{9,13},{10,... | collective-permute-start | bytes 491528 | tf_op jit(solution)/shard_map/ppermute | solution.py:484
  80.9 6.7 %collective-permute-start.23 = (bf16[160,512]{1,0:T(8,128)(2,1)S(1)}, bf16[160,512]{1,0:T(8,128)(2,1)S(1)}, u32[]{:S(2)}, u32[]{:S(2)}) collective-permute-start(bf16[160,512]{1,0:T(8,128)(2,1)S(1)} %add_convert_fusion.3), channel_id=1, source_target_pairs={{0,97},{1,96},{2,99},{3,98},{4,101},{5,100},{6,103},{7,102},{8,105... | collective-permute-start | bytes 491528 | tf_op jit(solution)/shard_map/ppermute | solution.py:484
  84.4 5.4 %collective-permute-start.21 = (bf16[160,512]{1,0:T(8,128)(2,1)S(1)}, bf16[160,512]{1,0:T(8,128)(2,1)S(1)}, u32[]{:S(2)}, u32[]{:S(2)}) collective-permute-start(bf16[160,512]{1,0:T(8,128)(2,1)S(1)} %add_convert_fusion.3), channel_id=1, source_target_pairs={{0,1},{1,0},{2,3},{3,2},{4,5},{5,4},{6,7},{7,6},{8,9},{9,8},{10,11... | collective-permute-start | bytes 491528 | tf_op jit(solution)/shard_map/ppermute | solution.py:484
  89.9 5.3 %collective-permute-start.26 = (bf16[160,512]{1,0:T(8,128)(2,1)S(1)}, bf16[160,512]{1,0:T(8,128)(2,1)S(1)}, u32[]{:S(2)}, u32[]{:S(2)}) collective-permute-start(bf16[160,512]{1,0:T(8,128)(2,1)S(1)} %add_convert_fusion.2), channel_id=1, source_target_pairs={{0,15},{1,14},{2,13},{3,12},{4,11},{5,10},{6,9},{7,8},{8,7},{9,6},... | collective-permute-start | bytes 491528 | tf_op jit(solution)/shard_map/ppermute | solution.py:484
  90.0 6.0 %collective-permute-start.25 = (bf16[160,512]{1,0:T(8,128)(2,1)S(1)}, bf16[160,512]{1,0:T(8,128)(2,1)S(1)}, u32[]{:S(2)}, u32[]{:S(2)}) collective-permute-start(bf16[160,512]{1,0:T(8,128)(2,1)S(1)} %add_convert_fusion.2), channel_id=1, source_target_pairs={{0,3},{1,2},{2,1},{3,0},{4,7},{5,6},{6,5},{7,4},{8,11},{9,10},{10,... | collective-permute-start | bytes 491528 | tf_op jit(solution)/shard_map/ppermute | solution.py:484
  90.1 5.9 %collective-permute-start.24 = (bf16[160,512]{1,0:T(8,128)(2,1)S(1)}, bf16[160,512]{1,0:T(8,128)(2,1)S(1)}, u32[]{:S(2)}, u32[]{:S(2)}) collective-permute-start(bf16[160,512]{1,0:T(8,128)(2,1)S(1)} %add_convert_fusion.2), channel_id=1, source_target_pairs={{0,12},{1,13},{2,14},{3,15},{4,8},{5,9},{6,10},{7,11},{8,4},{9,5},... | collective-permute-start | bytes 491528 | tf_op jit(solution)/shard_map/ppermute | solution.py:484
  96.1 7.7 %collective-permute-start.29 = (bf16[160,512]{1,0:T(8,128)(2,1)S(1)}, bf16[160,512]{1,0:T(8,128)(2,1)S(1)}, u32[]{:S(2)}, u32[]{:S(2)}) collective-permute-start(bf16[160,512]{1,0:T(8,128)(2,1)S(1)} %add_convert_fusion.1), channel_id=1, source_target_pairs={{0,36},{1,37},{2,38},{3,39},{4,32},{5,33},{6,34},{7,35},{8,44},{9,... | collective-permute-start | bytes 491528 | tf_op jit(solution)/shard_map/ppermute | solution.py:484
  98.9 6.5 %collective-permute-start.28 = (bf16[160,512]{1,0:T(8,128)(2,1)S(1)}, bf16[160,512]{1,0:T(8,128)(2,1)S(1)}, u32[]{:S(2)}, u32[]{:S(2)}) collective-permute-start(bf16[160,512]{1,0:T(8,128)(2,1)S(1)} %add_convert_fusion.1), channel_id=1, source_target_pairs={{0,4},{1,5},{2,6},{3,7},{4,0},{5,1},{6,2},{7,3},{8,12},{9,13},{10,... | collective-permute-start | bytes 491528 | tf_op jit(solution)/shard_map/ppermute | solution.py:484
  100.7 5.5 %collective-permute-start.27 = (bf16[160,512]{1,0:T(8,128)(2,1)S(1)}, bf16[160,512]{1,0:T(8,128)(2,1)S(1)}, u32[]{:S(2)}, u32[]{:S(2)}) collective-permute-start(bf16[160,512]{1,0:T(8,128)(2,1)S(1)} %add_convert_fusion.1), channel_id=1, source_target_pairs={{0,32},{1,33},{2,34},{3,35},{4,36},{5,37},{6,38},{7,39},{8,40},{9,... | collective-permute-start | bytes 491528 | tf_op jit(solution)/shard_map/ppermute | solution.py:484
  106.3 6.3 %collective-permute-start.30 = (bf16[640,512]{1,0:T(8,128)(2,1)S(1)}, bf16[640,512]{1,0:T(8,128)(2,1)S(1)}, u32[]{:S(2)}, u32[]{:S(2)}) collective-permute-start(bf16[640,512]{1,0:T(8,128)(2,1)S(1)} %pad_maximum_fusion.mine), channel_id=1, source_target_pairs={{0,16},{16,0},{32,48},{48,32},{64,80},{80,64},{96,112},{112,96},{1... | collective-permute-start | bytes 1966088 | tf_op jit(solution)/shard_map/ppermute | solution.py:435
  (28 other events, 175.9 us)

commit v7 on v6

--- a/solution.py
+++ b/solution.py
@@ -88,7 +88,14 @@
     pltpu.make_async_copy(source, target, sem).wait()
 
 
-def prepare_kernel(live_ref, senders, receivers, state, weight, terms, *hots):
+def prepare_kernel(
+    live_ref, senders, receivers, state, weight, pre_kept, mix_kept, terms, *refs
+):
+    pre_slope, mix_slope, *hots = refs
+    for kept, slope in ((pre_kept, pre_slope), (mix_kept, mix_slope)):
+        value = kept[...].astype(f32)
+        gate = sigmoid(value)
+        slope[...] = (gate * (1.0 + value * (1.0 - gate))).astype(bf16)
     nodes = state.shape[0]
     terms[0:nodes, :] = dot(state[...], weight[...]).astype(bf16)
     terms[nodes:, :] = jnp.zeros_like(terms[nodes:, :])
@@ -271,13 +278,9 @@
     edge_receiver,
     cotangent,
     ends,
-    pre_kept,
-    mix_kept,
     edge_grad,
     state_part,
     receive_hot,
-    pre_slope,
-    mix_slope,
 ):
     for block in range(ends.shape[0]):
         here = slice(block * lanes, (block + 1) * lanes)
@@ -285,10 +288,6 @@
     edge_grad[...] = cross_dot(sender_rows[...], mix_grads[...]).astype(bf16)
     receiver_grad = dot(place_hot[...], mix_grads[...]).astype(bf16)
     state_part[...] = cotangent[...].astype(f32) + back_dot(receiver_grad, edge_receiver[...])
-    for kept, slope in ((pre_kept, pre_slope), (mix_kept, mix_slope)):
-        value = kept[...].astype(f32)
-        gate = sigmoid(value)
-        slope[...] = (gate * (1.0 + value * (1.0 - gate))).astype(bf16)
 
 
 def encode_back_kernel(
@@ -595,11 +594,13 @@
         2,
         20,
     )
-    terms, process_send, process_receive, process_place, process_sender_place = call(
+    terms, pre_slope, mix_slope, process_send, process_receive, process_place, process_sender_place = call(
         prepare_kernel,
-        (process_live, process_senders, process_receivers, state, edge_receiver),
+        (process_live, process_senders, process_receivers, state, edge_receiver, pre_kept, mix_kept),
         [
             ((256, width), bf16, 0),
+            ((edges, width), bf16, 0),
+            ((edges, width), bf16, 0),
             ((edges, 256), bf16, 0),
             ((edges, 256), bf16, 0),
             ((nodes, edges), bf16, 0),
@@ -670,11 +671,10 @@
         for side in (0, 1)
     ]
     from_close, from_far = close(to_close), far(to_far)
-    edge_grad, state_part, receive_hot, pre_slope, mix_slope = call(
+    edge_grad, state_part, receive_hot = call(
         edge_kernel,
-        (sender_rows, mix_grad, process_place, edge_receiver, cotangent, ends, pre_kept, mix_kept),
-        [((width, width), bf16, 0), ((nodes, width), f32, 0), ((edges, 256), bf16, 0)]
-        + [((edges, width), bf16, 0)] * 2,
+        (sender_rows, mix_grad, process_place, edge_receiver, cotangent, ends),
+        [((width, width), bf16, 0), ((nodes, width), f32, 0), ((edges, 256), bf16, 0)],
         [],
         0,
         16,

time: 115 us -> 115 us (level)
    ppermute x6, waiting for transfers between devices: 7.27 us -> 4.81 us  [outer(): lax.ppermute(x, 'lat', [(i, i + 1) for i in ends] + [(i + 1, i) for i in...]
    ppermute x3, waiting for transfers between devices: 0.68 us -> 2.95 us  [far(): lax.ppermute(x, 'lon', [(i, (i + 1) % size) for i in ends] + [((i + 1) %...]
where the time goes in v7:
time: 115 us; the launch traced here: 114 us
  starting transfers between devices  58.2 us (51%)
  waiting for transfers between devices  28.3 us (25%)
  Pallas kernels  22.3 us (19%)
  between operations  2.67 us (2%)
  matrix products  1.19 us (1%)
    pallas_call x8, Pallas kernels, call(): pl.pallas_call(kernel, out_shape=[jax.ShapeDtypeStruct(shape, dtype) for...  22.3 us
    ppermute x6, starting transfers between devices, outer(): lax.ppermute(x, 'lat', [(i, i + 1) for i in ends] + [(i + 1, i) for i in...  20.9 us
    ppermute x12, waiting for transfers between devices, met(): return lax.ppermute(x, ('lat', 'lon'), pairs)  18.3 us
    ppermute x12, starting transfers between devices, met(): return lax.ppermute(x, ('lat', 'lon'), pairs)  17.7 us
    ppermute x3, starting transfers between devices, far(): lax.ppermute(x, 'lon', [(i, (i + 1) % size) for i in ends] + [((i + 1) %...  13.6 us
    ppermute x10, starting transfers between devices, partner(): lax.ppermute(x, axis, [(i, i ^ flip) for i in range(lax.axis_size(axis))])  6.04 us
    ppermute x6, waiting for transfers between devices, outer(): lax.ppermute(x, 'lat', [(i, i + 1) for i in ends] + [(i + 1, i) for i in...  4.81 us
    ppermute x3, waiting for transfers between devices, far(): lax.ppermute(x, 'lon', [(i, (i + 1) % size) for i in ends] + [((i + 1) %...  2.95 us
  transfers between devices with their start and end apart: 31, of which 17 were waited for; matrix products, arithmetic and copies ran while one was open for 0% of the time, Pallas kernels for 5%

profile of v7, /device:TPU:1, one launch (start us, length us, event | category | flops | bytes accessed | tf_op | source)
XLA Modules:
  0.0 114.3 jit_solution(12547581990608949286)
XLA Ops:
  1.8 7.1 %collective-permute-start.2 = (bf16[128,227]{1,0:T(8,128)(2,1)S(1)}, bf16[128,227]{1,0:T(8,128)(2,1)S(1)}, u32[]{:S(2)}, u32[]{:S(2)}) collective-permute-start(bf16[128,227]{1,0:T(8,128)(2,1)S(1)} %convolution_convert_fusion), channel_id=1, source_target_pairs={{1,2},{3,4},{5,6},{7,8},{9,10},{11,12},{13,14},{15,0},{2,1},{4,3},... | collective-permute-start | bytes 174344 | tf_op jit(solution)/shard_map/ppermute | solution.py:453
  9.9 3.0 %collective-permute-start.4 = (bf16[128,227]{1,0:T(8,128)(2,1)S(1)}, bf16[128,227]{1,0:T(8,128)(2,1)S(1)}, u32[]{:S(2)}, u32[]{:S(2)}) collective-permute-start(bf16[128,227]{1,0:T(8,128)(2,1)S(1)} %convolution_convert_fusion), channel_id=1, source_target_pairs={{16,32},{48,64},{80,96},{32,16},{64,48},{96,80},{17,33},{49,65},{8... | collective-permute-start | bytes 174344 | tf_op jit(solution)/shard_map/ppermute | solution.py:443
  13.7 3.8 %collective-permute-start.5 = (bf16[256,227]{1,0:T(8,128)(2,1)S(1)}, bf16[256,227]{1,0:T(8,128)(2,1)S(1)}, u32[]{:S(2)}, u32[]{:S(2)}) collective-permute-start(bf16[256,227]{1,0:T(8,128)(2,1)S(1)} %constant_dynamic-update-slice_fusion), channel_id=1, source_target_pairs={{16,32},{48,64},{80,96},{32,16},{64,48},{96,80},{17,33},{49,65},{8... | collective-permute-start | bytes 348680 | tf_op jit(solution)/shard_map/ppermute | solution.py:443
  20.4 4.6 %shard_map.256 = (bf16[160,512]{1,0:T(8,128)(2,1)S(1)}, bf16[128,512]{1,0:T(8,128)(2,1)S(1)}, bf16[1024,227]{1,0:T(8,128)(2,1)S(1)}, bf16[1024,512]{1,0:T(8,128)...) custom-call(s32[4]{0:T(128)S(1)} %pad_add_fusion.place_ref, ...), custom_call_target="tpu_custom_call" | custom-call | flops 4294967296 | bytes 8388608 | tf_op jit(solution)/shard_map/pallas_call | solution.py:420
  25.0 3.1 %collective-permute-start.8 = (bf16[128,512]{1,0:T(8,128)(2,1)S(1)}, bf16[128,512]{1,0:T(8,128)(2,1)S(1)}, u32[]{:S(2)}, u32[]{:S(2)}) collective-permute-start(bf16[128,512]{1,0:T(8,128)(2,1)S(1)} %get-tuple-element.49), channel_id=1, source_target_pairs={{1,2},{3,4},{5,6},{7,8},{9,10},{11,12},{13,14},{15,0},{2,1},{4,3},... | collective-permute-start | bytes 393224 | tf_op jit(solution)/shard_map/ppermute | solution.py:453
  28.8 3.9 %collective-permute-start.10 = (bf16[128,512]{1,0:T(8,128)(2,1)S(1)}, bf16[128,512]{1,0:T(8,128)(2,1)S(1)}, u32[]{:S(2)}, u32[]{:S(2)}) collective-permute-start(bf16[128,512]{1,0:T(8,128)(2,1)S(1)} %get-tuple-element.49), channel_id=1, source_target_pairs={{16,32},{48,64},{80,96},{32,16},{64,48},{96,80},{17,33},{49,65},{8... | collective-permute-start | bytes 393224 | tf_op jit(solution)/shard_map/ppermute | solution.py:443
  33.0 4.6 %collective-permute-start.11 = (bf16[256,512]{1,0:T(8,128)(2,1)S(1)}, bf16[256,512]{1,0:T(8,128)(2,1)S(1)}, u32[]{:S(2)}, u32[]{:S(2)}) collective-permute-start(bf16[256,512]{1,0:T(8,128)(2,1)S(1)} %constant_dynamic-update-slice_fusion.2), channel_id=1, source_target_pairs={{16,32},{48,64},{80,96},{32,16},{64,48},{96,80},{17,33},{49,65},{8... | collective-permute-start | bytes 786440 | tf_op jit(solution)/shard_map/ppermute | solution.py:443
  38.0 2.8 %shard_map.257 = (bf16[256,512]{1,0:T(8,128)(2,1)S(1)}, bf16[1024,512]{1,0:T(8,128)(2,1)S(1)}, bf16[1024,512]{1,0:T(8,128)(2,1)S(1)}, bf16[1024,256]{1,0:T(8,128...) custom-call(s32[1]{0:T(128)S(6)} %copy.37.live_ref, ...), custom_call_target="tpu_custom_call" | custom-call | flops 4294967296 | bytes 8388608 | tf_op jit(solution)/shard_map/pallas_call | solution.py:420
  41.7 6.3 %shard_map.258 = (bf16[160,512]{1,0:T(8,128)(2,1)}, f32[160,512]{1,0:T(8,128)S(1)}, bf16[256,512]{1,0:T(8,128)(2,1)S(1)}, bf16[384,512]{1,0:T(8,128)(2,1)S(1)}, ...) custom-call(s32[4]{0:T(128)S(1)} %pad_add_fusion.place_ref, ...), custom_call_target="tpu_custom_call" | custom-call | flops 4294967296 | bytes 8388608 | tf_op jit(solution)/shard_map/pallas_call | solution.py:420
  48.0 3.7 %collective-permute-start.13 = (bf16[256,512]{1,0:T(8,128)(2,1)S(1)}, bf16[256,512]{1,0:T(8,128)(2,1)S(1)}, u32[]{:S(2)}, u32[]{:S(2)}) collective-permute-start(bf16[256,512]{1,0:T(8,128)(2,1)S(1)} %get-tuple-element.68), channel_id=1, source_target_pairs={{16,32},{48,64},{80,96},{32,16},{64,48},{96,80},{17,33},{49,65},{8... | collective-permute-start | bytes 786440 | tf_op jit(solution)/shard_map/ppermute | solution.py:443
  53.6 2.1 %collective-permute-done.13 = bf16[256,512]{1,0:T(8,128)(2,1)S(1)} collective-permute-done((bf16[256,512]{1,0:T(8,128)(2,1)S(1)}, bf16[256,512]{1,0:T(8,128)(2,1)S(1)}, u32[]{:S(2)}, u32[]{:S(2)}) %collective-permute-start.13) | collective-permute-done | bytes 262176 | tf_op jit(solution)/shard_map/ppermute | solution.py:443
  55.9 3.4 %collective-permute-start.15 = (bf16[128,512]{1,0:T(8,128)(2,1)S(1)}, bf16[128,512]{1,0:T(8,128)(2,1)S(1)}, u32[]{:S(2)}, u32[]{:S(2)}) collective-permute-start(bf16[128,512]{1,0:T(8,128)(2,1)S(1)} %get-tuple-element.86), channel_id=1, source_target_pairs={{1,2},{3,4},{5,6},{7,8},{9,10},{11,12},{13,14},{15,0},{2,1},{4,3},... | collective-permute-start | bytes 393224 | tf_op jit(solution)/shard_map/ppermute | solution.py:453
  60.4 2.6 %collective-permute-done.15.from_far = bf16[128,512]{1,0:T(8,128)(2,1)S(1)} collective-permute-done((bf16[128,512]{1,0:T(8,128)(2,1)S(1)}, bf16[128,512]{1,0:T(8,128)(2,1)S(1)}, u32[]{:S(2)}, u32[]{:S(2)}) %collective-permute-start.15) | collective-permute-done | bytes 131104 | tf_op jit(solution)/shard_map/ppermute | solution.py:453
  63.1 4.2 %shard_map.260 = (bf16[640,512]{1,0:T(8,128)(2,1)S(1)}, bf16[640,512]{1,0:T(8,128)(2,1)S(1)}) custom-call(s32[4]{0:T(128)S(1)} %pad_add_fusion.place_ref, bf16[1024,256]{1,0:T(8,128)(2,1)S(1)} %get-tuple-element.63.receive_hot, s32[1,128]{1,0:T(1,128)S(1)} %bitcast.14, f32[160,512]{1,0:T(8,128)S(1)} %get-tuple-element.64.state_part, ...), custom_call_target="tpu_custom_call" | custom-call | flops 4294967296 | bytes 8388608 | tf_op jit(solution)/shard_map/pallas_call | solution.py:420
  69.7 3.4 %collective-permute-start.18 = (bf16[160,512]{1,0:T(8,128)(2,1)S(1)}, bf16[160,512]{1,0:T(8,128)(2,1)S(1)}, u32[]{:S(2)}, u32[]{:S(2)}) collective-permute-start(bf16[160,512]{1,0:T(8,128)(2,1)S(1)} %get-tuple-element.88), channel_id=1, source_target_pairs={{0,32},{1,33},{2,34},{3,35},{4,36},{5,37},{6,38},{7,39},{8,40},{9,... | collective-permute-start | bytes 491528 | tf_op jit(solution)/shard_map/ppermute | solution.py:483
  73.1 2.5 %collective-permute-start.19 = (bf16[160,512]{1,0:T(8,128)(2,1)S(1)}, bf16[160,512]{1,0:T(8,128)(2,1)S(1)}, u32[]{:S(2)}, u32[]{:S(2)}) collective-permute-start(bf16[160,512]{1,0:T(8,128)(2,1)S(1)} %get-tuple-element.90), channel_id=1, source_target_pairs={{0,4},{1,5},{2,6},{3,7},{4,0},{5,1},{6,2},{7,3},{8,12},{9,13},{10,... | collective-permute-start | bytes 491528 | tf_op jit(solution)/shard_map/ppermute | solution.py:483
  75.8 4.8 %collective-permute-done.20 = bf16[160,512]{1,0:T(8,128)(2,1)S(1)} collective-permute-done((bf16[160,512]{1,0:T(8,128)(2,1)S(1)}, bf16[160,512]{1,0:T(8,128)(2,1)S(1)}, u32[]{:S(2)}, u32[]{:S(2)}) %collective-permute-start.20) | collective-permute-done | bytes 163872 | tf_op jit(solution)/shard_map/ppermute | solution.py:483
  80.7 3.5 %collective-permute-start.23 = (bf16[160,512]{1,0:T(8,128)(2,1)S(1)}, bf16[160,512]{1,0:T(8,128)(2,1)S(1)}, u32[]{:S(2)}, u32[]{:S(2)}) collective-permute-start(bf16[160,512]{1,0:T(8,128)(2,1)S(1)} %add_convert_fusion.3), channel_id=1, source_target_pairs={{0,97},{1,96},{2,99},{3,98},{4,101},{5,100},{6,103},{7,102},{8,105... | collective-permute-start | bytes 491528 | tf_op jit(solution)/shard_map/ppermute | solution.py:483
  84.6 2.7 %collective-permute-done.23 = bf16[160,512]{1,0:T(8,128)(2,1)S(1)} collective-permute-done((bf16[160,512]{1,0:T(8,128)(2,1)S(1)}, bf16[160,512]{1,0:T(8,128)(2,1)S(1)}, u32[]{:S(2)}, u32[]{:S(2)}) %collective-permute-start.23) | collective-permute-done | bytes 163872 | tf_op jit(solution)/shard_map/ppermute | solution.py:483
  89.9 2.5 %collective-permute-start.24 = (bf16[160,512]{1,0:T(8,128)(2,1)S(1)}, bf16[160,512]{1,0:T(8,128)(2,1)S(1)}, u32[]{:S(2)}, u32[]{:S(2)}) collective-permute-start(bf16[160,512]{1,0:T(8,128)(2,1)S(1)} %add_convert_fusion.2), channel_id=1, source_target_pairs={{0,12},{1,13},{2,14},{3,15},{4,8},{5,9},{6,10},{7,11},{8,4},{9,5},... | collective-permute-start | bytes 491528 | tf_op jit(solution)/shard_map/ppermute | solution.py:483
  92.4 2.5 %collective-permute-done.26 = bf16[160,512]{1,0:T(8,128)(2,1)S(1)} collective-permute-done((bf16[160,512]{1,0:T(8,128)(2,1)S(1)}, bf16[160,512]{1,0:T(8,128)(2,1)S(1)}, u32[]{:S(2)}, u32[]{:S(2)}) %collective-permute-start.26) | collective-permute-done | bytes 163872 | tf_op jit(solution)/shard_map/ppermute | solution.py:483
  95.9 2.8 %collective-permute-start.29 = (bf16[160,512]{1,0:T(8,128)(2,1)S(1)}, bf16[160,512]{1,0:T(8,128)(2,1)S(1)}, u32[]{:S(2)}, u32[]{:S(2)}) collective-permute-start(bf16[160,512]{1,0:T(8,128)(2,1)S(1)} %add_convert_fusion.1), channel_id=1, source_target_pairs={{0,36},{1,37},{2,38},{3,39},{4,32},{5,33},{6,34},{7,35},{8,44},{9,... | collective-permute-start | bytes 491528 | tf_op jit(solution)/shard_map/ppermute | solution.py:483
  101.0 2.5 %collective-permute-done.29 = bf16[160,512]{1,0:T(8,128)(2,1)S(1)} collective-permute-done((bf16[160,512]{1,0:T(8,128)(2,1)S(1)}, bf16[160,512]{1,0:T(8,128)(2,1)S(1)}, u32[]{:S(2)}, u32[]{:S(2)}) %collective-permute-start.29) | collective-permute-done | bytes 163872 | tf_op jit(solution)/shard_map/ppermute | solution.py:483
  106.1 4.6 %collective-permute-start.30 = (bf16[640,512]{1,0:T(8,128)(2,1)S(1)}, bf16[640,512]{1,0:T(8,128)(2,1)S(1)}, u32[]{:S(2)}, u32[]{:S(2)}) collective-permute-start(bf16[640,512]{1,0:T(8,128)(2,1)S(1)} %pad_maximum_fusion.mine), channel_id=1, source_target_pairs={{0,16},{16,0},{32,48},{48,32},{64,80},{80,64},{96,112},{112,96},{1... | collective-permute-start | bytes 1966088 | tf_op jit(solution)/shard_map/ppermute | solution.py:434
  (101 shorter events, 24.6 us)
Async XLA Ops:
  1.8 11.7 %collective-permute-start.2 = (bf16[128,227]{1,0:T(8,128)(2,1)S(1)}, bf16[128,227]{1,0:T(8,128)(2,1)S(1)}, u32[]{:S(2)}, u32[]{:S(2)}) collective-permute-start(bf16[128,227]{1,0:T(8,128)(2,1)S(1)} %convolution_convert_fusion), channel_id=1, source_target_pairs={{1,2},{3,4},{5,6},{7,8},{9,10},{11,12},{13,14},{15,0},{2,1},{4,3},... | collective-permute-start | bytes 174344 | tf_op jit(solution)/shard_map/ppermute | solution.py:453
  9.9 8.6 %collective-permute-start.4 = (bf16[128,227]{1,0:T(8,128)(2,1)S(1)}, bf16[128,227]{1,0:T(8,128)(2,1)S(1)}, u32[]{:S(2)}, u32[]{:S(2)}) collective-permute-start(bf16[128,227]{1,0:T(8,128)(2,1)S(1)} %convolution_convert_fusion), channel_id=1, source_target_pairs={{16,32},{48,64},{80,96},{32,16},{64,48},{96,80},{17,33},{49,65},{8... | collective-permute-start | bytes 174344 | tf_op jit(solution)/shard_map/ppermute | solution.py:443
  13.7 6.5 %collective-permute-start.5 = (bf16[256,227]{1,0:T(8,128)(2,1)S(1)}, bf16[256,227]{1,0:T(8,128)(2,1)S(1)}, u32[]{:S(2)}, u32[]{:S(2)}) collective-permute-start(bf16[256,227]{1,0:T(8,128)(2,1)S(1)} %constant_dynamic-update-slice_fusion), channel_id=1, source_target_pairs={{16,32},{48,64},{80,96},{32,16},{64,48},{96,80},{17,33},{49,65},{8... | collective-permute-start | bytes 348680 | tf_op jit(solution)/shard_map/ppermute | solution.py:443
  25.0 7.9 %collective-permute-start.8 = (bf16[128,512]{1,0:T(8,128)(2,1)S(1)}, bf16[128,512]{1,0:T(8,128)(2,1)S(1)}, u32[]{:S(2)}, u32[]{:S(2)}) collective-permute-start(bf16[128,512]{1,0:T(8,128)(2,1)S(1)} %get-tuple-element.49), channel_id=1, source_target_pairs={{1,2},{3,4},{5,6},{7,8},{9,10},{11,12},{13,14},{15,0},{2,1},{4,3},... | collective-permute-start | bytes 393224 | tf_op jit(solution)/shard_map/ppermute | solution.py:453
  28.1 4.9 %collective-permute-start.7 = (bf16[128,512]{1,0:T(8,128)(2,1)S(1)}, bf16[128,512]{1,0:T(8,128)(2,1)S(1)}, u32[]{:S(2)}, u32[]{:S(2)}) collective-permute-start(bf16[128,512]{1,0:T(8,128)(2,1)S(1)} %get-tuple-element.49), channel_id=1, source_target_pairs={{0,1},{1,0},{2,3},{3,2},{4,5},{5,4},{6,7},{7,6},{8,9},{9,8},{10,11... | collective-permute-start | bytes 393224 | tf_op jit(solution)/shard_map/ppermute | solution.py:434
  28.1 4.9 %collective-permute-start.6 = (bf16[128,512]{1,0:T(8,128)(2,1)S(1)}, bf16[128,512]{1,0:T(8,128)(2,1)S(1)}, u32[]{:S(2)}, u32[]{:S(2)}) collective-permute-start(bf16[128,512]{1,0:T(8,128)(2,1)S(1)} %get-tuple-element.49), channel_id=1, source_target_pairs={{0,16},{16,0},{32,48},{48,32},{64,80},{80,64},{96,112},{112,96},{1... | collective-permute-start | bytes 393224 | tf_op jit(solution)/shard_map/ppermute | solution.py:434
  28.8 12.0 %collective-permute-start.10 = (bf16[128,512]{1,0:T(8,128)(2,1)S(1)}, bf16[128,512]{1,0:T(8,128)(2,1)S(1)}, u32[]{:S(2)}, u32[]{:S(2)}) collective-permute-start(bf16[128,512]{1,0:T(8,128)(2,1)S(1)} %get-tuple-element.49), channel_id=1, source_target_pairs={{16,32},{48,64},{80,96},{32,16},{64,48},{96,80},{17,33},{49,65},{8... | collective-permute-start | bytes 393224 | tf_op jit(solution)/shard_map/ppermute | solution.py:443
  33.0 8.6 %collective-permute-start.11 = (bf16[256,512]{1,0:T(8,128)(2,1)S(1)}, bf16[256,512]{1,0:T(8,128)(2,1)S(1)}, u32[]{:S(2)}, u32[]{:S(2)}) collective-permute-start(bf16[256,512]{1,0:T(8,128)(2,1)S(1)} %constant_dynamic-update-slice_fusion.2), channel_id=1, source_target_pairs={{16,32},{48,64},{80,96},{32,16},{64,48},{96,80},{17,33},{49,65},{8... | collective-permute-start | bytes 786440 | tf_op jit(solution)/shard_map/ppermute | solution.py:443
  48.0 7.8 %collective-permute-start.12 = (bf16[384,512]{1,0:T(8,128)(2,1)S(1)}, bf16[384,512]{1,0:T(8,128)(2,1)S(1)}, u32[]{:S(2)}, u32[]{:S(2)}) collective-permute-start(bf16[384,512]{1,0:T(8,128)(2,1)S(1)} %get-tuple-element.66), channel_id=1, source_target_pairs={{0,16},{16,0},{32,48},{48,32},{64,80},{80,64},{96,112},{112,96},{1... | collective-permute-start | bytes 1179656 | tf_op jit(solution)/shard_map/ppermute | solution.py:434
  48.0 7.7 %collective-permute-start.13 = (bf16[256,512]{1,0:T(8,128)(2,1)S(1)}, bf16[256,512]{1,0:T(8,128)(2,1)S(1)}, u32[]{:S(2)}, u32[]{:S(2)}) collective-permute-start(bf16[256,512]{1,0:T(8,128)(2,1)S(1)} %get-tuple-element.68), channel_id=1, source_target_pairs={{16,32},{48,64},{80,96},{32,16},{64,48},{96,80},{17,33},{49,65},{8... | collective-permute-start | bytes 786440 | tf_op jit(solution)/shard_map/ppermute | solution.py:443
  51.7 8.7 %collective-permute-start.16 = (bf16[128,512]{1,0:T(8,128)(2,1)S(1)}, bf16[128,512]{1,0:T(8,128)(2,1)S(1)}, u32[]{:S(2)}, u32[]{:S(2)}) collective-permute-start(bf16[128,512]{1,0:T(8,128)(2,1)S(1)} %get-tuple-element.69), channel_id=1, source_target_pairs={{16,32},{48,64},{80,96},{32,16},{64,48},{96,80},{17,33},{49,65},{8... | collective-permute-start | bytes 393224 | tf_op jit(solution)/shard_map/ppermute | solution.py:443
  55.9 7.2 %collective-permute-start.15 = (bf16[128,512]{1,0:T(8,128)(2,1)S(1)}, bf16[128,512]{1,0:T(8,128)(2,1)S(1)}, u32[]{:S(2)}, u32[]{:S(2)}) collective-permute-start(bf16[128,512]{1,0:T(8,128)(2,1)S(1)} %get-tuple-element.86), channel_id=1, source_target_pairs={{1,2},{3,4},{5,6},{7,8},{9,10},{11,12},{13,14},{15,0},{2,1},{4,3},... | collective-permute-start | bytes 393224 | tf_op jit(solution)/shard_map/ppermute | solution.py:453
  69.7 6.1 %collective-permute-start.18 = (bf16[160,512]{1,0:T(8,128)(2,1)S(1)}, bf16[160,512]{1,0:T(8,128)(2,1)S(1)}, u32[]{:S(2)}, u32[]{:S(2)}) collective-permute-start(bf16[160,512]{1,0:T(8,128)(2,1)S(1)} %get-tuple-element.88), channel_id=1, source_target_pairs={{0,32},{1,33},{2,34},{3,35},{4,36},{5,37},{6,38},{7,39},{8,40},{9,... | collective-permute-start | bytes 491528 | tf_op jit(solution)/shard_map/ppermute | solution.py:483
  73.1 7.5 %collective-permute-start.20 = (bf16[160,512]{1,0:T(8,128)(2,1)S(1)}, bf16[160,512]{1,0:T(8,128)(2,1)S(1)}, u32[]{:S(2)}, u32[]{:S(2)}) collective-permute-start(bf16[160,512]{1,0:T(8,128)(2,1)S(1)} %get-tuple-element.89), channel_id=1, source_target_pairs={{0,36},{1,37},{2,38},{3,39},{4,32},{5,33},{6,34},{7,35},{8,44},{9,... | collective-permute-start | bytes 491528 | tf_op jit(solution)/shard_map/ppermute | solution.py:483
  73.1 7.5 %collective-permute-start.19 = (bf16[160,512]{1,0:T(8,128)(2,1)S(1)}, bf16[160,512]{1,0:T(8,128)(2,1)S(1)}, u32[]{:S(2)}, u32[]{:S(2)}) collective-permute-start(bf16[160,512]{1,0:T(8,128)(2,1)S(1)} %get-tuple-element.90), channel_id=1, source_target_pairs={{0,4},{1,5},{2,6},{3,7},{4,0},{5,1},{6,2},{7,3},{8,12},{9,13},{10,... | collective-permute-start | bytes 491528 | tf_op jit(solution)/shard_map/ppermute | solution.py:483
  80.7 6.7 %collective-permute-start.23 = (bf16[160,512]{1,0:T(8,128)(2,1)S(1)}, bf16[160,512]{1,0:T(8,128)(2,1)S(1)}, u32[]{:S(2)}, u32[]{:S(2)}) collective-permute-start(bf16[160,512]{1,0:T(8,128)(2,1)S(1)} %add_convert_fusion.3), channel_id=1, source_target_pairs={{0,97},{1,96},{2,99},{3,98},{4,101},{5,100},{6,103},{7,102},{8,105... | collective-permute-start | bytes 491528 | tf_op jit(solution)/shard_map/ppermute | solution.py:483
  84.2 5.4 %collective-permute-start.21 = (bf16[160,512]{1,0:T(8,128)(2,1)S(1)}, bf16[160,512]{1,0:T(8,128)(2,1)S(1)}, u32[]{:S(2)}, u32[]{:S(2)}) collective-permute-start(bf16[160,512]{1,0:T(8,128)(2,1)S(1)} %add_convert_fusion.3), channel_id=1, source_target_pairs={{0,1},{1,0},{2,3},{3,2},{4,5},{5,4},{6,7},{7,6},{8,9},{9,8},{10,11... | collective-permute-start | bytes 491528 | tf_op jit(solution)/shard_map/ppermute | solution.py:483
  89.7 5.3 %collective-permute-start.26 = (bf16[160,512]{1,0:T(8,128)(2,1)S(1)}, bf16[160,512]{1,0:T(8,128)(2,1)S(1)}, u32[]{:S(2)}, u32[]{:S(2)}) collective-permute-start(bf16[160,512]{1,0:T(8,128)(2,1)S(1)} %add_convert_fusion.2), channel_id=1, source_target_pairs={{0,15},{1,14},{2,13},{3,12},{4,11},{5,10},{6,9},{7,8},{8,7},{9,6},... | collective-permute-start | bytes 491528 | tf_op jit(solution)/shard_map/ppermute | solution.py:483
  89.8 6.0 %collective-permute-start.25 = (bf16[160,512]{1,0:T(8,128)(2,1)S(1)}, bf16[160,512]{1,0:T(8,128)(2,1)S(1)}, u32[]{:S(2)}, u32[]{:S(2)}) collective-permute-start(bf16[160,512]{1,0:T(8,128)(2,1)S(1)} %add_convert_fusion.2), channel_id=1, source_target_pairs={{0,3},{1,2},{2,1},{3,0},{4,7},{5,6},{6,5},{7,4},{8,11},{9,10},{10,... | collective-permute-start | bytes 491528 | tf_op jit(solution)/shard_map/ppermute | solution.py:483
  89.9 5.9 %collective-permute-start.24 = (bf16[160,512]{1,0:T(8,128)(2,1)S(1)}, bf16[160,512]{1,0:T(8,128)(2,1)S(1)}, u32[]{:S(2)}, u32[]{:S(2)}) collective-permute-start(bf16[160,512]{1,0:T(8,128)(2,1)S(1)} %add_convert_fusion.2), channel_id=1, source_target_pairs={{0,12},{1,13},{2,14},{3,15},{4,8},{5,9},{6,10},{7,11},{8,4},{9,5},... | collective-permute-start | bytes 491528 | tf_op jit(solution)/shard_map/ppermute | solution.py:483
  95.9 7.7 %collective-permute-start.29 = (bf16[160,512]{1,0:T(8,128)(2,1)S(1)}, bf16[160,512]{1,0:T(8,128)(2,1)S(1)}, u32[]{:S(2)}, u32[]{:S(2)}) collective-permute-start(bf16[160,512]{1,0:T(8,128)(2,1)S(1)} %add_convert_fusion.1), channel_id=1, source_target_pairs={{0,36},{1,37},{2,38},{3,39},{4,32},{5,33},{6,34},{7,35},{8,44},{9,... | collective-permute-start | bytes 491528 | tf_op jit(solution)/shard_map/ppermute | solution.py:483
  98.7 6.5 %collective-permute-start.28 = (bf16[160,512]{1,0:T(8,128)(2,1)S(1)}, bf16[160,512]{1,0:T(8,128)(2,1)S(1)}, u32[]{:S(2)}, u32[]{:S(2)}) collective-permute-start(bf16[160,512]{1,0:T(8,128)(2,1)S(1)} %add_convert_fusion.1), channel_id=1, source_target_pairs={{0,4},{1,5},{2,6},{3,7},{4,0},{5,1},{6,2},{7,3},{8,12},{9,13},{10,... | collective-permute-start | bytes 491528 | tf_op jit(solution)/shard_map/ppermute | solution.py:483
  100.5 5.5 %collective-permute-start.27 = (bf16[160,512]{1,0:T(8,128)(2,1)S(1)}, bf16[160,512]{1,0:T(8,128)(2,1)S(1)}, u32[]{:S(2)}, u32[]{:S(2)}) collective-permute-start(bf16[160,512]{1,0:T(8,128)(2,1)S(1)} %add_convert_fusion.1), channel_id=1, source_target_pairs={{0,32},{1,33},{2,34},{3,35},{4,36},{5,37},{6,38},{7,39},{8,40},{9,... | collective-permute-start | bytes 491528 | tf_op jit(solution)/shard_map/ppermute | solution.py:483
  106.1 6.3 %collective-permute-start.30 = (bf16[640,512]{1,0:T(8,128)(2,1)S(1)}, bf16[640,512]{1,0:T(8,128)(2,1)S(1)}, u32[]{:S(2)}, u32[]{:S(2)}) collective-permute-start(bf16[640,512]{1,0:T(8,128)(2,1)S(1)} %pad_maximum_fusion.mine), channel_id=1, source_target_pairs={{0,16},{16,0},{32,48},{48,32},{64,80},{80,64},{96,112},{112,96},{1... | collective-permute-start | bytes 1966088 | tf_op jit(solution)/shard_map/ppermute | solution.py:434
  (28 other events, 175.3 us)
